TPU v7x, 32 devices: a whole 2x2x4 slice. The times are simulated.
32 devices in a mesh: fsdp: 4 (over x, core), ctx: 8 (over z, y).
Axes of the slice: x: 2, y: 2, z: 4, core: 2. Of those that a mesh axis runs over, the one named last changes fastest.
Arguments:
- tokens: bfloat16 [8, 1024, 2048], P('fsdp', 'ctx'), may hold values from -6 to 6
- lengths: int32 [8], P('fsdp'), may hold values from 256 to 1024, as said below
- cotangent: bfloat16 [8, 1024, 2048], P('fsdp', 'ctx'), may hold values from -6 to 6
- attn_gain: bfloat16 [2048], P(('fsdp', 'ctx')), may hold values from 0.5 to 1.5
- w_query: bfloat16 [2048, 2048], P(('fsdp', 'ctx')), may hold values from -0.1875 to 0.1875
- w_key: bfloat16 [2048, 512], P(('fsdp', 'ctx')), may hold values from -0.1875 to 0.1875
- w_value: bfloat16 [2048, 512], P(('fsdp', 'ctx')), may hold values from -0.125 to 0.125
- w_out: bfloat16 [2048, 2048], P(('fsdp', 'ctx')), may hold values from -1 to 1
- mlp_gain: bfloat16 [2048], P(('fsdp', 'ctx')), may hold values from 0.5 to 1.5
- w_gate: bfloat16 [2048, 8192], P(('fsdp', 'ctx')), may hold values from -0.125 to 0.125
- w_up: bfloat16 [2048, 8192], P(('fsdp', 'ctx')), may hold values from -0.125 to 0.125
- w_down: bfloat16 [8192, 2048], P(('fsdp', 'ctx')), may hold values from -0.0625 to 0.0625
Outputs:
- layer_out: bfloat16 [8, 1024, 2048], P('fsdp', 'ctx')
- grad_tokens: bfloat16 [8, 1024, 2048], P('fsdp', 'ctx')
- grad_attn_gain: float32 [2048], P(('fsdp', 'ctx'))
- grad_w_query: float32 [2048, 2048], P(('fsdp', 'ctx'))
- grad_w_key: float32 [2048, 512], P(('fsdp', 'ctx'))
- grad_w_value: float32 [2048, 512], P(('fsdp', 'ctx'))
- grad_w_out: float32 [2048, 2048], P(('fsdp', 'ctx'))
- grad_mlp_gain: float32 [2048], P(('fsdp', 'ctx'))
- grad_w_gate: float32 [2048, 8192], P(('fsdp', 'ctx'))
- grad_w_up: float32 [2048, 8192], P(('fsdp', 'ctx'))
- grad_w_down: float32 [8192, 2048], P(('fsdp', 'ctx'))
Inputs may be any that keep to these rules, and one draw needn't show every extreme that they name: `lengths`: valid tokens of each sequence, counted from its start; among the 2 sequences on one index of fsdp one has all 1024.
All inputs are finite; a program needn't handle non-finite values.
Results may differ from a plain program's by a relative error of at most 0.018.
Values may be sent and summed in bfloat16 or wider, within the bound.
A program may use at most 512 MiB of HBM per device.

v0:
```python
import jax
import jax.numpy as jnp
from jax import lax
from jax.sharding import PartitionSpec as P

HEADS = 32
KVH = 8
HD = 64


EPSILON = 1e-05
NEGATIVE = -1e30


def rope_tables(positions, head_width):
    half_width = head_width // 2
    frequency = 500000.0 ** (-jnp.arange(half_width, dtype=jnp.float32) * 2.0 / head_width)
    angles = positions.astype(jnp.float32)[:, None] * frequency[None, :]
    return (jnp.cos(angles)[:, None, :], jnp.sin(angles)[:, None, :])


def rotate(field, cos_table, sin_table):
    half_width = field.shape[-1] // 2
    first_half = field[..., :half_width]
    second_half = field[..., half_width:]
    return jnp.concatenate(
        [
            first_half * cos_table - second_half * sin_table,
            second_half * cos_table + first_half * sin_table,
        ],
        -1,
    )


def rotate_back(grad_field, cos_table, sin_table):
    half_width = grad_field.shape[-1] // 2
    first_half = grad_field[..., :half_width]
    second_half = grad_field[..., half_width:]
    return jnp.concatenate(
        [
            first_half * cos_table + second_half * sin_table,
            second_half * cos_table - first_half * sin_table,
        ],
        -1,
    )


def rms_scale(field):
    return lax.rsqrt(jnp.mean(field * field, -1, keepdims=True) + EPSILON)


def norm_back(grad_normed, normed, scale_rows):
    return scale_rows * (grad_normed - normed * jnp.mean(grad_normed * normed, -1, keepdims=True))


def matmul(left_side, right_side):
    return jnp.dot(left_side, right_side, preferred_element_type=jnp.float32)


def left_product(left_side, right_side):
    return jnp.einsum("rd,re->de", left_side, right_side, preferred_element_type=jnp.float32)


def right_product(left_side, right_side):
    return jnp.einsum("re,de->rd", left_side, right_side, preferred_element_type=jnp.float32)


def on_device(
    tokens,
    lengths,
    cotangent,
    attn_gain,
    w_query,
    w_key,
    w_value,
    w_out,
    mlp_gain,
    w_gate,
    w_up,
    w_down,
):
    seq_count, block_len, model_width = tokens.shape
    ctx_count = lax.axis_size("ctx")
    seq_length = block_len * ctx_count
    key_block = min(512, seq_length)
    key_steps = seq_length // key_block
    group_size = HEADS // KVH
    score_scale = HD ** (-0.5)
    row_count = seq_count * block_len
    block_start = lax.axis_index("ctx") * block_len
    query_pos = block_start + jnp.arange(block_len, dtype=jnp.int32)
    query_last = block_start + block_len - 1
    cos_table, sin_table = rope_tables(jnp.tile(query_pos, seq_count), HD)
    step_index = jnp.arange(key_steps, dtype=jnp.int32)
    gathered = (
        lax.all_gather(attn_gain, ("fsdp", "ctx"), axis=0, tiled=True),
        lax.all_gather(w_query, ("fsdp", "ctx"), axis=0, tiled=True),
        lax.all_gather(w_key, ("fsdp", "ctx"), axis=0, tiled=True),
        lax.all_gather(w_value, ("fsdp", "ctx"), axis=0, tiled=True),
        lax.all_gather(w_out, ("fsdp", "ctx"), axis=0, tiled=True),
        lax.all_gather(mlp_gain, ("fsdp", "ctx"), axis=0, tiled=True),
        lax.all_gather(w_gate, ("fsdp", "ctx"), axis=0, tiled=True),
        lax.all_gather(w_up, ("fsdp", "ctx"), axis=0, tiled=True),
        lax.all_gather(w_down, ("fsdp", "ctx"), axis=0, tiled=True),
    )
    gain_one, query_w, key_w, value_w, out_w, gain_two, gate_w, up_w, down_w = gathered
    resid_in = tokens.reshape(row_count, model_width).astype(jnp.float32)
    scale_one = rms_scale(resid_in)
    normed_one = resid_in * scale_one
    hidden_one = (normed_one * gain_one.astype(jnp.float32)).astype(jnp.bfloat16)
    query_rows = rotate(
        matmul(hidden_one, query_w).reshape(row_count, HEADS, HD), cos_table, sin_table
    ).astype(jnp.bfloat16)
    key_rows = rotate(
        matmul(hidden_one, key_w).reshape(row_count, KVH, HD), cos_table, sin_table
    ).astype(jnp.bfloat16)
    value_rows = matmul(hidden_one, value_w).astype(jnp.bfloat16)
    queries = query_rows.reshape(seq_count, block_len, KVH, group_size, HD).transpose(0, 2, 3, 1, 4)
    key_own = key_rows.reshape(seq_count, block_len, KVH, HD)
    value_own = value_rows.reshape(seq_count, block_len, KVH, HD)
    keys_all, values_all = (
        lax.all_gather(key_own, "ctx", axis=1, tiled=True),
        lax.all_gather(value_own, "ctx", axis=1, tiled=True),
    )

    def key_mask(key_start):
        key_pos = key_start + jnp.arange(key_block, dtype=jnp.int32)
        causal = key_pos[None, :] <= query_pos[:, None]
        inside = key_pos[None, :] < lengths[:, None]
        return causal[None, None, None, :, :] & inside[:, None, None, None, :]

    def is_live(index):
        return index * key_block <= query_last

    def block_scores(keys_src, index):
        key_start = index * key_block
        key_part = lax.dynamic_slice_in_dim(keys_src, key_start, key_block, 1)
        raw_scores = jnp.einsum(
            "skgqd,snkd->skgqn", queries, key_part, preferred_element_type=jnp.float32
        )
        return (jnp.where(key_mask(key_start), raw_scores * score_scale, NEGATIVE), key_part)

    stat_shape = (seq_count, KVH, group_size, block_len)
    head_shape = (seq_count, KVH, group_size, block_len, HD)

    def stats_step(state, index):

        def stats_active(state_in):
            running_max, running_sum = state_in
            masked, key_part = block_scores(keys_all, index)
            fresh_max = jnp.maximum(running_max, jnp.max(masked, -1))
            fresh_sum = running_sum * jnp.exp(running_max - fresh_max) + jnp.sum(
                jnp.exp(masked - fresh_max[..., None]), -1
            )
            return (fresh_max, fresh_sum)

        def stats_passive(state_in):
            return state_in

        return (lax.cond(is_live(index), stats_active, stats_passive, state), None)

    start_state = (jnp.full(stat_shape, NEGATIVE, jnp.float32), jnp.zeros(stat_shape, jnp.float32))
    (row_max, row_sum), unused = lax.scan(stats_step, start_state, step_index)
    log_total = row_max + jnp.log(row_sum)

    def output_step(attn_accum, index):

        def output_active(acc_in):
            masked, key_part = block_scores(keys_all, index)
            soft_low = jnp.exp(masked - log_total[..., None]).astype(jnp.bfloat16)
            value_part = lax.dynamic_slice_in_dim(values_all, index * key_block, key_block, 1)
            return acc_in + jnp.einsum(
                "skgqn,snkd->skgqd", soft_low, value_part, preferred_element_type=jnp.float32
            )

        def output_passive(acc_in):
            return acc_in

        return (lax.cond(is_live(index), output_active, output_passive, attn_accum), None)

    attended, unused = lax.scan(output_step, jnp.zeros(head_shape, jnp.float32), step_index)
    attended_low = (
        attended.astype(jnp.bfloat16).transpose(0, 3, 1, 2, 4).reshape(row_count, model_width)
    )
    resid_mid = resid_in + matmul(attended_low, out_w)
    scale_two = rms_scale(resid_mid)
    normed_two = resid_mid * scale_two
    hidden_two = (normed_two * gain_two.astype(jnp.float32)).astype(jnp.bfloat16)
    gate_pre = matmul(hidden_two, gate_w)
    up_pre = matmul(hidden_two, up_w)
    sigmoid_gate = jax.nn.sigmoid(gate_pre)
    gate_act = gate_pre * sigmoid_gate
    mlp_inner = (gate_act * up_pre).astype(jnp.bfloat16)
    layer_out = (resid_mid + matmul(mlp_inner, down_w)).astype(jnp.bfloat16)
    back_set = (
        lax.all_gather(attn_gain, ("fsdp", "ctx"), axis=0, tiled=True),
        lax.all_gather(w_query, ("fsdp", "ctx"), axis=0, tiled=True),
        lax.all_gather(w_key, ("fsdp", "ctx"), axis=0, tiled=True),
        lax.all_gather(w_value, ("fsdp", "ctx"), axis=0, tiled=True),
        lax.all_gather(w_out, ("fsdp", "ctx"), axis=0, tiled=True),
        lax.all_gather(mlp_gain, ("fsdp", "ctx"), axis=0, tiled=True),
        lax.all_gather(w_gate, ("fsdp", "ctx"), axis=0, tiled=True),
        lax.all_gather(w_up, ("fsdp", "ctx"), axis=0, tiled=True),
        lax.all_gather(w_down, ("fsdp", "ctx"), axis=0, tiled=True),
    )
    back_keys, back_values = (
        lax.all_gather(key_own, "ctx", axis=1, tiled=True),
        lax.all_gather(value_own, "ctx", axis=1, tiled=True),
    )
    back_query, back_key, back_value, back_out = (
        back_set[1],
        back_set[2],
        back_set[3],
        back_set[4],
    )
    back_gate, back_up, back_down = (back_set[6], back_set[7], back_set[8])
    valid = (query_pos[None, :] < lengths[:, None]).astype(jnp.float32)
    grad_out = (cotangent.astype(jnp.float32) * valid[..., None]).reshape(row_count, model_width)
    grad_low = grad_out.astype(jnp.bfloat16)
    grad_down = left_product(mlp_inner, grad_low)
    grad_inner = right_product(grad_low, back_down).astype(jnp.bfloat16)
    gate_slope = sigmoid_gate * (1.0 + gate_pre * (1.0 - sigmoid_gate))
    grad_gate = (grad_inner * up_pre * gate_slope).astype(jnp.bfloat16)
    grad_up = (grad_inner * gate_act).astype(jnp.bfloat16)
    grad_gate_w = left_product(hidden_two, grad_gate)
    grad_up_w = left_product(hidden_two, grad_up)
    grad_hidden_two = right_product(grad_gate, back_gate) + right_product(grad_up, back_up)
    grad_gain_two = jnp.sum(grad_hidden_two * normed_two, 0)
    late = (
        lax.psum_scatter(grad_gain_two, ("fsdp", "ctx"), scatter_dimension=0, tiled=True),
        lax.psum_scatter(grad_gate_w, ("fsdp", "ctx"), scatter_dimension=0, tiled=True),
        lax.psum_scatter(grad_up_w, ("fsdp", "ctx"), scatter_dimension=0, tiled=True),
        lax.psum_scatter(grad_down, ("fsdp", "ctx"), scatter_dimension=0, tiled=True),
    )
    grad_mid = grad_out + norm_back(
        grad_hidden_two * back_set[5].astype(jnp.float32), normed_two, scale_two
    )
    grad_attn = grad_mid.astype(jnp.bfloat16)
    grad_out_w = left_product(attended_low, grad_attn)
    grad_heads = right_product(grad_attn, back_out).astype(jnp.bfloat16)
    grad_attended = grad_heads.reshape(seq_count, block_len, KVH, group_size, HD).transpose(
        0, 2, 3, 1, 4
    )
    delta_rows = jnp.sum(grad_attended.astype(jnp.float32) * attended, -1)

    def back_step(grad_query, index):

        def back_active(grad_in):
            masked, key_part = block_scores(back_keys, index)
            value_part = lax.dynamic_slice_in_dim(back_values, index * key_block, key_block, 1)
            soft = jnp.exp(masked - log_total[..., None])
            grad_soft = jnp.einsum(
                "skgqd,snkd->skgqn", grad_attended, value_part, preferred_element_type=jnp.float32
            )
            grad_score = (score_scale * soft * (grad_soft - delta_rows[..., None])).astype(
                jnp.bfloat16
            )
            grad_next = grad_in + jnp.einsum(
                "skgqn,snkd->skgqd", grad_score, key_part, preferred_element_type=jnp.float32
            )
            grad_key_part = jnp.einsum(
                "skgqn,skgqd->snkd", grad_score, queries, preferred_element_type=jnp.float32
            )
            grad_value_part = jnp.einsum(
                "skgqn,skgqd->snkd",
                soft.astype(jnp.bfloat16),
                grad_attended,
                preferred_element_type=jnp.float32,
            )
            return (grad_next, grad_key_part, grad_value_part)

        def back_passive(grad_in):
            empty = jnp.zeros((seq_count, key_block, KVH, HD), jnp.float32)
            return (grad_in, empty, empty)

        grad_next, grad_key_part, grad_value_part = lax.cond(
            is_live(index), back_active, back_passive, grad_query
        )
        return (grad_next, (grad_key_part, grad_value_part))

    grad_queries, (key_parts, value_parts) = lax.scan(
        back_step, jnp.zeros(head_shape, jnp.float32), step_index
    )
    grad_keys_all = key_parts.transpose(1, 0, 2, 3, 4).reshape(seq_count, seq_length, KVH, HD)
    grad_values_all = value_parts.transpose(1, 0, 2, 3, 4).reshape(seq_count, seq_length, KVH, HD)
    grad_keys, grad_values = (
        lax.psum_scatter(
            grad_keys_all.astype(jnp.bfloat16), "ctx", scatter_dimension=1, tiled=True
        ).astype(jnp.float32),
        lax.psum_scatter(
            grad_values_all.astype(jnp.bfloat16), "ctx", scatter_dimension=1, tiled=True
        ).astype(jnp.float32),
    )
    grad_query_rows = (
        rotate_back(
            grad_queries.transpose(0, 3, 1, 2, 4).reshape(row_count, HEADS, HD),
            cos_table,
            sin_table,
        )
        .reshape(row_count, model_width)
        .astype(jnp.bfloat16)
    )
    grad_key_rows = (
        rotate_back(grad_keys.reshape(row_count, KVH, HD), cos_table, sin_table)
        .reshape(row_count, KVH * HD)
        .astype(jnp.bfloat16)
    )
    grad_value_rows = grad_values.reshape(row_count, KVH * HD).astype(jnp.bfloat16)
    grad_query_w = left_product(hidden_one, grad_query_rows)
    grad_key_w = left_product(hidden_one, grad_key_rows)
    grad_value_w = left_product(hidden_one, grad_value_rows)
    grad_hidden_one = (
        right_product(grad_query_rows, back_query)
        + right_product(grad_key_rows, back_key)
        + right_product(grad_value_rows, back_value)
    )
    grad_gain_one = jnp.sum(grad_hidden_one * normed_one, 0)
    grad_input = grad_mid + norm_back(
        grad_hidden_one * back_set[0].astype(jnp.float32), normed_one, scale_one
    )
    early = (
        lax.psum_scatter(grad_gain_one, ("fsdp", "ctx"), scatter_dimension=0, tiled=True),
        lax.psum_scatter(grad_query_w, ("fsdp", "ctx"), scatter_dimension=0, tiled=True),
        lax.psum_scatter(grad_key_w, ("fsdp", "ctx"), scatter_dimension=0, tiled=True),
        lax.psum_scatter(grad_value_w, ("fsdp", "ctx"), scatter_dimension=0, tiled=True),
        lax.psum_scatter(grad_out_w, ("fsdp", "ctx"), scatter_dimension=0, tiled=True),
    )
    return (
        layer_out.reshape(seq_count, block_len, model_width),
        grad_input.reshape(seq_count, block_len, model_width).astype(jnp.bfloat16),
        early[0],
        early[1],
        early[2],
        early[3],
        early[4],
        late[0],
        late[1],
        late[2],
        late[3],
    )


def solution(mesh):
    placed = (
        P("fsdp", "ctx", None),
        P("fsdp"),
        P("fsdp", "ctx", None),
        P(("fsdp", "ctx")),
        P(("fsdp", "ctx"), None),
        P(("fsdp", "ctx"), None),
        P(("fsdp", "ctx"), None),
        P(("fsdp", "ctx"), None),
        P(("fsdp", "ctx")),
        P(("fsdp", "ctx"), None),
        P(("fsdp", "ctx"), None),
        P(("fsdp", "ctx"), None),
    )
    return jax.shard_map(
        on_device,
        mesh=mesh,
        in_specs=placed,
        out_specs=(
            P("fsdp", "ctx", None),
            P("fsdp", "ctx", None),
            P(("fsdp", "ctx")),
            P(("fsdp", "ctx"), None),
            P(("fsdp", "ctx"), None),
            P(("fsdp", "ctx"), None),
            P(("fsdp", "ctx"), None),
            P(("fsdp", "ctx")),
            P(("fsdp", "ctx"), None),
            P(("fsdp", "ctx"), None),
            P(("fsdp", "ctx"), None),
        ),
        check_vma=False,
    )
```

profile of v0, /device:TPU:0, one launch (start us, length us, event | category | flops | bytes accessed | tf_op | source)
XLA Modules:
  0.0 6546.5 jit_solution(2269572062546024182)
XLA Ops:
  10.4 42.1 all-reduce.5
  55.8 14.5 all-gather.16.cloned.1.call-done
  74.7 53.9 all-gather.10.cloned.1.call-done
  128.7 3.9 copy.87
  142.3 53.7 all-gather.18.cloned.1.call-done
  196.0 3.6 copy.94
  199.5 76.7 %all-gather.14.cloned.1.call-done = bf16[2048,2048]{1,0:T(8,128)(2,1)} async-done(((bf16[64,2048]{1,0:T(8,128)(2,1)}), bf16[2048,2048]{1,0:T(8,128)(2,1)}) %all-gather.14.cloned.1.call-update) | async-done | bytes 8388624 | tf_op jit(solution)/shard_map/all_gather | solution.py:97
  276.2 12.3 copy.90
  288.5 5.8 fusion.79
  295.3 33.1 all-gather.12.cloned.1.call-done
  328.4 23.3 while.45
  329.7 20.7 conditional.9
  331.4 8.7 fusion.6
  340.2 10.2 exponential_reduce_fusion
  353.3 13.1 while.46
  354.8 10.4 conditional.10
  356.5 8.6 fusion.19
  369.9 36.9 all-gather.20.cloned.1.call-done
  406.8 5.8 multiply_reduce_fusion.5
  414.3 189.0 %all-gather.26.cloned.1.call-done = bf16[8192,2048]{1,0:T(8,128)(2,1)} async-done(((bf16[256,2048]{1,0:T(8,128)(2,1)}), bf16[8192,2048]{1,0:T(8,128)(2,1)}) %all-gather.26.cloned.1.call-update) | async-done | bytes 33554448 | tf_op jit(solution)/shard_map/all_gather | solution.py:104
  603.2 17.8 convolution_convert_fusion
  621.0 178.3 %all-gather.22.cloned.1.call-done = bf16[2048,8192]{1,0:T(8,128)(2,1)} async-done(((bf16[64,8192]{1,0:T(8,128)(2,1)}), bf16[2048,8192]{1,0:T(8,128)(2,1)}) %all-gather.22.cloned.1.call-update) | async-done | bytes 33554448 | tf_op jit(solution)/shard_map/all_gather | solution.py:102
  799.3 18.3 fusion.80
  817.6 177.7 %all-gather.24.cloned.1.call-done = bf16[2048,8192]{1,0:T(8,128)(2,1)} async-done(((bf16[64,8192]{1,0:T(8,128)(2,1)}), bf16[2048,8192]{1,0:T(8,128)(2,1)}) %all-gather.24.cloned.1.call-update) | async-done | bytes 33554448 | tf_op jit(solution)/shard_map/all_gather | solution.py:103
  995.3 26.6 fusion.55
  1021.9 17.0 fusion.81
  1039.0 20.9 multiply_reduce_fusion
  1059.9 2.7 bitcast_add_fusion
  1064.1 6.7 convolution_convert_fusion.1
  1070.8 5.2 reshape.472
  1076.0 4.3 copy.97
  1082.3 48.4 while.47
  1083.8 37.3 conditional.11
  1084.5 9.5 fusion.44
  1095.1 9.8 fusion.32
  1106.7 3.6 convolution_bitcast_fusion
  1110.3 10.7 fusion.39
  1121.1 3.1 constant_dynamic-update-slice_fusion.3
  1127.6 3.1 constant_dynamic-update-slice_fusion.3
  1130.7 6.6 copy.123
  1137.2 6.5 reshape.473
  1143.8 6.2 copy.124
  1150.0 6.5 reshape.475
  1156.6 88.4 %reduce-scatter.28.cloned.1.call-done = bf16[128,1024]{1,0:T(8,128)(2,1)} async-done(((bf16[1024,1024]{1,0:T(8,128)(2,1)}), bf16[128,1024]{1,0:T(8,128)(2,1)}) %reduce-scatter.28.cloned.1.call-update) | async-done | bytes 262160
  1249.4 2.7 fusion.84
  1252.2 63.6 reduce-scatter.30.cloned.1.call-done
  1319.4 2.7 fusion.66
  1322.2 3.0 copy.101
  1325.2 3.1 reshape.454
  1329.7 8.2 fusion.83
  1339.7 8.1 fusion.59
  1349.0 25.5 fusion.85
  1374.6 28.3 fusion.75
  1404.2 25.7 fusion.86
  1431.2 7.3 fusion.82
  1438.4 16.7 fusion.58
  1460.4 43.1 all-reduce.4
  1504.6 3.2 add_convert_fusion
  1507.8 97.7 %reduce-scatter.18.cloned.1.call-done = f32[64,512]{1,0:T(8,128)} async-done(((f32[2048,512]{1,0:T(8,128)}), f32[64,512]{1,0:T(8,128)}) %reduce-scatter.18.cloned.1.call-update) | async-done | bytes 131088 | tf_op jit(solution)/shard_map/reduce_scatter | solution.py:325
  1605.5 358.7 %reduce-scatter.14.cloned.1.call-done = f32[64,2048]{1,0:T(8,128)} async-done(((f32[2048,2048]{1,0:T(8,128)}), f32[64,2048]{1,0:T(8,128)}) %reduce-scatter.14.cloned.1.call-update) | async-done | bytes 524304 | tf_op jit(solution)/shard_map/reduce_scatter | solution.py:323
  1964.2 360.0 %reduce-scatter.20.cloned.1.call-done = f32[64,2048]{1,0:T(8,128)} async-done(((f32[2048,2048]{1,0:T(8,128)}), f32[64,2048]{1,0:T(8,128)}) %reduce-scatter.20.cloned.1.call-update) | async-done | bytes 524304 | tf_op jit(solution)/shard_map/reduce_scatter | solution.py:326
  2324.2 1404.6 %reduce-scatter.22.cloned.1.call-done = f32[64,8192]{1,0:T(8,128)} async-done(((f32[2048,8192]{1,0:T(8,128)}), f32[64,8192]{1,0:T(8,128)}) %reduce-scatter.22.cloned.1.call-update) | async-done | bytes 2097168 | tf_op jit(solution)/shard_map/reduce_scatter | solution.py:231
  3728.8 1405.3 %reduce-scatter.24.cloned.1.call-done = f32[64,8192]{1,0:T(8,128)} async-done(((f32[2048,8192]{1,0:T(8,128)}), f32[64,8192]{1,0:T(8,128)}) %reduce-scatter.24.cloned.1.call-update) | async-done | bytes 2097168 | tf_op jit(solution)/shard_map/reduce_scatter | solution.py:232
  5134.1 1405.3 %reduce-scatter.26.cloned.1.call-done = f32[256,2048]{1,0:T(8,128)} async-done(((f32[8192,2048]{1,0:T(8,128)}), f32[256,2048]{1,0:T(8,128)}) %reduce-scatter.26.cloned.1.call-update) | async-done | bytes 2097168 | tf_op jit(solution)/shard_map/reduce_scatter | solution.py:233
  (214 shorter events, 65.8 us)
Async XLA Ops:
  7.2 63.1 all-gather.16.cloned.1.call-start
  7.9 120.8 %all-gather.10.cloned.1.call-start = ((), (), s32[]{:S(2)}) async-start(), calls=%async_computation.9 | async-start | bytes 2162688 | tf_op jit(solution)/shard_map/all_gather | solution.py:98
  8.7 187.3 %all-gather.18.cloned.1.call-start = ((), (), s32[]{:S(2)}) async-start(), calls=%async_computation.13 | async-start | bytes 2359296 | tf_op jit(solution)/shard_map/all_gather | solution.py:123
  52.5 21.9 copy-start.33
  52.5 21.9 copy-start.1
  54.1 1.6 copy-start.37
  73.5 202.7 %all-gather.14.cloned.1.call-start = ((), (), s32[]{:S(2)}) async-start(), calls=%async_computation.11 | async-start | bytes 8650752 | tf_op jit(solution)/shard_map/all_gather | solution.py:97
  74.1 254.3 %all-gather.12.cloned.1.call-start = ((), (), s32[]{:S(2)}) async-start(), calls=%async_computation.10 | async-start | bytes 2359296 | tf_op jit(solution)/shard_map/all_gather | solution.py:122
  74.4 220.0 %copy-start.29 = (f32[256,32]{0,1:T(8,128)}, f32[256,32]{0,1:T(8,128)S(1)}, u32[]{:S(2)}) copy-start(f32[256,32]{0,1:T(8,128)S(1)} %get-tuple-element.541) | copy-start | bytes 98308
  74.4 220.0 %copy-start.31 = (f32[256,32]{0,1:T(8,128)}, f32[256,32]{0,1:T(8,128)S(1)}, u32[]{:S(2)}) copy-start(f32[256,32]{0,1:T(8,128)S(1)} %get-tuple-element.542) | copy-start | bytes 98308
  74.7 213.8 %copy-start.3 = (bf16[2,128,2048]{2,1,0:T(8,128)(2,1)}, bf16[2,128,2048]{2,1,0:T(8,128)(2,1)S(1)}, u32[]{:S(2)}) copy-start(bf16[2,128,2048]{2,1,0:T(8,128)(2,1)S(1)} %multiply_convert_fusion.3) | copy-start | bytes 3145732
  132.6 7.1 copy-start.28
  135.9 270.9 %all-gather.20.cloned.1.call-start = ((), (), s32[]{:S(2)}) async-start(), calls=%async_computation.14 | async-start | bytes 8650752 | tf_op jit(solution)/shard_map/all_gather | solution.py:100
  136.5 466.8 %all-gather.26.cloned.1.call-start = ((), (), s32[]{:S(2)}) async-start(), calls=%async_computation.17 | async-start | bytes 34603008 | tf_op jit(solution)/shard_map/all_gather | solution.py:104
  137.2 662.1 %all-gather.22.cloned.1.call-start = ((), (), s32[]{:S(2)}) async-start(), calls=%async_computation.15 | async-start | bytes 34603008 | tf_op jit(solution)/shard_map/all_gather | solution.py:102
  138.0 857.4 %all-gather.24.cloned.1.call-start = ((), (), s32[]{:S(2)}) async-start(), calls=%async_computation.16 | async-start | bytes 34603008 | tf_op jit(solution)/shard_map/all_gather | solution.py:103
  138.7 1106.2 %reduce-scatter.28.cloned.1.call-start = ((), (), s32[]{:S(2)}) async-start(), calls=%async_computation.25 | async-start | bytes 2359296
  139.9 1.3 copy-start.12
  366.4 0.6 copy-start.35
  369.9 42.7 copy-start.13
  412.7 1.3 copy-start.9
  414.2 581.1 %copy-start.15 = (bf16[256,2048]{1,0:T(8,128)(2,1)}, bf16[256,2048]{1,0:T(8,128)(2,1)S(1)}, u32[]{:S(2)}) copy-start(bf16[256,2048]{1,0:T(8,128)(2,1)S(1)} %multiply_convert_fusion.1) | copy-start | bytes 3145732
  1021.9 17.0 copy-start.10
  1062.7 1.4 copy-start.5
  1070.8 9.6 copy-start.8
  1076.0 6.3 copy-start.36
  1084.5 10.6 copy-start.20
  1095.1 9.9 copy-start
  1143.7 172.0 %reduce-scatter.30.cloned.1.call-start = ((), (), s32[]{:S(2)}) async-start(), calls=%async_computation.26 | async-start | bytes 2359296
  1150.0 98.6 %copy-start.30 = (f32[256,32]{0,1:T(8,128)S(1)}, f32[256,32]{0,1:T(8,128)}, u32[]{:S(2)}) copy-start(f32[256,32]{0,1:T(8,128)} %copy-done.29) | copy-start | bytes 98308
  1150.0 98.6 %copy-start.32 = (f32[256,32]{0,1:T(8,128)S(1)}, f32[256,32]{0,1:T(8,128)}, u32[]{:S(2)}) copy-start(f32[256,32]{0,1:T(8,128)} %copy-done.31) | copy-start | bytes 98308
  1156.5 92.9 %copy-start.4 = (bf16[2,128,2048]{2,1,0:T(8,128)(2,1)S(1)}, bf16[2,128,2048]{2,1,0:T(8,128)(2,1)}, u32[]{:S(2)}) copy-start(bf16[2,128,2048]{2,1,0:T(8,128)(2,1)} %copy-done.3) | copy-start | bytes 3145732
  1156.5 351.3 %reduce-scatter.16.cloned.1.call-start = ((), (), s32[]{:S(2)}) async-start(), calls=%async_computation.19 | async-start | bytes 4325376 | tf_op jit(solution)/shard_map/reduce_scatter | solution.py:324
  1248.7 0.7 copy-start.25
  1252.1 353.4 %reduce-scatter.18.cloned.1.call-start = ((), (), s32[]{:S(2)}) async-start(), calls=%async_computation.20 | async-start | bytes 4325376 | tf_op jit(solution)/shard_map/reduce_scatter | solution.py:325
  1319.4 2.8 copy-start.23
  1322.2 642.0 %reduce-scatter.14.cloned.1.call-start = ((), (), s32[]{:S(2)}) async-start(), calls=%async_computation.18 | async-start | bytes 17301504 | tf_op jit(solution)/shard_map/reduce_scatter | solution.py:323
  1328.7 1.0 copy-start.21
  1337.9 1.6 copy-start.6
  1337.9 1.9 copy-start.14
  1337.9 986.3 %reduce-scatter.20.cloned.1.call-start = ((), (), s32[]{:S(2)}) async-start(), calls=%async_computation.21 | async-start | bytes 17301504 | tf_op jit(solution)/shard_map/reduce_scatter | solution.py:326
  1347.8 1.2 copy-start.16
  1347.8 2381.0 %reduce-scatter.22.cloned.1.call-start = ((), (), s32[]{:S(2)}) async-start(), calls=%async_computation.22 | async-start | bytes 69206016 | tf_op jit(solution)/shard_map/reduce_scatter | solution.py:231
  1374.6 3759.5 %reduce-scatter.24.cloned.1.call-start = ((), (), s32[]{:S(2)}) async-start(), calls=%async_computation.23 | async-start | bytes 69206016 | tf_op jit(solution)/shard_map/reduce_scatter | solution.py:232
  1403.0 1.2 copy-start.19
  1403.0 5136.4 %reduce-scatter.26.cloned.1.call-start = ((), (), s32[]{:S(2)}) async-start(), calls=%async_computation.24 | async-start | bytes 69206016 | tf_op jit(solution)/shard_map/reduce_scatter | solution.py:233
  1429.9 1.2 copy-start.22
  1431.2 7.3 copy-start.11
  1431.2 7.3 copy-start.18
  1438.4 16.7 copy-start.17
  1438.4 16.7 copy-start.26
  1455.1 2.6 copy-start.2
  1455.1 2.6 copy-start.24
  1455.2 2.6 copy-start.27
  1455.2 2.6 copy-start.34
  1455.2 2.6 copy-start.38
  1457.8 2.6 copy-start.39
  1457.8 46.8 copy-start.7
Sparse Core Ops, SparseCore 0:
  11.0 59.2 all-gather.15
  73.2 55.3 all-gather.9
  131.3 64.6 all-gather.17
  198.8 77.3 all-gather.13
  278.7 49.6 all-gather.11
  331.2 75.5 all-gather.19
  409.8 193.3 all-gather.25
  606.2 193.0 all-gather.21
  802.3 192.9 all-gather.23
  1143.9 101.0 reduce-scatter.27
  1249.0 66.6 reduce-scatter.29
  1318.4 142.8 reduce-scatter.15
  1464.1 141.3 reduce-scatter.17
  1608.2 355.8 reduce-scatter.13
  1966.9 357.2 reduce-scatter.19
  2327.0 1401.7 reduce-scatter.21
  3731.6 1402.4 reduce-scatter.23
  5136.9 1402.4 reduce-scatter.25
where the time goes:
time: 6550 us
  waiting for transfers between devices  6000 us (92%)
  matrix products  307 us (5%)
  local copies, waits for them, and re-layouts  99.2 us (2%)
  blocking collectives  85.2 us (1%)
    reduce_scatter x1, waiting for transfers between devices, on_device(): lax.psum_scatter(grad_down, ('fsdp', 'ctx'), scatter_dimension=0, tiled=T...  1410 us
    reduce_scatter x1, waiting for transfers between devices, on_device(): lax.psum_scatter(grad_up_w, ('fsdp', 'ctx'), scatter_dimension=0, tiled=T...  1410 us
    reduce_scatter x1, waiting for transfers between devices, on_device(): lax.psum_scatter(grad_gate_w, ('fsdp', 'ctx'), scatter_dimension=0, tiled...  1400 us
    reduce_scatter x1, waiting for transfers between devices, on_device(): lax.psum_scatter(grad_out_w, ('fsdp', 'ctx'), scatter_dimension=0, tiled=...  360 us
    reduce_scatter x1, waiting for transfers between devices, on_device(): lax.psum_scatter(grad_query_w, ('fsdp', 'ctx'), scatter_dimension=0, tile...  359 us
    all_gather x1, waiting for transfers between devices, on_device(): lax.all_gather(w_down, ('fsdp', 'ctx'), axis=0, tiled=True)  189 us
    all_gather x1, waiting for transfers between devices, on_device(): lax.all_gather(w_gate, ('fsdp', 'ctx'), axis=0, tiled=True)  178 us
    all_gather x1, waiting for transfers between devices, on_device(): lax.all_gather(w_up, ('fsdp', 'ctx'), axis=0, tiled=True)  178 us
  transfers between devices with their start and end apart: 18, of which 17 were waited for; matrix products, arithmetic and copies ran while one was open for 4% of the time, Pallas kernels for 0%

commit v1 on v0

v1 whole, which is shorter than its diff:
```python
import jax
import jax.numpy as jnp
from jax import lax
from jax.sharding import Mesh
from jax.sharding import PartitionSpec as P

HEADS = 32
KVH = 8
HD = 64
EPSILON = 1e-05
NEGATIVE = -1e30
BF = jnp.bfloat16
F32 = jnp.float32
GROUP = ("a", "core", "cl")


def rope_tables(positions, head_width):
    half_width = head_width // 2
    frequency = 500000.0 ** (-jnp.arange(half_width, dtype=F32) * 2.0 / head_width)
    angles = positions.astype(F32)[:, None] * frequency[None, :]
    return jnp.cos(angles), jnp.sin(angles)


def rotate(field, cos, sin):
    half = field.shape[-1] // 2
    u1, u2 = field[..., :half], field[..., half:]
    return jnp.concatenate([u1 * cos - u2 * sin, u2 * cos + u1 * sin], -1)


def rotate_back(field, cos, sin):
    return rotate(field, cos, -sin)


def rms_scale(field):
    return lax.rsqrt(jnp.mean(field * field, -1, keepdims=True) + EPSILON)


def norm_back(grad_normed, normed, scale_rows):
    return scale_rows * (grad_normed - normed * jnp.mean(grad_normed * normed, -1, keepdims=True))


def mm(a, b):
    return jnp.dot(a, b, preferred_element_type=F32)


def mm_tn(a, b):
    return jnp.einsum("rd,re->de", a, b, preferred_element_type=F32)


def mm_nt(a, b):
    return jnp.einsum("re,de->rd", a, b, preferred_element_type=F32)


def gather_group(x):
    return lax.all_gather(x, GROUP, axis=0, tiled=True)


def sum_group(x):
    return lax.psum_scatter(x.astype(BF), GROUP, scatter_dimension=0, tiled=True).astype(F32)


def swap_group(x):
    return lax.all_to_all(x, GROUP, 0, 0, tiled=True)


def rows_of(x):
    nz = lax.axis_size("cm")
    x = lax.all_gather(x, "cm", axis=0)
    _, _, r, c = x.shape
    return x.reshape(nz, 4, 2, r, c).transpose(1, 0, 2, 3, 4).reshape(nz * 8 * r, c)


def rows_to(g):
    nz = lax.axis_size("cm")
    rows, c = g.shape
    r = rows // (8 * nz)
    g = g.astype(BF).reshape(4, nz, 2, r, c).transpose(1, 0, 2, 3, 4).reshape(nz * 8, r, c)
    g = lax.psum_scatter(g, "cm", scatter_dimension=0, tiled=True)
    return swap_group(g)


def on_device(
    tokens, lengths, cotangent, attn_gain, w_query, w_key, w_value, w_out, mlp_gain, w_gate, w_up, w_down
):
    seqs, block, width = tokens.shape
    nz = lax.axis_size("cm")
    rows = seqs * block
    r = w_query.shape[0]
    fb = w_down.shape[0]
    nseq = 4 * seqs
    slots = 2 * block
    length = slots * nz
    qh = HEADS // 8
    scale = HD ** (-0.5)
    cm = lax.axis_index("cm")
    cl = lax.axis_index("cl")

    gains = jnp.stack([attn_gain, mlp_gain], -1)
    gains = jnp.pad(gains, ((0, 0), (0, 126)))
    pack = jnp.concatenate(
        [
            w_query.reshape(r, 8, qh * HD),
            w_key.reshape(r, 8, HD),
            w_value.reshape(r, 8, HD),
            jnp.broadcast_to(gains[:, None], (r, 8, 128)),
        ],
        -1,
    ).transpose(1, 0, 2)
    pack = rows_of(swap_group(pack))
    wqkv = pack[:, : qh * HD + 2 * HD]
    gain_one = pack[:, qh * HD + 2 * HD].astype(F32)
    gain_two = pack[:, qh * HD + 2 * HD + 1].astype(F32)
    perm = [(c, (c % nz) * 2 + c // nz) for c in range(2 * nz)]
    wo = lax.all_gather(lax.ppermute(w_out, ("cm", "cl"), perm), "cm", axis=0, tiled=True)

    def ff_cols(w):
        w = w.reshape(r, 4, nz, 2, fb).transpose(1, 3, 0, 2, 4).reshape(8, r, nz * fb)
        return rows_of(swap_group(w))

    wg = ff_cols(w_gate)
    wu = ff_cols(w_up)
    wd = lax.all_gather(w_down, "cm", axis=0, tiled=True)
    lens = lax.all_gather(lengths, ("a", "core"), axis=0, tiled=True)

    own = tokens.reshape(rows, width)
    resid_in = own.astype(F32)
    tok_all = gather_group(own)
    tok_f = tok_all.astype(F32)
    hidden_one = (tok_f * rms_scale(tok_f) * gain_one).astype(BF)

    def by_seq(x):
        e = x.shape[-1]
        return x.reshape(4, 2, seqs, block, e).transpose(0, 2, 1, 3, 4).reshape(nseq, slots, e)

    def by_row(x):
        e = x.shape[-1]
        return x.reshape(4, seqs, 2, block, e).transpose(0, 2, 1, 3, 4).reshape(8 * rows, e)

    pos = cm * slots + jnp.arange(slots, dtype=jnp.int32)
    cos, sin = rope_tables(pos, HD)
    qkv = by_seq(mm(hidden_one, wqkv))
    q = qkv[..., : qh * HD].reshape(nseq, slots, qh, HD).transpose(0, 2, 1, 3)
    q = rotate(q, cos, sin).astype(BF)
    k = rotate(qkv[..., qh * HD : qh * HD + HD], cos, sin).astype(BF)
    v = qkv[..., qh * HD + HD :].astype(BF)
    kv = lax.all_gather(jnp.concatenate([k, v], -1), "cm", axis=1, tiled=True)
    keys, values = kv[..., :HD], kv[..., HD:]
    key_pos = jnp.arange(length, dtype=jnp.int32)
    allowed = (key_pos[None, None, :] <= pos[None, :, None]) & (key_pos[None, None, :] < lens[:, None, None])
    scores = jnp.einsum("shqd,snd->shqn", q, keys, preferred_element_type=F32) * scale
    scores = jnp.where(allowed[:, None], scores, NEGATIVE)
    top = jnp.max(scores, -1, keepdims=True)
    log_total = top + jnp.log(jnp.sum(jnp.exp(scores - top), -1, keepdims=True))
    soft = jnp.exp(scores - log_total)
    probs = soft.astype(BF)
    attended = jnp.einsum("shqn,snd->shqd", probs, values, preferred_element_type=F32)
    attended_low = by_row(attended.astype(BF).transpose(0, 2, 1, 3).reshape(nseq, slots, qh * HD))

    resid_mid = resid_in + sum_group(mm(attended_low, wo))
    scale_two = rms_scale(resid_mid)
    normed_two = resid_mid * scale_two
    hidden_two = gather_group((normed_two * gain_two).astype(BF))
    gate_pre = mm(hidden_two, wg)
    up_pre = mm(hidden_two, wu)
    sig = jax.nn.sigmoid(gate_pre)
    act = gate_pre * sig
    inner = (act * up_pre).astype(BF)
    layer_out = (resid_mid + sum_group(mm(inner, wd))).astype(BF)

    own_pos = cm * slots + cl * block + jnp.arange(block, dtype=jnp.int32)
    valid = (own_pos[None, :] < lengths[:, None]).astype(F32)
    grad_out = (cotangent.astype(F32) * valid[..., None]).reshape(rows, width)
    grad_low = gather_group(grad_out.astype(BF))
    grad_wd = lax.psum_scatter(mm_tn(inner, grad_low).astype(BF), "cm", scatter_dimension=0, tiled=True)
    grad_inner = mm_nt(grad_low, wd).astype(BF).astype(F32)
    grad_gate = (grad_inner * up_pre * (sig * (1.0 + gate_pre * (1.0 - sig)))).astype(BF)
    grad_up = (grad_inner * act).astype(BF)

    def ff_back(g):
        g = rows_to(g)
        return g.reshape(4, 2, r, nz, fb).transpose(2, 0, 3, 1, 4).reshape(r, 8 * nz * fb).astype(F32)

    grad_wg = ff_back(mm_tn(hidden_two, grad_gate))
    grad_wu = ff_back(mm_tn(hidden_two, grad_up))
    grad_hidden_two = sum_group(mm_nt(grad_gate, wg) + mm_nt(grad_up, wu))
    gain_grad_two = jnp.sum(grad_wg * w_gate.astype(F32) + grad_wu * w_up.astype(F32), -1) / mlp_gain.astype(F32)
    grad_mid = grad_out + norm_back(grad_hidden_two * gain_two, normed_two, scale_two)
    grad_attn = gather_group(grad_mid.astype(BF))
    grad_wo = lax.psum_scatter(mm_tn(attended_low, grad_attn).astype(BF), "cm", scatter_dimension=0, tiled=True)
    grad_wo = lax.ppermute(grad_wo, ("cm", "cl"), [(t, s) for s, t in perm]).astype(F32)
    grad_heads = by_seq(mm_nt(grad_attn, wo).astype(BF)).reshape(nseq, slots, qh, HD).transpose(0, 2, 1, 3)
    delta = jnp.sum(grad_heads.astype(F32) * attended, -1, keepdims=True)
    grad_soft = jnp.einsum("shqd,snd->shqn", grad_heads, values, preferred_element_type=F32)
    grad_scores = (scale * soft * (grad_soft - delta)).astype(BF)
    grad_q = jnp.einsum("shqn,snd->shqd", grad_scores, keys, preferred_element_type=F32)
    grad_k = jnp.einsum("shqn,shqd->snd", grad_scores, q, preferred_element_type=F32)
    grad_v = jnp.einsum("shqn,shqd->snd", probs, grad_heads, preferred_element_type=F32)
    grad_kv = jnp.concatenate([grad_k, grad_v], -1).astype(BF)
    grad_kv = lax.psum_scatter(grad_kv, "cm", scatter_dimension=1, tiled=True).astype(F32)
    grad_rows = by_row(
        jnp.concatenate(
            [
                rotate_back(grad_q, cos, sin).transpose(0, 2, 1, 3).reshape(nseq, slots, qh * HD).astype(BF),
                rotate_back(grad_kv[..., :HD], cos, sin).astype(BF),
                grad_kv[..., HD:].astype(BF),
            ],
            -1,
        )
    )
    back = rows_to(mm_tn(hidden_one, grad_rows))
    back = back.transpose(1, 0, 2).astype(F32)
    grad_wq = back[..., : qh * HD].reshape(r, HEADS * HD)
    grad_wk = back[..., qh * HD : qh * HD + HD].reshape(r, KVH * HD)
    grad_wv = back[..., qh * HD + HD :].reshape(r, KVH * HD)
    gain_grad_one = (
        jnp.sum(grad_wq * w_query.astype(F32), -1)
        + jnp.sum(grad_wk * w_key.astype(F32), -1)
        + jnp.sum(grad_wv * w_value.astype(F32), -1)
    ) / attn_gain.astype(F32)
    grad_hidden_one = sum_group(mm_nt(grad_rows, wqkv))
    scale_one = rms_scale(resid_in)
    grad_tokens = grad_mid + norm_back(grad_hidden_one * gain_one, resid_in * scale_one, scale_one)
    return (
        layer_out.reshape(seqs, block, width),
        grad_tokens.reshape(seqs, block, width).astype(BF),
        gain_grad_one,
        grad_wq,
        grad_wk,
        grad_wv,
        grad_wo,
        gain_grad_two,
        grad_wg,
        grad_wu,
        grad_wd.astype(F32),
    )


def solution(mesh):
    fsdp, ctx = mesh.devices.shape
    fine = Mesh(mesh.devices.reshape(fsdp // 2, 2, ctx // 2, 2), ("a", "core", "cm", "cl"))
    token = P(("a", "core"), ("cm", "cl"), None)
    vector = P(("a", "core", "cm", "cl"))
    matrix = P(("a", "core", "cm", "cl"), None)
    return jax.shard_map(
        on_device,
        mesh=fine,
        in_specs=(
            token,
            P(("a", "core")),
            token,
            vector,
            matrix,
            matrix,
            matrix,
            matrix,
            vector,
            matrix,
            matrix,
            matrix,
        ),
        out_specs=(token, token, vector, matrix, matrix, matrix, matrix, vector, matrix, matrix, matrix),
        check_vma=False,
    )
```

time: 6550 us -> 1480 us (0.23)
  waiting for transfers between devices: 6000 us -> 962 us
    reduce_scatter x7 -> x10, waiting for transfers between devices: 5030 us -> 438 us  [the longest x4 224 us: sum_group(): lax.psum_scatter(x.astype(BF), GROUP, scatter_dimension=0, tiled=True)]
    all_gather x9 -> x10, waiting for transfers between devices: 814 us -> 519 us  [the longest x4 206 us: gather_group(): return lax.all_gather(x, GROUP, axis=0, tiled=True)]
    unnamed x20, waiting for transfers between devices: 157 us -> 1.69 us
    unnamed x2 -> x1, blocking collectives: 85.2 us -> 4.88 us
    dot_general x28 -> x21, matrix products: 307 us -> 267 us  [the longest x5 61.8 us: mm(): return jnp.dot(a, b, preferred_element_type=F32)]
  transfers between devices with their start and end apart: 18 -> 25, of which waited for: 17 -> 19; matrix products, arithmetic and copies ran while one was open for 4% -> 16% of each run, Pallas kernels for 0% -> 0%
where the time goes in v1:
time: 1480 us; the launch traced here: 1470 us
  waiting for transfers between devices  962 us (65%)
  matrix products  267 us (18%)
  local copies, waits for them, and re-layouts  74.4 us (5%)
  other arithmetic  66.9 us (5%)
  blocking collectives  66.9 us (5%)
  starting transfers between devices  18 us (1%)
  between operations  16.1 us (1%)
    reduce_scatter x4, waiting for transfers between devices, sum_group(): lax.psum_scatter(x.astype(BF), GROUP, scatter_dimension=0, tiled=True)  224 us
    all_gather x4, waiting for transfers between devices, gather_group(): return lax.all_gather(x, GROUP, axis=0, tiled=True)  206 us
    all_gather x3, waiting for transfers between devices, rows_of(): x = lax.all_gather(x, 'cm', axis=0)  199 us
    reduce_scatter x3, waiting for transfers between devices, rows_to(): g = lax.psum_scatter(g, 'cm', scatter_dimension=0, tiled=True)  132 us
    all_gather x1, waiting for transfers between devices, on_device(): wd = lax.all_gather(w_down, 'cm', axis=0, tiled=True)  76.1 us
    reduce_scatter x1, waiting for transfers between devices, on_device(): lax.psum_scatter(mm_tn(inner, grad_low).astype(BF), 'cm', scatter_dimensi...  74.4 us
    all_to_all x3, blocking collectives, swap_group(): return lax.all_to_all(x, GROUP, 0, 0, tiled=True)  62 us
    dot_general x5, matrix products, mm(): return jnp.dot(a, b, preferred_element_type=F32)  61.8 us
  transfers between devices with their start and end apart: 25, of which 19 were waited for; matrix products, arithmetic and copies ran while one was open for 16% of the time, Pallas kernels for 0%

profile of v1, /device:TPU:0, one launch (start us, length us, event | category | flops | bytes accessed | tf_op | source)
XLA Modules:
  0.0 1471.2 jit_solution(13465474489473135161)
XLA Ops:
  11.4 13.9 all_to_all.30
  27.0 44.7 %all-gather.28.cloned.1.call-done = bf16[32,64,512]{2,1,0:T(8,128)(2,1)} async-done(((bf16[8,64,512]{2,1,0:T(8,128)(2,1)}), bf16[32,64,512]{2,1,0:T(8,128)(2,1)}) %all-gather.28.cloned.1.call-update) | async-done | bytes 2097168 | tf_op jit(solution)/shard_map/all_gather | solution.py:68
  74.0 52.7 %all-gather.14.cloned.1.call-done = bf16[2048,2048]{1,0:T(8,128)(2,1)} async-done(((bf16[256,2048]{1,0:T(8,128)(2,1)}), bf16[2048,2048]{1,0:T(8,128)(2,1)}) %all-gather.14.cloned.1.call-update) | async-done | bytes 8388624 | tf_op jit(solution)/shard_map/all_gather | solution.py:55
  126.7 5.2 fusion.2
  132.5 6.3 fusion.12
  138.8 4.3 copy.129
  143.0 3.7 reshape.464
  152.9 4.9 all-reduce.1
  161.7 38.8 %all-gather.16.cloned.1.call-done = bf16[8,1024,128]{1,2,0:T(8,128)(2,1)} async-done(((bf16[8,256,128]{1,2,0:T(8,128)(2,1)}), bf16[8,1024,128]{1,2,0:T(8,128)(2,1)}) %all-gather.16.cloned.1.call-update) | async-done | bytes 2097168 | tf_op jit(solution)/shard_map/all_gather | solution.py:146
  200.5 15.8 %fusion.1 = (f32[8,4,256]{2,1,0:T(4,128)S(1)}, f32[8,4,256,1024]{3,2,1,0:T(8,128)}) fusion(pred[8,256,1024]{2,1,0:T(8,128)(4,1)} %broadcast_and_fusion, bf16[8,1024,128]{1,2,0:T(8,128)(2,1)} %all-gather.16.cloned.1.call-done, bf16[8,4,256,32]{2,3,1,0:T(8,128)(2,1)S(1)} %get-tuple-element.20, bf16[8,4,256,32]{2,3,1,0:T(8,128)(2,1)S(1)} %get-tuple-element.19), kind=kOutput, calls=%fused_computation.5 | convolution fusion | flops 1100996608 | bytes 37781504 | tf_op jit(solution)/shard_map/shqd,snd->shqn/dot_general | solution.py:150
  216.3 15.3 %exponential_reduce_fusion = f32[8,4,256]{2,1,0:T(4,128)S(1)} fusion(f32[8,4,256,1024]{3,2,1,0:T(8,128)} %get-tuple-element.31, f32[8,4,256]{2,1,0:T(4,128)S(1)} %get-tuple-element.30, pred[8,256,1024]{2,1,0:T(8,128)(4,1)S(1)} %copy-done.6), kind=kLoop, calls=%fused_computation.2 | loop fusion | flops 33546240 | bytes 35717120 | tf_op jit(solution)/shard_map/reduce_sum | solution.py:153
  231.6 15.7 %fusion.26 = f32[8,4,256,64]{2,3,1,0:T(8,128)} fusion(bf16[8,1024,128]{1,2,0:T(8,128)(2,1)} %all-gather.16.cloned.1.call-done, f32[8,4,256,1024]{3,2,1,0:T(8,128)} %get-tuple-element.31, f32[8,4,256]{2,1,0:T(4,128)S(1)} %bitcast.189, pred[8,256,1024]{2,1,0:T(8,128)(4,1)S(1)} %copy-done.6), kind=kOutput, calls=%fused_computation.78 | convolution fusion | flops 1107296256 | bytes 38830080 | tf_op jit(solution)/shard_map/shqn,snd->shqd/dot_general | solution.py:156
  250.2 7.2 convolution_convert_fusion.2
  260.6 19.0 %all_to_all.31 = bf16[8,64,1024]{2,1,0:T(8,128)(2,1)} all-to-all(bf16[8,64,1024]{2,1,0:T(8,128)(2,1)S(1)} %reshape.468), channel_id=1, replica_groups=mesh['a'=2,'core'=2,'cm'=4,'cl'=2] {'a','core','cl'}, dimensions={0} | all-to-all | bytes 2097152 | tf_op jit(solution)/shard_map/all_to_all | solution.py:63
  281.6 29.1 %all_to_all.32 = bf16[8,64,1024]{2,1,0:T(8,128)(2,1)} all-to-all(bf16[8,64,1024]{2,1,0:T(8,128)(2,1)S(1)} %reshape.472), channel_id=1, replica_groups=mesh['a'=2,'core'=2,'cm'=4,'cl'=2] {'a','core','cl'}, dimensions={0} | all-to-all | bytes 2097152 | tf_op jit(solution)/shard_map/all_to_all | solution.py:63
  314.4 24.9 %reduce-scatter.11.cloned.1.call-done = bf16[256,2048]{1,0:T(8,128)(2,1)} async-done(((bf16[2048,2048]{1,0:T(8,128)(2,1)}), bf16[256,2048]{1,0:T(8,128)(2,1)}) %reduce-scatter.11.cloned.1.call-update) | async-done | bytes 1048592 | tf_op jit(solution)/shard_map/reduce_scatter | solution.py:59
  341.0 2.6 multiply_convert_fusion.2
  343.6 78.0 %all-gather.30.cloned.1.call-done = bf16[32,64,1024]{2,1,0:T(8,128)(2,1)} async-done(((bf16[8,64,1024]{2,1,0:T(8,128)(2,1)}), bf16[32,64,1024]{2,1,0:T(8,128)(2,1)}) %all-gather.30.cloned.1.call-update) | async-done | bytes 4194320 | tf_op jit(solution)/shard_map/all_gather | solution.py:68
  421.6 5.0 copy.132
  426.6 76.0 %all-gather.32.cloned.1.call-done = bf16[32,64,1024]{2,1,0:T(8,128)(2,1)} async-done(((bf16[8,64,1024]{2,1,0:T(8,128)(2,1)}), bf16[32,64,1024]{2,1,0:T(8,128)(2,1)}) %all-gather.32.cloned.1.call-update) | async-done | bytes 4194320 | tf_op jit(solution)/shard_map/all_gather | solution.py:68
  502.6 4.9 copy.134
  507.4 76.1 %all-gather.22.cloned.1.call-done = bf16[1024,2048]{1,0:T(8,128)(2,1)} async-done(((bf16[256,2048]{1,0:T(8,128)(2,1)}), bf16[1024,2048]{1,0:T(8,128)(2,1)}) %all-gather.22.cloned.1.call-update) | async-done | bytes 4194320 | tf_op jit(solution)/shard_map/all_gather | solution.py:122
  583.6 55.6 %all-gather.24.cloned.1.call-done = bf16[2048,2048]{1,0:T(8,128)(2,1)} async-done(((bf16[256,2048]{1,0:T(8,128)(2,1)}), bf16[2048,2048]{1,0:T(8,128)(2,1)}) %all-gather.24.cloned.1.call-update) | async-done | bytes 8388624 | tf_op jit(solution)/shard_map/all_gather | solution.py:55
  639.1 13.9 convolution_convert_fusion.4
  653.0 43.0 %all-gather.20.cloned.1.call-done = bf16[2048,2048]{1,0:T(8,128)(2,1)} async-done(((bf16[256,2048]{1,0:T(8,128)(2,1)}), bf16[2048,2048]{1,0:T(8,128)(2,1)}) %all-gather.20.cloned.1.call-update) | async-done | bytes 8388624 | tf_op jit(solution)/shard_map/all_gather | solution.py:55
  696.0 14.6 fusion.37
  710.6 19.7 %fusion.6 = (bf16[2048,1024]{1,0:T(8,128)(2,1)S(1)}, bf16[2048,1024]{1,0:T(8,128)(2,1)}) fusion(bf16[2048,1024]{1,0:T(8,128)(2,1)} %convolution_convert_fusion.4, f32[2048,1024]{1,0:T(8,128)} %fusion.37, bf16[2048,2048]{1,0:T(8,128)(2,1)} %all-gather.20.cloned.1.call-done, bf16[2048,1024]{1,0:T(8,128)(2,1)S(1)} %bitcast.168), kind=kOutput, calls=%fused_computation.15 | convolution fusion | flops 8619294720 | bytes 33554432 | tf_op jit(solution)/shard_map/dot_general | solution.py:43
  732.2 11.7 fusion.38
  744.0 20.5 %add_convert_fusion = bf16[2048,2048]{1,0:T(8,128)(2,1)} fusion(f32[2048,2048]{1,0:T(8,128)} %fusion.38, bf16[2048,1024]{1,0:T(8,128)(2,1)} %bitcast.167, bf16[2048,1024]{1,0:T(8,128)(2,1)} %convolution_convert_fusion.4, f32[2048,1024]{1,0:T(8,128)} %fusion.37), kind=kOutput, calls=%fused_computation.11 | convolution fusion | flops 8613003264 | bytes 41943040 | tf_op jit(solution)/shard_map/re,de->rd/dot_general | solution.py:51
  764.6 71.4 %reduce-scatter.15.cloned.1.call-done = bf16[256,2048]{1,0:T(8,128)(2,1)} async-done(((bf16[2048,2048]{1,0:T(8,128)(2,1)}), bf16[256,2048]{1,0:T(8,128)(2,1)}) %reduce-scatter.15.cloned.1.call-update) | async-done | bytes 1048592 | tf_op jit(solution)/shard_map/reduce_scatter | solution.py:59
  838.2 3.3 fusion.33
  841.6 54.5 %all-gather.26.cloned.1.call-done = bf16[2048,2048]{1,0:T(8,128)(2,1)} async-done(((bf16[256,2048]{1,0:T(8,128)(2,1)}), bf16[2048,2048]{1,0:T(8,128)(2,1)}) %all-gather.26.cloned.1.call-update) | async-done | bytes 8388624 | tf_op jit(solution)/shard_map/all_gather | solution.py:55
  896.1 6.0 convolution_convert_fusion.9
  908.3 15.7 %bitcast_convert_fusion = bf16[8,1024,64]{1,2,0:T(8,128)(2,1)} fusion(bf16[8,256,4,64]{1,3,2,0:T(8,128)(2,1)S(1)} %reshape_reshape.7, f32[8,4,256,1024]{3,2,1,0:T(8,128)} %get-tuple-element.31, f32[8,4,256]{2,1,0:T(4,128)S(1)} %bitcast.190, pred[8,256,1024]{2,1,0:T(8,128)(4,1)S(1)} %copy-done.7), kind=kOutput, calls=%fused_computation.42 | convolution fusion | flops 1107820544 | bytes 37781504 | tf_op jit(solution)/shard_map/shqn,shqd->snd/dot_general | solution.py:197
  924.0 22.0 %multiply_convert_fusion = bf16[8,4,256,1024]{3,2,1,0:T(8,128)(2,1)} fusion(f32[8,4,256,1024]{3,2,1,0:T(8,128)} %get-tuple-element.31, f32[8,4,256]{2,1,0:T(4,128)S(1)} %multiply_reduce_fusion, f32[8,4,256]{2,1,0:T(4,128)S(1)} %bitcast.191, pred[8,256,1024]{2,1,0:T(8,128)(4,1)S(1)} %copy-done.7, bf16[8,256,4,64]{1,3,2,0:T(8,128)(2,1)S(1)} %reshape_reshape.7, ...), kind=kOutput, calls=%fused_computation | convolution fusion | flops 1132462080 | bytes 54591488 | tf_op jit(solution)/shard_map/shqd,snd->shqn/dot_general | solution.py:193
  946.1 8.9 bitcast_convert_fusion.1
  956.7 14.8 %convolution_convert_fusion.5 = bf16[2048,1024]{1,0:T(8,128)(2,1)S(1)} fusion(bf16[2048,2048]{1,0:T(8,128)(2,1)} %all-gather.20.cloned.1.call-done, bf16[2048,1024]{1,0:T(8,128)(2,1)} %convolution_convert_fusion.4, f32[2048,1024]{1,0:T(8,128)} %fusion.37), kind=kOutput, calls=%fused_computation.26 | convolution fusion | flops 8606711808 | bytes 25165824 | tf_op jit(solution)/shard_map/rd,re->de/dot_general | solution.py:47
  971.5 2.5 copy.147
  974.0 12.7 convolution_convert_fusion.6
  989.3 14.1 convolution_convert_fusion.3
  1004.6 6.7 convolution_convert_fusion.8
  1011.4 9.4 fusion.24
  1025.7 9.0 convolution_convert_fusion.7
  1036.9 8.3 convolution_convert_fusion
  1045.3 14.1 convolution_convert_fusion.1
  1059.4 19.6 %reduce-scatter.27.cloned.1.call-done = bf16[8,64,1024]{2,1,0:T(8,128)(2,1)} async-done(((bf16[32,64,1024]{2,1,0:T(8,128)(2,1)}), bf16[8,64,1024]{2,1,0:T(8,128)(2,1)}) %reduce-scatter.27.cloned.1.call-update) | async-done | bytes 1048592 | tf_op jit(solution)/shard_map/reduce_scatter | solution.py:78
  1079.0 3.7 all-to-all-start.5
  1082.7 75.8 %reduce-scatter.25.cloned.1.call-done = bf16[8,64,1024]{2,1,0:T(8,128)(2,1)} async-done(((bf16[32,64,1024]{2,1,0:T(8,128)(2,1)}), bf16[8,64,1024]{2,1,0:T(8,128)(2,1)}) %reduce-scatter.25.cloned.1.call-update) | async-done | bytes 1048592 | tf_op jit(solution)/shard_map/reduce_scatter | solution.py:78
  1158.5 4.2 all-to-all-start.4
  1163.6 74.4 %reduce-scatter.29.cloned.1.call-done = bf16[256,2048]{1,0:T(8,128)(2,1)} async-done(((bf16[1024,2048]{1,0:T(8,128)(2,1)}), bf16[256,2048]{1,0:T(8,128)(2,1)}) %reduce-scatter.29.cloned.1.call-update) | async-done | bytes 1048592 | tf_op jit(solution)/shard_map/reduce_scatter | solution.py:174
  1238.0 2.8 convert_element_type.277
  1242.8 2.9 copy.148
  1245.7 2.9 reshape.492
  1248.7 3.4 reshape.493
  1252.1 4.6 copy.146
  1256.6 3.9 reshape.491
  1260.5 7.9 reduce-scatter.23.cloned.1.call-done
  1268.4 3.6 collective-permute-start.1
  1272.0 36.5 %reduce-scatter.21.cloned.1.call-done = bf16[8,64,384]{2,1,0:T(8,128)(2,1)} async-done(((bf16[32,64,384]{2,1,0:T(8,128)(2,1)}), bf16[8,64,384]{2,1,0:T(8,128)(2,1)}) %reduce-scatter.21.cloned.1.call-update) | async-done | bytes 393232 | tf_op jit(solution)/shard_map/reduce_scatter | solution.py:78
  1308.5 3.7 all-to-all-start.3
  1312.1 2.7 add_reduce_fusion
  1329.4 54.9 %reduce-scatter.19.cloned.1.call-done = bf16[256,2048]{1,0:T(8,128)(2,1)} async-done(((bf16[2048,2048]{1,0:T(8,128)(2,1)}), bf16[256,2048]{1,0:T(8,128)(2,1)}) %reduce-scatter.19.cloned.1.call-update) | async-done | bytes 1048592 | tf_op jit(solution)/shard_map/reduce_scatter | solution.py:59
  1386.1 72.8 %reduce-scatter.13.cloned.1.call-done = bf16[256,2048]{1,0:T(8,128)(2,1)} async-done(((bf16[2048,2048]{1,0:T(8,128)(2,1)}), bf16[256,2048]{1,0:T(8,128)(2,1)}) %reduce-scatter.13.cloned.1.call-update) | async-done | bytes 1048592 | tf_op jit(solution)/shard_map/reduce_scatter | solution.py:59
  1458.9 5.2 fusion.18
  (215 shorter events, 73.2 us)
Async XLA Ops:
  7.2 64.5 %all-gather.28.cloned.1.call-start = ((), (), s32[]{:S(2)}) async-start(), calls=%async_computation.33 | async-start | bytes 2621440 | tf_op jit(solution)/shard_map/all_gather | solution.py:68
  25.3 101.4 %all-gather.14.cloned.1.call-start = ((), (), s32[]{:S(2)}) async-start(), calls=%async_computation.16 | async-start | bytes 9437184 | tf_op jit(solution)/shard_map/all_gather | solution.py:55
  26.1 174.4 %all-gather.16.cloned.1.call-start = ((), (), s32[]{:S(2)}) async-start(), calls=%async_computation.17 | async-start | bytes 2621440 | tf_op jit(solution)/shard_map/all_gather | solution.py:146
  26.9 134.4 %copy-start.24 = (f32[256,32]{0,1:T(8,128)}, f32[256,32]{0,1:T(8,128)S(1)}, u32[]{:S(2)}) copy-start(f32[256,32]{0,1:T(8,128)S(1)} %get-tuple-element.29) | copy-start | bytes 98308
  73.4 58.5 %copy-start.10 = (bf16[4,4,2,64,512]{4,3,2,1,0:T(8,128)(2,1)}, bf16[4,4,2,64,512]{4,3,2,1,0:T(8,128)(2,1)S(1)}, u32[]{:S(2)}) copy-start(bf16[4,4,2,64,512]{4,3,2,1,0:T(8,128)(2,1)S(1)} %copy.128) | copy-start | bytes 6291460
  73.9 58.0 %copy-start.31 = (f32[2048]{0:T(1024)}, f32[2048]{0:T(1024)S(1)}, u32[]{:S(2)}) copy-start(f32[2048]{0:T(1024)S(1)} %get-tuple-element.12) | copy-start | bytes 24580
  74.0 764.2 %copy-start.29 = (f32[2048]{0:T(1024)}, f32[2048]{0:T(1024)S(1)}, u32[]{:S(2)}) copy-start(f32[2048]{0:T(1024)S(1)} %get-tuple-element.11) | copy-start | bytes 24580
  126.7 5.8 copy-start.9
  131.9 6.8 copy-start.37
  143.0 6.8 copy-start.41
  143.0 8.0 copy-start.39
  148.9 12.4 slice-start
  149.8 100.5 %all-gather.18.cloned.1.call-start = ((), (), s32[]{:S(2)}) async-start(), calls=%async_computation.18 | async-start | bytes 1310720 | tf_op jit(solution)/shard_map/all_gather | solution.py:114
  151.3 9.1 collective-permute-start
  161.1 178.2 %reduce-scatter.11.cloned.1.call-start = ((), (), s32[]{:S(2)}) async-start(), calls=%async_computation.19 | async-start | bytes 9437184 | tf_op jit(solution)/shard_map/reduce_scatter | solution.py:59
  161.7 54.5 %copy-start.18 = (bf16[8,4,256,32]{2,3,1,0:T(8,128)(2,1)}, bf16[8,4,256,32]{2,3,1,0:T(8,128)(2,1)S(1)}, u32[]{:S(2)}) copy-start(bf16[8,4,256,32]{2,3,1,0:T(8,128)(2,1)S(1)} %get-tuple-element.19) | copy-start | bytes 1572868
  161.7 54.5 %copy-start.20 = (bf16[8,4,256,32]{2,3,1,0:T(8,128)(2,1)}, bf16[8,4,256,32]{2,3,1,0:T(8,128)(2,1)S(1)}, u32[]{:S(2)}) copy-start(bf16[8,4,256,32]{2,3,1,0:T(8,128)(2,1)S(1)} %get-tuple-element.20) | copy-start | bytes 1572868
  200.5 15.8 %copy-start.6 = (pred[8,256,1024]{2,1,0:T(8,128)(4,1)S(1)}, pred[8,256,1024]{2,1,0:T(8,128)(4,1)}, u32[]{:S(2)}) copy-start(pred[8,256,1024]{2,1,0:T(8,128)(4,1)} %broadcast_and_fusion) | copy-start | bytes 6291460
  231.6 15.8 %copy-start.33 = (f32[4,8,256]{2,1,0:T(8,128)}, f32[4,8,256]{2,1,0:T(8,128)S(1)}, u32[]{:S(2)}) copy-start(f32[4,8,256]{2,1,0:T(8,128)S(1)} %log_add_fusion) | copy-start | bytes 98308
  250.2 7.2 copy-start.4
  257.4 164.2 %all-gather.30.cloned.1.call-start = ((), (), s32[]{:S(2)}) async-start(), calls=%async_computation.34 | async-start | bytes 5242880 | tf_op jit(solution)/shard_map/all_gather | solution.py:68
  259.4 20.2 %copy-start.14 = (bf16[64,8192]{1,0:T(8,128)(2,1)S(1)}, bf16[64,8192]{1,0:T(8,128)(2,1)}, u32[]{:S(2)}) copy-start(bf16[64,8192]{1,0:T(8,128)(2,1)} %param.22) | copy-start | bytes 3145732
  279.6 223.0 %all-gather.32.cloned.1.call-start = ((), (), s32[]{:S(2)}) async-start(), calls=%async_computation.35 | async-start | bytes 5242880 | tf_op jit(solution)/shard_map/all_gather | solution.py:68
  310.8 28.5 %copy-start = (bf16[2,128,2048]{2,1,0:T(8,128)(2,1)S(1)}, bf16[2,128,2048]{2,1,0:T(8,128)(2,1)}, u32[]{:S(2)}) copy-start(bf16[2,128,2048]{2,1,0:T(8,128)(2,1)} %param.12) | copy-start | bytes 3145732
  310.8 272.7 %all-gather.22.cloned.1.call-start = ((), (), s32[]{:S(2)}) async-start(), calls=%async_computation.21 | async-start | bytes 5242880 | tf_op jit(solution)/shard_map/all_gather | solution.py:122
  311.6 327.6 %all-gather.24.cloned.1.call-start = ((), (), s32[]{:S(2)}) async-start(), calls=%async_computation.23 | async-start | bytes 9437184 | tf_op jit(solution)/shard_map/all_gather | solution.py:55
  313.1 525.1 %copy-start.2 = (f32[2,128,2048]{2,1,0:T(8,128)}, f32[2,128,2048]{2,1,0:T(8,128)S(1)}, u32[]{:S(2)}) copy-start(f32[2,128,2048]{2,1,0:T(8,128)S(1)} %convert_multiply_fusion.7) | copy-start | bytes 6291460
  314.3 381.7 %all-gather.20.cloned.1.call-start = ((), (), s32[]{:S(2)}) async-start(), calls=%async_computation.20 | async-start | bytes 9437184 | tf_op jit(solution)/shard_map/all_gather | solution.py:55
  341.0 497.2 %copy-start.35 = (f32[256]{0:T(256)}, f32[256]{0:T(256)S(1)}, u32[]{:S(2)}) copy-start(f32[256]{0:T(256)S(1)} %add_rsqrt_fusion.1) | copy-start | bytes 3076
  343.6 492.4 %reduce-scatter.15.cloned.1.call-start = ((), (), s32[]{:S(2)}) async-start(), calls=%async_computation.24 | async-start | bytes 9437184 | tf_op jit(solution)/shard_map/reduce_scatter | solution.py:59
  696.0 14.6 copy-start.17
  710.6 21.7 %copy-start.16 = (bf16[4,4,2,64,1024]{4,3,2,1,0:T(8,128)(2,1)S(1)}, bf16[4,4,2,64,1024]{4,3,2,1,0:T(8,128)(2,1)}, u32[]{:S(2)}) copy-start(bf16[4,4,2,64,1024]{4,3,2,1,0:T(8,128)(2,1)} %copy.132) | copy-start | bytes 12582916
  730.3 2.0 copy-start.42
  764.5 131.6 %all-gather.26.cloned.1.call-start = ((), (), s32[]{:S(2)}) async-start(), calls=%async_computation.25 | async-start | bytes 9437184 | tf_op jit(solution)/shard_map/all_gather | solution.py:55
  838.2 63.9 %copy-start.36 = (f32[256]{0:T(256)}, f32[256]{0:T(256)S(1)}, u32[]{:S(2)}) copy-start(f32[256]{0:T(256)S(1)} %broadcast_multiply_fusion.1) | copy-start | bytes 3076
  841.6 180.2 %reduce-scatter.17.cloned.1.call-start = ((), (), s32[]{:S(2)}) async-start(), calls=%async_computation.26 | async-start | bytes 2621440 | tf_op jit(solution)/shard_map/reduce_scatter | solution.py:199
  902.1 6.1 copy-start.7
  902.1 6.1 copy-start.34
  924.0 22.1 %copy-start.19 = (bf16[8,4,256,32]{2,3,1,0:T(8,128)(2,1)S(1)}, bf16[8,4,256,32]{2,3,1,0:T(8,128)(2,1)}, u32[]{:S(2)}) copy-start(bf16[8,4,256,32]{2,3,1,0:T(8,128)(2,1)} %copy-done.18) | copy-start | bytes 1572868
  924.0 22.1 %copy-start.21 = (bf16[8,4,256,32]{2,3,1,0:T(8,128)(2,1)S(1)}, bf16[8,4,256,32]{2,3,1,0:T(8,128)(2,1)}, u32[]{:S(2)}) copy-start(bf16[8,4,256,32]{2,3,1,0:T(8,128)(2,1)} %copy-done.20) | copy-start | bytes 1572868
  946.1 8.9 copy-start.23
  956.6 122.4 %reduce-scatter.27.cloned.1.call-start = ((), (), s32[]{:S(2)}) async-start(), calls=%async_computation.31 | async-start | bytes 5242880 | tf_op jit(solution)/shard_map/reduce_scatter | solution.py:78
  974.0 184.5 %reduce-scatter.25.cloned.1.call-start = ((), (), s32[]{:S(2)}) async-start(), calls=%async_computation.30 | async-start | bytes 5242880 | tf_op jit(solution)/shard_map/reduce_scatter | solution.py:78
  989.2 248.8 %reduce-scatter.29.cloned.1.call-start = ((), (), s32[]{:S(2)}) async-start(), calls=%async_computation.32 | async-start | bytes 5242880 | tf_op jit(solution)/shard_map/reduce_scatter | solution.py:174
  1003.4 265.0 %reduce-scatter.23.cloned.1.call-start = ((), (), s32[]{:S(2)}) async-start(), calls=%async_computation.29 | async-start | bytes 1310720 | tf_op jit(solution)/shard_map/reduce_scatter | solution.py:189
  1011.3 9.5 copy-start.25
  1011.3 9.5 copy-start.27
  1011.4 297.1 %reduce-scatter.21.cloned.1.call-start = ((), (), s32[]{:S(2)}) async-start(), calls=%async_computation.28 | async-start | bytes 1966080 | tf_op jit(solution)/shard_map/reduce_scatter | solution.py:78
  1024.3 1.3 copy-start.32
  1025.6 9.1 copy-start.22
  1034.7 2.2 copy-start.11
  1036.1 348.2 %reduce-scatter.19.cloned.1.call-start = ((), (), s32[]{:S(2)}) async-start(), calls=%async_computation.27 | async-start | bytes 9437184 | tf_op jit(solution)/shard_map/reduce_scatter | solution.py:59
  1045.2 413.7 %reduce-scatter.13.cloned.1.call-start = ((), (), s32[]{:S(2)}) async-start(), calls=%async_computation.22 | async-start | bytes 9437184 | tf_op jit(solution)/shard_map/reduce_scatter | solution.py:59
  1059.4 103.3 %copy-start.1 = (bf16[2,128,2048]{2,1,0:T(8,128)(2,1)S(1)}, bf16[2,128,2048]{2,1,0:T(8,128)(2,1)}, u32[]{:S(2)}) copy-start(bf16[2,128,2048]{2,1,0:T(8,128)(2,1)} %param.12) | copy-start | bytes 3145732
  1079.0 79.4 %all-to-all-start.5 = ((bf16[8,64,1024]{2,1,0:T(8,128)(2,1)}), bf16[8,64,1024]{2,1,0:T(8,128)(2,1)S(1)}, u32[]{:S(2)}, u32[]{:S(2)}) async-start(bf16[8,64,1024]{2,1,0:T(8,128)(2,1)} %reduce-scatter.27.cloned.1.call-done), calls=%async_computation.14 | async-start | bytes 2097152 | tf_op jit(solution)/shard_map/all_to_all | solution.py:63
  1158.5 79.5 %copy-start.15 = (bf16[8,64,1024]{2,1,0:T(8,128)(2,1)}, bf16[8,64,1024]{2,1,0:T(8,128)(2,1)S(1)}, u32[]{:S(2)}) copy-start(bf16[8,64,1024]{2,1,0:T(8,128)(2,1)S(1)} %all-to-all-done.5) | copy-start | bytes 3145732
  1158.5 90.2 %all-to-all-start.4 = ((bf16[8,64,1024]{2,1,0:T(8,128)(2,1)}), bf16[8,64,1024]{2,1,0:T(8,128)(2,1)}, u32[]{:S(2)}, u32[]{:S(2)}) async-start(bf16[8,64,1024]{2,1,0:T(8,128)(2,1)} %reduce-scatter.25.cloned.1.call-done), calls=%async_computation.12 | async-start | bytes 2097152 | tf_op jit(solution)/shard_map/all_to_all | solution.py:63
  1248.7 63.4 %copy-start.8 = (f32[64,8192]{1,0:T(8,128)}, f32[64,8192]{1,0:T(8,128)S(1)}, u32[]{:S(2)}) copy-start(f32[64,8192]{1,0:T(8,128)S(1)} %reshape.492) | copy-start | bytes 6291460
  1260.5 54.3 %copy-start.40 = (bf16[64]{0:T(256)(128)(2,1)S(1)}, bf16[64]{0:T(256)(128)(2,1)}, u32[]{:S(2)}) copy-start(bf16[64]{0:T(256)(128)(2,1)} %param.20) | copy-start | bytes 388
  1268.4 46.9 %collective-permute-start.1 = (bf16[64,2048]{1,0:T(8,128)(2,1)}, bf16[64,2048]{1,0:T(8,128)(2,1)}, u32[]{:S(2)}, u32[]{:S(2)}) collective-permute-start(bf16[64,2048]{1,0:T(8,128)(2,1)} %reduce-scatter.23.cloned.1.call-done), channel_id=1, source_target_pairs={{0,0},{2,1},{4,2},{6,3},{1,4},{3,5},{5,6},{7,7},{8,8},{10,9},{12,1... | collective-permute-start | bytes 786440 | tf_op jit(solution)/shard_map/ppermute | solution.py:190
  1308.5 11.0 all-to-all-start.3
  1320.4 138.5 %copy-start.3 = (f32[2,128,2048]{2,1,0:T(8,128)S(1)}, f32[2,128,2048]{2,1,0:T(8,128)}, u32[]{:S(2)}) copy-start(f32[2,128,2048]{2,1,0:T(8,128)} %copy-done.2) | copy-start | bytes 6291460
  1320.4 138.5 %copy-start.30 = (f32[2048]{0:T(1024)S(1)}, f32[2048]{0:T(1024)}, u32[]{:S(2)}) copy-start(f32[2048]{0:T(1024)} %copy-done.29) | copy-start | bytes 24580
  1321.5 142.5 %copy-start.26 = (f32[64,512]{1,0:T(8,128)}, f32[64,512]{1,0:T(8,128)S(1)}, u32[]{:S(2)}) copy-start(f32[64,512]{1,0:T(8,128)S(1)} %reshape.483) | copy-start | bytes 393220
  (5 other events, 5.4 us)
Sparse Core Ops, SparseCore 0:
  25.4 46.1 all-gather.27
  73.5 53.1 all-gather.13
  149.9 50.5 all-gather.15
  202.5 27.0 all-gather.17
  257.6 81.7 reduce-scatter.10
  340.8 80.7 all-gather.29
  423.3 79.2 all-gather.31
  504.2 79.2 all-gather.21
  586.2 52.9 all-gather.23
  641.6 54.3 all-gather.19
  764.7 71.3 reduce-scatter.14
  841.7 54.3 all-gather.25
  956.7 43.8 reduce-scatter.16
  1002.9 76.1 reduce-scatter.26
  1081.2 77.2 reduce-scatter.24
  1160.7 77.2 reduce-scatter.28
  1240.7 27.6 reduce-scatter.22
  1270.7 37.7 reduce-scatter.20
  1312.3 71.9 reduce-scatter.18
  1387.6 71.2 reduce-scatter.12

commit v2 on v1

--- a/solution.py
+++ b/solution.py
@@ -1,6 +1,10 @@
+import functools
+
 import jax
 import jax.numpy as jnp
 from jax import lax
+from jax.experimental import pallas as pl
+from jax.experimental.pallas import tpu as pltpu
 from jax.sharding import Mesh
 from jax.sharding import PartitionSpec as P
 
@@ -14,6 +18,335 @@
 GROUP = ("a", "core", "cl")
 
 
+TILE = 32
+MESH = pl.DeviceIdType.MESH
+
+def places():
+    a, core, cl = (lax.axis_index(n) for n in ("a", "core", "cl"))
+    return a, core, cl
+
+def index_of(a, core, cl):
+    return (a * 2 + core) * 2 + cl
+
+def meet(names):
+    barrier = pltpu.get_barrier_semaphore()
+    for name in names:
+        pl.semaphore_signal(barrier, inc=1, device_id={name: 1 - lax.axis_index(name)}, device_id_type=MESH)
+    pl.semaphore_wait(barrier, len(names))
+
+def remote(src, dst, send, recv, name):
+    return pltpu.make_async_remote_copy(
+        src_ref=src, dst_ref=dst, send_sem=send, recv_sem=recv,
+        device_id={name: 1 - lax.axis_index(name)}, device_id_type=MESH)
+
+def gather_kernel(x_ref, *refs):
+    o_ref, local, ss, rs = refs[-4:]
+    a, core, cl = places()
+    half = x_ref.shape[0] // 2
+    lo, hi = pl.ds(0, half), pl.ds(half, half)
+    me = index_of(a, core, cl)
+    sx = index_of(1 - a, core, cl)
+    sy = index_of(a, core, 1 - cl)
+    sd = index_of(1 - a, core, 1 - cl)
+    meet(("a", "core", "cl"))
+    mine = pltpu.make_async_copy(x_ref, o_ref.at[me], local)
+    def put(i, slot, part, name, src=None):
+        src = o_ref.at[slot, part] if src is None else src
+        return remote(src, o_ref.at[slot, part], ss.at[i], rs.at[i], name)
+    x0 = put(0, me, lo, "a", x_ref.at[lo])
+    y0 = put(1, me, hi, "cl", x_ref.at[hi])
+    x1 = put(2, me, hi, "a", x_ref.at[hi])
+    y1 = put(3, me, lo, "cl", x_ref.at[lo])
+    c0 = put(4, me, pl.ds(0, 2 * half), "core", x_ref)
+    for c in (x0, y0, x1, y1, c0, mine):
+        c.start()
+    def got(i, slot, part, name):
+        return put(i, slot, part, name)
+    fx0 = got(0, sx, lo, "a")
+    fx0.wait_recv()
+    y2 = put(5, sx, lo, "cl")
+    y2.start()
+    k0 = put(6, sx, lo, "core")
+    k0.start()
+    fy0 = got(1, sy, hi, "cl")
+    fy0.wait_recv()
+    x2 = put(7, sy, hi, "a")
+    x2.start()
+    k1 = put(8, sy, hi, "core")
+    k1.start()
+    got(2, sx, hi, "a").wait_recv()
+    k2 = put(9, sx, hi, "core")
+    k2.start()
+    got(3, sy, lo, "cl").wait_recv()
+    k3 = put(10, sy, lo, "core")
+    k3.start()
+    got(5, sd, lo, "cl").wait_recv()
+    k4 = put(11, sd, lo, "core")
+    k4.start()
+    got(7, sd, hi, "a").wait_recv()
+    k5 = put(12, sd, hi, "core")
+    k5.start()
+    def other(slot):
+        return slot + 2 - 4 * core
+    got(4, other(me), pl.ds(0, 2 * half), "core").wait_recv()
+    for i, slot, part in ((6, sx, lo), (8, sy, hi), (9, sx, hi), (10, sy, lo), (11, sd, lo), (12, sd, hi)):
+        got(i, other(slot), part, "core").wait_recv()
+    for c in (x0, y0, x1, y1, c0, y2, k0, x2, k1, k2, k3, k4, k5):
+        c.wait_send()
+    mine.wait()
+
+def plane_gather(x, cid, deps=()):
+    rows, cols = x.shape
+    out = pl.pallas_call(
+        gather_kernel,
+        out_shape=jax.ShapeDtypeStruct((8, rows, cols), x.dtype),
+        in_specs=[pl.BlockSpec(memory_space=pl.ANY)] * (1 + len(deps)),
+        out_specs=pl.BlockSpec(memory_space=pl.ANY),
+        scratch_shapes=[pltpu.SemaphoreType.DMA, pltpu.SemaphoreType.DMA((13,)), pltpu.SemaphoreType.DMA((13,))],
+        compiler_params=pltpu.CompilerParams(collective_id=cid, has_side_effects=True),
+        name=f"gather{cid}",
+    )(x, *deps)
+    return out.reshape(8 * rows, cols)
+
+
+def sum_kernel(x_ref, *refs):
+    o_ref, mine, theirs, first, last, osem, lsem, cs, cr, ss, rs = refs[-11:]
+    a, core, cl = places()
+    rows = x_ref.shape[1]
+    half = rows // 2
+    lo, hi = pl.ds(0, half), pl.ds(half, half)
+    chips = ((a, cl), (1 - a, cl), (a, 1 - cl), (1 - a, 1 - cl))
+    meet(("a", "core", "cl"))
+    order = (3, 1, 2, 0)
+    out, loc = {}, {}
+    for p in order:
+        ca, cc = chips[p]
+        out[p] = remote(x_ref.at[index_of(ca, 1 - core, cc)], theirs.at[p], cs.at[p], cr.at[p], "core")
+        out[p].start()
+        loc[p] = pltpu.make_async_copy(x_ref.at[index_of(ca, core, cc)], mine.at[p], lsem.at[p])
+        loc[p].start()
+
+    def add(dst, src_list, n):
+        @pl.loop(0, n // TILE)
+        def _(i):
+            part = pl.ds(pl.multiple_of(i * TILE, TILE), TILE)
+            total = src_list[0][part, :].astype(F32)
+            for s in src_list[1:]:
+                total = total + s[part, :].astype(F32)
+            dst[part, :] = total.astype(dst.dtype)
+
+    def chip_sum(p):
+        out[p].wait_recv()
+        loc[p].wait()
+        add(mine.at[p], (mine.at[p], theirs.at[p]), rows)
+
+    chip_sum(3)
+    xd = remote(mine.at[3, lo], first.at[0], ss.at[0], rs.at[0], "a")
+    yd = remote(mine.at[3, hi], first.at[1], ss.at[1], rs.at[1], "cl")
+    xd.start()
+    yd.start()
+    chip_sum(1)
+    xo = remote(mine.at[1, lo], first.at[2], ss.at[2], rs.at[2], "a")
+    xo.start()
+    chip_sum(2)
+    yo = remote(mine.at[2, hi], first.at[3], ss.at[3], rs.at[3], "cl")
+    yo.start()
+    chip_sum(0)
+    xd.wait_recv()
+    add(mine.at[2, lo], (mine.at[2, lo], first.at[0]), half)
+    y2 = remote(mine.at[2, lo], last.at[0], ss.at[4], rs.at[4], "cl")
+    y2.start()
+    yd.wait_recv()
+    add(mine.at[1, hi], (mine.at[1, hi], first.at[1]), half)
+    x2 = remote(mine.at[1, hi], last.at[1], ss.at[5], rs.at[5], "a")
+    x2.start()
+    xo.wait_recv()
+    add(mine.at[0, lo], (mine.at[0, lo], first.at[2]), half)
+    yo.wait_recv()
+    add(mine.at[0, hi], (mine.at[0, hi], first.at[3]), half)
+    y2.wait_recv()
+    add(mine.at[0, lo], (mine.at[0, lo], last.at[0]), half)
+    x2.wait_recv()
+    add(mine.at[0, hi], (mine.at[0, hi], last.at[1]), half)
+    done = pltpu.make_async_copy(mine.at[0], o_ref, osem)
+    done.start()
+    for c in (*out.values(), xd, yd, xo, yo, y2, x2):
+        c.wait_send()
+    done.wait()
+
+def plane_sum(x, cid, deps=()):
+    total, cols = x.shape
+    rows = total // 8
+    half = rows // 2
+    return pl.pallas_call(
+        sum_kernel,
+        out_shape=jax.ShapeDtypeStruct((rows, cols), x.dtype),
+        in_specs=[pl.BlockSpec(memory_space=pl.ANY)] * (1 + len(deps)),
+        out_specs=pl.BlockSpec(memory_space=pl.ANY),
+        scratch_shapes=[
+            pltpu.VMEM((4, rows, cols), x.dtype),
+            pltpu.VMEM((4, rows, cols), x.dtype),
+            pltpu.VMEM((4, half, cols), x.dtype),
+            pltpu.VMEM((2, half, cols), x.dtype),
+            pltpu.SemaphoreType.DMA,
+            pltpu.SemaphoreType.DMA((4,)),
+            pltpu.SemaphoreType.DMA((4,)),
+            pltpu.SemaphoreType.DMA((4,)),
+            pltpu.SemaphoreType.DMA((6,)),
+            pltpu.SemaphoreType.DMA((6,)),
+        ],
+        compiler_params=pltpu.CompilerParams(collective_id=cid, has_side_effects=True, vmem_limit_bytes=40 * 2**20),
+        name=f"sum{cid}",
+    )(x.reshape(8, rows, cols), *deps)
+
+
+def partners():
+    a, core, cl = places()
+    out = []
+    for t in range(1, 8):
+        at = (a ^ (t >> 2), core ^ ((t >> 1) & 1), cl ^ (t & 1))
+        out.append((dict(zip(GROUP, at)), index_of(*at)))
+    return out
+
+
+def columns(ref, i, width):
+    return ref.at[:, pl.ds(pl.multiple_of(i * width, width), width)]
+
+
+def moved_to(c, nz):
+    return lax.rem(c, nz), c // nz
+
+
+def moved_from(c, nz):
+    block = lax.rem(c, 2) * nz + c // 2
+    return block // 2, lax.rem(block, 2)
+
+
+def swap_kernel(kinds, nz, *refs):
+    n = len(kinds)
+    ins, outs, (lsem, ss, rs) = refs[:n], refs[-3 - n : -3], refs[-3:]
+    me = index_of(*places())
+    others = partners()
+    moving = [k for k, (kind, _) in enumerate(kinds) if kind in ("move", "home")]
+    barrier = pltpu.get_barrier_semaphore()
+    for device, _ in others:
+        pl.semaphore_signal(barrier, inc=1, device_id=device, device_id_type=MESH)
+    if moving:
+        here = lax.axis_index("cm") * 2 + lax.axis_index("cl")
+        pair = [dict(zip(("cm", "cl"), f(here, nz))) for f in (moved_to, moved_from)]
+        if kinds[moving[0]][0] == "home":
+            pair.reverse()
+        stays = pair[0]["cm"] * 2 + pair[0]["cl"] == here
+
+        @pl.when(jnp.logical_not(stays))
+        def _():
+            for device in pair:
+                pl.semaphore_signal(barrier, inc=1, device_id=device, device_id_type=MESH)
+            pl.semaphore_wait(barrier, len(others) + 2)
+
+        @pl.when(stays)
+        def _():
+            pl.semaphore_wait(barrier, len(others))
+
+    else:
+        pl.semaphore_wait(barrier, len(others))
+    copies = []
+    for k, (kind, pieces) in enumerate(kinds):
+        if kind in ("move", "home"):
+            mine = pltpu.make_async_copy(ins[k], outs[k], lsem.at[k, 0])
+            away = pltpu.make_async_remote_copy(
+                src_ref=ins[k],
+                dst_ref=outs[k],
+                send_sem=ss.at[k, 0, 0],
+                recv_sem=rs.at[k, 0, 0],
+                device_id=pair[0],
+                device_id_type=MESH,
+            )
+            pl.when(stays)(mine.start)
+            pl.when(jnp.logical_not(stays))(away.start)
+            continue
+        for p in range(pieces):
+
+            def block(f, k=k, kind=kind, pieces=pieces, p=p):
+                i = ((f // 2) * pieces + p) * 2 + lax.rem(f, 2) if pieces > 1 else f
+                return i
+
+            width = (outs[k] if kind == "cols" else ins[k]).shape[-1] // pieces
+
+            def part(ref, i, p=p, width=width, pieces=pieces):
+                return ref.at[i] if pieces == 1 else ref.at[i, :, pl.ds(p * width, width)]
+
+            def source(f):
+                return columns(ins[k], block(f), width) if kind == "cols" else part(ins[k], f)
+
+            target = columns(outs[k], block(me), width) if kind == "back" else part(outs[k], me)
+            for t, (device, index) in enumerate(others):
+                copy = pltpu.make_async_remote_copy(
+                    src_ref=source(index),
+                    dst_ref=target,
+                    send_sem=ss.at[k, p, t],
+                    recv_sem=rs.at[k, p, t],
+                    device_id=device,
+                    device_id_type=MESH,
+                )
+                copy.start()
+                copies.append(copy)
+            mine = pltpu.make_async_copy(source(me), target, lsem.at[k, p])
+            mine.start()
+            copies.append(mine)
+    for copy in copies:
+        copy.wait()
+    for k in moving:
+        mine = pltpu.make_async_copy(ins[k], outs[k], lsem.at[k, 0])
+        away = pltpu.make_async_remote_copy(
+            src_ref=ins[k],
+            dst_ref=outs[k],
+            send_sem=ss.at[k, 0, 0],
+            recv_sem=rs.at[k, 0, 0],
+            device_id=pair[0],
+            device_id_type=MESH,
+        )
+        pl.when(stays)(mine.wait)
+        pl.when(jnp.logical_not(stays))(away.wait)
+
+
+def after(x, deps):
+    return pl.pallas_call(
+        lambda *refs: None,
+        out_shape=jax.ShapeDtypeStruct(x.shape, x.dtype),
+        in_specs=[pl.BlockSpec(memory_space=pl.ANY)] * (1 + len(deps)),
+        out_specs=pl.BlockSpec(memory_space=pl.ANY),
+        input_output_aliases={0: 0},
+    )(x, *deps)
+
+
+def plane_swap(kinds, arrays, cid, deps=()):
+    shapes = []
+    most = max(pieces for _, pieces in kinds)
+    for (kind, _), x in zip(kinds, arrays):
+        if kind == "cols":
+            shape = (8, x.shape[0], x.shape[1] // 8)
+        elif kind == "back":
+            shape = (x.shape[1], 8 * x.shape[2])
+        else:
+            shape = x.shape
+        shapes.append(jax.ShapeDtypeStruct(shape, x.dtype))
+    n = len(kinds)
+    return pl.pallas_call(
+        functools.partial(swap_kernel, kinds, lax.axis_size("cm")),
+        out_shape=shapes,
+        in_specs=[pl.BlockSpec(memory_space=pl.ANY)] * (n + len(deps)),
+        out_specs=[pl.BlockSpec(memory_space=pl.ANY)] * n,
+        scratch_shapes=[
+            pltpu.SemaphoreType.DMA((n, most)),
+            pltpu.SemaphoreType.DMA((n, most, 7)),
+            pltpu.SemaphoreType.DMA((n, most, 7)),
+        ],
+        compiler_params=pltpu.CompilerParams(collective_id=cid, has_side_effects=True),
+        name=f"swap{cid}",
+    )(*arrays, *deps)
+
+
 def rope_tables(positions, head_width):
     half_width = head_width // 2
     frequency = 500000.0 ** (-jnp.arange(half_width, dtype=F32) * 2.0 / head_width)
@@ -51,18 +384,6 @@
     return jnp.einsum("re,de->rd", a, b, preferred_element_type=F32)
 
 
-def gather_group(x):
-    return lax.all_gather(x, GROUP, axis=0, tiled=True)
-
-
-def sum_group(x):
-    return lax.psum_scatter(x.astype(BF), GROUP, scatter_dimension=0, tiled=True).astype(F32)
-
-
-def swap_group(x):
-    return lax.all_to_all(x, GROUP, 0, 0, tiled=True)
-
-
 def rows_of(x):
     nz = lax.axis_size("cm")
     x = lax.all_gather(x, "cm", axis=0)
@@ -70,13 +391,15 @@
     return x.reshape(nz, 4, 2, r, c).transpose(1, 0, 2, 3, 4).reshape(nz * 8 * r, c)
 
 
-def rows_to(g):
+def sum_planes(g):
+    return lax.psum_scatter(g, "cm", scatter_dimension=0, tiled=True)
+
+
+def rows_first(g):
     nz = lax.axis_size("cm")
     rows, c = g.shape
     r = rows // (8 * nz)
-    g = g.astype(BF).reshape(4, nz, 2, r, c).transpose(1, 0, 2, 3, 4).reshape(nz * 8, r, c)
-    g = lax.psum_scatter(g, "cm", scatter_dimension=0, tiled=True)
-    return swap_group(g)
+    return g.astype(BF).reshape(4, nz, 2, r, c).transpose(1, 0, 2, 3, 4).reshape(nz * 8, r, c)
 
 
 def on_device(
@@ -86,7 +409,6 @@
     nz = lax.axis_size("cm")
     rows = seqs * block
     r = w_query.shape[0]
-    fb = w_down.shape[0]
     nseq = 4 * seqs
     slots = 2 * block
     length = slots * nz
@@ -106,25 +428,22 @@
         ],
         -1,
     ).transpose(1, 0, 2)
-    pack = rows_of(swap_group(pack))
+    (pack,) = plane_swap((("slab", 1),), (pack,), 9)
+    pack = rows_of(pack)
     wqkv = pack[:, : qh * HD + 2 * HD]
     gain_one = pack[:, qh * HD + 2 * HD].astype(F32)
     gain_two = pack[:, qh * HD + 2 * HD + 1].astype(F32)
+    pieces = nz if w_down.shape[0] % 128 == 0 else 1
     perm = [(c, (c % nz) * 2 + c // nz) for c in range(2 * nz)]
-    wo = lax.all_gather(lax.ppermute(w_out, ("cm", "cl"), perm), "cm", axis=0, tiled=True)
-
-    def ff_cols(w):
-        w = w.reshape(r, 4, nz, 2, fb).transpose(1, 3, 0, 2, 4).reshape(8, r, nz * fb)
-        return rows_of(swap_group(w))
-
-    wg = ff_cols(w_gate)
-    wu = ff_cols(w_up)
-    wd = lax.all_gather(w_down, "cm", axis=0, tiled=True)
+    home = [(t, s) for s, t in perm]
+    wd_home = w_down if pieces > 1 else lax.ppermute(w_down, ("cm", "cl"), perm)
+    wg, wo_home = plane_swap((("cols", pieces), ("move", 1)), (w_gate, w_out), 10)
+    wg = rows_of(wg)
     lens = lax.all_gather(lengths, ("a", "core"), axis=0, tiled=True)
 
     own = tokens.reshape(rows, width)
     resid_in = own.astype(F32)
-    tok_all = gather_group(own)
+    tok_all = plane_gather(own, 1)
     tok_f = tok_all.astype(F32)
     hidden_one = (tok_f * rms_scale(tok_f) * gain_one).astype(BF)
 
@@ -145,6 +464,10 @@
     v = qkv[..., qh * HD + HD :].astype(BF)
     kv = lax.all_gather(jnp.concatenate([k, v], -1), "cm", axis=1, tiled=True)
     keys, values = kv[..., :HD], kv[..., HD:]
+    (wu,) = plane_swap((("cols", pieces),), (w_up,), 13, (k, v))
+    wo = lax.all_gather(wo_home, "cm", axis=0, tiled=True)
+    wu = rows_of(wu)
+    wd = lax.all_gather(wd_home, "cm", axis=0, tiled=True)
     key_pos = jnp.arange(length, dtype=jnp.int32)
     allowed = (key_pos[None, None, :] <= pos[None, :, None]) & (key_pos[None, None, :] < lens[:, None, None])
     scores = jnp.einsum("shqd,snd->shqn", q, keys, preferred_element_type=F32) * scale
@@ -156,38 +479,41 @@
     attended = jnp.einsum("shqn,snd->shqd", probs, values, preferred_element_type=F32)
     attended_low = by_row(attended.astype(BF).transpose(0, 2, 1, 3).reshape(nseq, slots, qh * HD))
 
-    resid_mid = resid_in + sum_group(mm(attended_low, wo))
+    resid_mid = resid_in + plane_sum(mm(attended_low, wo).astype(BF), 5).astype(F32)
     scale_two = rms_scale(resid_mid)
     normed_two = resid_mid * scale_two
-    hidden_two = gather_group((normed_two * gain_two).astype(BF))
+    hidden_two = plane_gather((normed_two * gain_two).astype(BF), 2)
     gate_pre = mm(hidden_two, wg)
     up_pre = mm(hidden_two, wu)
     sig = jax.nn.sigmoid(gate_pre)
     act = gate_pre * sig
     inner = (act * up_pre).astype(BF)
-    layer_out = (resid_mid + sum_group(mm(inner, wd))).astype(BF)
+    layer_out = (resid_mid + plane_sum(mm(inner, wd).astype(BF), 6).astype(F32)).astype(BF)
 
     own_pos = cm * slots + cl * block + jnp.arange(block, dtype=jnp.int32)
     valid = (own_pos[None, :] < lengths[:, None]).astype(F32)
     grad_out = (cotangent.astype(F32) * valid[..., None]).reshape(rows, width)
-    grad_low = gather_group(grad_out.astype(BF))
-    grad_wd = lax.psum_scatter(mm_tn(inner, grad_low).astype(BF), "cm", scatter_dimension=0, tiled=True)
+    grad_low = plane_gather(grad_out.astype(BF), 3, (k, v))
+    grad_wd = mm_tn(inner, grad_low).astype(BF)
     grad_inner = mm_nt(grad_low, wd).astype(BF).astype(F32)
     grad_gate = (grad_inner * up_pre * (sig * (1.0 + gate_pre * (1.0 - sig)))).astype(BF)
     grad_up = (grad_inner * act).astype(BF)
 
-    def ff_back(g):
-        g = rows_to(g)
-        return g.reshape(4, 2, r, nz, fb).transpose(2, 0, 3, 1, 4).reshape(r, 8 * nz * fb).astype(F32)
-
-    grad_wg = ff_back(mm_tn(hidden_two, grad_gate))
-    grad_wu = ff_back(mm_tn(hidden_two, grad_up))
-    grad_hidden_two = sum_group(mm_nt(grad_gate, wg) + mm_nt(grad_up, wu))
+    grad_wg = rows_first(mm_tn(hidden_two, grad_gate))
+    grad_wu = rows_first(mm_tn(hidden_two, grad_up))
+    grad_hidden_two = plane_sum(
+        (mm_nt(grad_gate, wg) + mm_nt(grad_up, wu)).astype(BF), 7, (grad_wd, grad_wg, grad_wu)
+    ).astype(F32)
+    grad_wd, grad_wu, grad_wg = sum_planes(grad_wd), sum_planes(grad_wu), sum_planes(grad_wg)
+    ff_sums = (grad_wd, grad_wu, grad_wg)
+    if pieces == 1:
+        grad_wd = lax.ppermute(grad_wd, ("cm", "cl"), home)
+    grad_wg, grad_wu = plane_swap((("back", pieces),) * 2, (grad_wg, grad_wu), 11)
+    grad_wg, grad_wu = grad_wg.astype(F32), grad_wu.astype(F32)
     gain_grad_two = jnp.sum(grad_wg * w_gate.astype(F32) + grad_wu * w_up.astype(F32), -1) / mlp_gain.astype(F32)
     grad_mid = grad_out + norm_back(grad_hidden_two * gain_two, normed_two, scale_two)
-    grad_attn = gather_group(grad_mid.astype(BF))
-    grad_wo = lax.psum_scatter(mm_tn(attended_low, grad_attn).astype(BF), "cm", scatter_dimension=0, tiled=True)
-    grad_wo = lax.ppermute(grad_wo, ("cm", "cl"), [(t, s) for s, t in perm]).astype(F32)
+    grad_attn = plane_gather(grad_mid.astype(BF), 4)
+    grad_wo = mm_tn(attended_low, grad_attn).astype(BF)
     grad_heads = by_seq(mm_nt(grad_attn, wo).astype(BF)).reshape(nseq, slots, qh, HD).transpose(0, 2, 1, 3)
     delta = jnp.sum(grad_heads.astype(F32) * attended, -1, keepdims=True)
     grad_soft = jnp.einsum("shqd,snd->shqn", grad_heads, values, preferred_element_type=F32)
@@ -196,7 +522,9 @@
     grad_k = jnp.einsum("shqn,shqd->snd", grad_scores, q, preferred_element_type=F32)
     grad_v = jnp.einsum("shqn,shqd->snd", probs, grad_heads, preferred_element_type=F32)
     grad_kv = jnp.concatenate([grad_k, grad_v], -1).astype(BF)
-    grad_kv = lax.psum_scatter(grad_kv, "cm", scatter_dimension=1, tiled=True).astype(F32)
+    grad_kv = lax.psum_scatter(after(grad_kv, ff_sums), "cm", scatter_dimension=1, tiled=True)
+    grad_wo = sum_planes(after(grad_wo, (grad_kv,)))
+    grad_kv = grad_kv.astype(F32)
     grad_rows = by_row(
         jnp.concatenate(
             [
@@ -207,7 +535,8 @@
             -1,
         )
     )
-    back = rows_to(mm_tn(hidden_one, grad_rows))
+    back = sum_planes(rows_first(mm_tn(hidden_one, grad_rows)))
+    back, grad_wo = plane_swap((("slab", 1), ("home", 1)), (back, grad_wo), 12)
     back = back.transpose(1, 0, 2).astype(F32)
     grad_wq = back[..., : qh * HD].reshape(r, HEADS * HD)
     grad_wk = back[..., qh * HD : qh * HD + HD].reshape(r, KVH * HD)
@@ -217,7 +546,7 @@
         + jnp.sum(grad_wk * w_key.astype(F32), -1)
         + jnp.sum(grad_wv * w_value.astype(F32), -1)
     ) / attn_gain.astype(F32)
-    grad_hidden_one = sum_group(mm_nt(grad_rows, wqkv))
+    grad_hidden_one = plane_sum(mm_nt(grad_rows, wqkv).astype(BF), 8).astype(F32)
     scale_one = rms_scale(resid_in)
     grad_tokens = grad_mid + norm_back(grad_hidden_one * gain_one, resid_in * scale_one, scale_one)
     return (
@@ -227,7 +556,7 @@
         grad_wq,
         grad_wk,
         grad_wv,
-        grad_wo,
+        grad_wo.astype(F32),
         gain_grad_two,
         grad_wg,
         grad_wu,

time: 1480 us -> 882 us (0.60)
  waiting for transfers between devices: 962 us -> 42.5 us
  Pallas kernels: 0 us -> 410 us
  blocking collectives: 66.9 us -> 15.9 us
  local copies, waits for them, and re-layouts: 74.4 us -> 53.9 us
  starting transfers between devices: 18 us -> 1.28 us
    reduce_scatter x10 -> x6, waiting for transfers between devices: 438 us -> 25.5 us  [the longest x1 25.4 us: on_device(): lax.psum_scatter(after(grad_kv, ff_sums), 'cm', scatter_dimension=1, tile...]
    pallas_call x0 -> x15, Pallas kernels: none -> 410 us  [the longest x4 162 us: plane_sum(): pl.pallas_call(sum_kernel, out_shape=jax.ShapeDtypeStruct((rows, cols), x...]
    all_gather x6 -> x2, waiting for transfers between devices: 282 us -> 0.02 us  [the longest x1 0.02 us: on_device(): wo = lax.all_gather(wo_home, 'cm', axis=0, tiled=True)]
    all_gather x3, waiting for transfers between devices: 199 us -> 11.7 us  [rows_of(): x = lax.all_gather(x, 'cm', axis=0)]
    all_to_all x3 -> x0, blocking collectives: 62 us -> none  [swap_group(): return lax.all_to_all(x, GROUP, 0, 0, tiled=True)]
    all_gather x1, waiting for transfers between devices: 38.8 us -> 4.11 us  [on_device(): kv = lax.all_gather(jnp.concatenate([k, v], -1), 'cm', axis=1, tiled=True)]
    convert_element_type x6 -> x0, local copies, waits for them, and re-layouts: 19.7 us -> none  [ff_back(): g.reshape(4, 2, r, nz, fb).transpose(2, 0, 3, 1, 4).reshape(r, 8 * nz * fb)]
  transfers between devices with their start and end apart: 25 -> 12, of which waited for: 19 -> 3; matrix products, arithmetic and copies ran while one was open for 16% -> 42% of each run, Pallas kernels for 0% -> 44%
where the time goes in v2:
time: 882 us; the launch traced here: 873 us
  Pallas kernels  410 us (46%)
  matrix products  264 us (30%)
  other arithmetic  68.7 us (8%)
  local copies, waits for them, and re-layouts  53.9 us (6%)
  waiting for transfers between devices  42.5 us (5%)
  between operations  16.3 us (2%)
  blocking collectives  15.9 us (2%)
    pallas_call x4, Pallas kernels, plane_sum(): pl.pallas_call(sum_kernel, out_shape=jax.ShapeDtypeStruct((rows, cols), x...  162 us
    pallas_call x4, Pallas kernels, plane_gather(): pl.pallas_call(gather_kernel, out_shape=jax.ShapeDtypeStruct((8, rows, co...  161 us
    pallas_call x5, Pallas kernels, plane_swap(): pl.pallas_call(functools.partial(swap_kernel, kinds, lax.axis_size('cm'))...  87.7 us
    dot_general x5, matrix products, mm_nt(): return jnp.einsum('re,de->rd', a, b, preferred_element_type=F32)  61.9 us
    dot_general x5, matrix products, mm(): return jnp.dot(a, b, preferred_element_type=F32)  60.3 us
    dot_general x5, matrix products, mm_tn(): return jnp.einsum('rd,re->de', a, b, preferred_element_type=F32)  50.8 us
    reduce_scatter x1, waiting for transfers between devices, on_device(): lax.psum_scatter(after(grad_kv, ff_sums), 'cm', scatter_dimension=1, tile...  25.4 us
    dot_general x1, matrix products, on_device(): jnp.einsum('shqd,snd->shqn', grad_heads, values, preferred_element_type=F32)  24.8 us
  transfers between devices with their start and end apart: 12, of which 3 were waited for; matrix products, arithmetic and copies ran while one was open for 42% of the time, Pallas kernels for 44%

profile of v2, /device:TPU:0, one launch (start us, length us, event | category | flops | bytes accessed | tf_op | source)
XLA Modules:
  0.0 873.2 jit_solution(15884552047083182895)
XLA Ops:
  12.0 11.0 %swap9.1 = bf16[8,64,512]{2,1,0:T(8,128)(2,1)} custom-call(bf16[8,64,512]{2,1,0:T(8,128)(2,1)} %maximum_bitcast_fusion.refs_0_), custom_call_target="tpu_custom_call" | custom-call | tf_op jit(solution)/shard_map/swap9/pallas_call | solution.py:335
  23.1 21.2 %swap10.1 = (bf16[8,64,1024]{2,1,0:T(8,128)(2,1)}, bf16[64,2048]{1,0:T(8,128)(2,1)}) custom-call(bf16[64,8192]{1,0:T(8,128)(2,1)} %refs_0_.2, bf16[64,2048]{1,0:T(8,128)(2,1)} %refs_1_.1), custom_call_target="tpu_custom_call" | custom-call | tf_op jit(solution)/shard_map/swap10/pallas_call | solution.py:335
  45.5 40.7 %gather1.1 = bf16[8,256,2048]{2,1,0:T(8,128)(2,1)} custom-call(bf16[256,2048]{1,0:T(8,128)(2,1)} %bitcast.168), custom_call_target="tpu_custom_call" | custom-call | tf_op jit(solution)/shard_map/gather1/pallas_call | solution.py:100
  86.2 5.1 multiply_reduce_fusion
  91.4 1.8 copy.160
  93.8 7.2 fusion.16
  107.0 15.9 %all-reduce.1 = s32[8]{0:T(128)S(1)} all-reduce(s32[8]{0:T(128)S(1)} %dynamic-update-slice), channel_id=1, replica_groups=mesh['a'=2,'core'=2,'cm'=4,'cl'=2] {'a','core'}, use_global_device_ids=true, to_apply=%add.1 | all-reduce | flops 8 | bytes 64
  123.2 2.3 broadcast_and_fusion
  129.3 1.5 slice.86
  130.8 2.0 copy.162
  134.0 15.5 %swap13.1 = bf16[8,64,1024]{2,1,0:T(8,128)(2,1)} custom-call(bf16[64,8192]{1,0:T(8,128)(2,1)} %refs_0_.3, bf16[8,256,64]{2,1,0:T(8,128)(2,1)} %pad_maximum_fusion.7.refs_1_.refs_0_, bf16[8,256,64]{2,1,0:T(8,128)(2,1)} %copy-done.16), custom_call_target="tpu_custom_call" | custom-call | tf_op jit(solution)/shard_map/swap13/pallas_call | solution.py:335
  149.5 40.1 %gather3.1 = bf16[8,256,2048]{2,1,0:T(8,128)(2,1)} custom-call(bf16[256,2048]{1,0:T(8,128)(2,1)} %bitcast_convert_fusion.2.x_ref, bf16[8,256,64]{2,1,0:T(8,128)(2,1)} %pad_maximum_fusion.7.refs_1_.refs_0_, bf16[8,256,64]{2,1,0:T(8,128)(2,1)} %copy-done.16), custom_call_target="tpu_custom_call" | custom-call | tf_op jit(solution)/shard_map/gather3/pallas_call | solution.py:100
  190.2 5.3 copy.168
  195.5 4.1 all-gather.10.cloned.1.call-done
  199.6 16.2 %fusion.1 = (f32[8,4,256]{2,1,0:T(4,128)S(1)}, f32[8,4,256,1024]{3,2,1,0:T(8,128)}) fusion(pred[8,256,1024]{2,1,0:T(8,128)(4,1)S(1)} %copy-done.13, bf16[8,1024,128]{2,1,0:T(8,128)(2,1)} %all-gather.10.cloned.1.call-done, bf16[8,4,256,32]{2,3,1,0:T(8,128)(2,1)S(1)} %get-tuple-element.35, bf16[8,4,256,32]{2,3,1,0:T(8,128)(2,1)S(1)} %get-tuple-element.34), kind=kOutput, calls=%fused_computation.5 | convolution fusion | flops 1100996608 | bytes 38830080 | tf_op jit(solution)/shard_map/shqd,snd->shqn/dot_general | solution.py:473
  215.8 15.4 %exponential_reduce_fusion = f32[8,4,256]{2,1,0:T(4,128)S(1)} fusion(f32[8,4,256,1024]{3,2,1,0:T(8,128)} %get-tuple-element.46, f32[8,4,256]{2,1,0:T(4,128)S(1)} %get-tuple-element.45, pred[8,256,1024]{2,1,0:T(8,128)(4,1)S(1)} %copy-done.13), kind=kLoop, calls=%fused_computation.2 | loop fusion | flops 33546240 | bytes 35717120 | tf_op jit(solution)/shard_map/reduce_sum | solution.py:476
  231.2 14.3 %fusion.20 = f32[8,4,256,64]{2,3,1,0:T(8,128)S(1)} fusion(bf16[8,1024,128]{2,1,0:T(8,128)(2,1)S(1)} %copy-done.27, f32[8,4,256,1024]{3,2,1,0:T(8,128)} %get-tuple-element.46, f32[8,4,256]{2,1,0:T(4,128)S(1)} %bitcast.215, pred[8,256,1024]{2,1,0:T(8,128)(4,1)S(1)} %copy-done.13), kind=kOutput, calls=%fused_computation.62 | convolution fusion | flops 1107296256 | bytes 39878656 | tf_op jit(solution)/shard_map/shqn,snd->shqd/dot_general | solution.py:479
  248.2 3.9 convolution_convert_fusion.2
  252.2 40.4 %sum5.1 = bf16[256,2048]{1,0:T(8,128)(2,1)S(1)} custom-call(bf16[8,256,2048]{2,1,0:T(8,128)(2,1)S(1)} %bitcast.160), custom_call_target="tpu_custom_call" | custom-call | tf_op jit(solution)/shard_map/sum5/pallas_call | solution.py:181
  293.6 1.6 multiply_convert_fusion.5.x_ref
  295.2 40.0 %gather2.1 = bf16[8,256,2048]{2,1,0:T(8,128)(2,1)} custom-call(bf16[256,2048]{1,0:T(8,128)(2,1)} %multiply_convert_fusion.5.x_ref), custom_call_target="tpu_custom_call" | custom-call | tf_op jit(solution)/shard_map/gather2/pallas_call | solution.py:100
  335.2 14.9 %fusion.37 = f32[2048,1024]{1,0:T(8,128)} fusion(bf16[2048,2048]{1,0:T(8,128)(2,1)} %bitcast.179, bf16[2048,1024]{1,0:T(8,128)(2,1)} %bitcast.193), kind=kOutput, calls=%fused_computation.116 | convolution fusion | flops 8589934592 | bytes 20971520 | tf_op jit(solution)/shard_map/dot_general | solution.py:376
  350.2 14.1 %convolution_convert_fusion.4 = bf16[2048,1024]{1,0:T(8,128)(2,1)} fusion(bf16[2048,2048]{1,0:T(8,128)(2,1)} %bitcast.176, bf16[1024,2048]{1,0:T(8,128)(2,1)} %all-gather.14.cloned.1.call-done), kind=kOutput, calls=%fused_computation.26 | convolution fusion | flops 8592031744 | bytes 16777216 | tf_op jit(solution)/shard_map/re,de->rd/dot_general | solution.py:384
  364.2 11.5 %convolution_convert_fusion.5 = bf16[2048,1024]{1,0:T(8,128)(2,1)S(1)} fusion(bf16[2048,2048]{1,0:T(8,128)(2,1)S(1)} %bitcast.181, bf16[2048,1024]{1,0:T(8,128)(2,1)} %convolution_convert_fusion.4, f32[2048,1024]{1,0:T(8,128)S(1)} %copy-done.61), kind=kOutput, calls=%fused_computation.27 | convolution fusion | flops 8606711808 | bytes 25165824 | tf_op jit(solution)/shard_map/rd,re->de/dot_general | solution.py:380
  375.8 2.5 copy.171
  378.5 11.6 %all-gather.20.cloned.1.call-done = bf16[32,64,1024]{2,1,0:T(8,128)(2,1)} async-done(((bf16[8,64,1024]{2,1,0:T(8,128)(2,1)}), bf16[32,64,1024]{2,1,0:T(8,128)(2,1)}) %all-gather.20.cloned.1.call-update) | async-done | bytes 4194320 | tf_op jit(solution)/shard_map/all_gather | solution.py:389
  390.1 2.9 copy.169
  393.0 22.1 %fusion.3 = (bf16[2048,1024]{1,0:T(8,128)(2,1)}, bf16[2048,1024]{1,0:T(8,128)(2,1)}) fusion(bf16[2048,1024]{1,0:T(8,128)(2,1)} %convolution_convert_fusion.4, f32[2048,1024]{1,0:T(8,128)} %fusion.37, bf16[2048,2048]{1,0:T(8,128)(2,1)} %bitcast.180, bf16[2048,1024]{1,0:T(8,128)(2,1)S(1)} %bitcast.196), kind=kOutput, calls=%fused_computation.13 | convolution fusion | flops 8619294720 | bytes 33554432 | tf_op jit(solution)/shard_map/dot_general | solution.py:376
  415.1 11.2 %convolution_convert_fusion.6 = bf16[2048,1024]{1,0:T(8,128)(2,1)S(1)} fusion(bf16[2048,2048]{1,0:T(8,128)(2,1)S(1)} %bitcast.184, bf16[2048,1024]{1,0:T(8,128)(2,1)} %get-tuple-element.28), kind=kOutput, calls=%fused_computation.28 | convolution fusion | flops 8592031744 | bytes 16777216 | tf_op jit(solution)/shard_map/rd,re->de/dot_general | solution.py:380
  426.3 2.4 copy.170
  429.1 15.5 %fusion.38 = f32[2048,2048]{1,0:T(8,128)} fusion(bf16[2048,1024]{1,0:T(8,128)(2,1)} %get-tuple-element.28, bf16[2048,1024]{1,0:T(8,128)(2,1)} %bitcast.194), kind=kOutput, calls=%fused_computation.117 | convolution fusion | flops 8589934592 | bytes 25165824 | tf_op jit(solution)/shard_map/re,de->rd/dot_general | solution.py:384
  444.6 12.8 %convolution_convert_fusion.3.refs_0_ = bf16[1024,2048]{1,0:T(8,128)(2,1)} fusion(bf16[2048,1024]{1,0:T(8,128)(2,1)S(1)} %copy-done.60, bf16[2048,2048]{1,0:T(8,128)(2,1)} %bitcast.177), kind=kOutput, calls=%fused_computation.25 | convolution fusion | flops 8592031744 | bytes 16777216 | tf_op jit(solution)/shard_map/rd,re->de/dot_general | solution.py:380
  457.8 20.5 %add_convert_fusion = bf16[2048,2048]{1,0:T(8,128)(2,1)} fusion(f32[2048,2048]{1,0:T(8,128)} %fusion.38, bf16[2048,1024]{1,0:T(8,128)(2,1)} %bitcast.197, bf16[2048,1024]{1,0:T(8,128)(2,1)} %convolution_convert_fusion.4, f32[2048,1024]{1,0:T(8,128)} %fusion.37), kind=kOutput, calls=%fused_computation.7 | convolution fusion | flops 8613003264 | bytes 41943040 | tf_op jit(solution)/shard_map/re,de->rd/dot_general | solution.py:384
  478.3 2.2 copy-done.2
  480.5 2.2 copy-done.3
  482.7 2.2 copy-done.4
  484.9 40.9 %sum7.1 = bf16[256,2048]{1,0:T(8,128)(2,1)S(1)} custom-call(bf16[8,256,2048]{2,1,0:T(8,128)(2,1)} %bitcast.185, bf16[1024,2048]{1,0:T(8,128)(2,1)S(1)} %copy-done.4, bf16[32,64,1024]{2,1,0:T(8,128)(2,1)S(1)} %bitcast.164, bf16[32,64,1024]{2,1,0:T(8,128)(2,1)S(1)} %bitcast.162), custom_call_target="tpu_custom_call" | custom-call | tf_op jit(solution)/shard_map/sum7/pallas_call | solution.py:181
  527.4 2.1 fusion.32.x_ref
  529.5 39.9 %gather4.1 = bf16[8,256,2048]{2,1,0:T(8,128)(2,1)} custom-call(bf16[256,2048]{1,0:T(8,128)(2,1)} %fusion.32.x_ref), custom_call_target="tpu_custom_call" | custom-call | tf_op jit(solution)/shard_map/gather4/pallas_call | solution.py:100
  569.4 7.1 convolution_convert_fusion.9
  576.5 3.7 copy.172
  580.1 2.5 reshape_reshape.7
  582.7 2.2 multiply_reduce_fusion.1
  584.9 24.8 %multiply_convert_fusion = bf16[8,4,256,1024]{3,2,1,0:T(8,128)(2,1)} fusion(f32[8,4,256,1024]{3,2,1,0:T(8,128)} %get-tuple-element.46, f32[8,4,256]{2,1,0:T(4,128)S(1)} %multiply_reduce_fusion.1, f32[8,4,256]{2,1,0:T(4,128)S(1)} %bitcast.216, pred[8,256,1024]{2,1,0:T(8,128)(4,1)} %broadcast_and_fusion, ...), kind=kOutput, calls=%fused_computation | convolution fusion | flops 1132462080 | bytes 55640064 | tf_op jit(solution)/shard_map/shqd,snd->shqn/dot_general | solution.py:519
  609.7 9.9 %bitcast_convert_fusion.1 = bf16[8,1024,64]{1,2,0:T(8,128)(2,1)} fusion(bf16[8,4,256,1024]{3,2,1,0:T(8,128)(2,1)} %multiply_convert_fusion, bf16[8,4,256,32]{2,3,1,0:T(8,128)(2,1)S(1)} %copy-done.31, bf16[8,4,256,32]{2,3,1,0:T(8,128)(2,1)S(1)} %copy-done.29), kind=kOutput, calls=%fused_computation.45 | convolution fusion | flops 1076363264 | bytes 18874368 | tf_op jit(solution)/shard_map/shqn,shqd->snd/dot_general | solution.py:522
  619.6 2.7 copy.175
  622.3 16.9 %bitcast_convert_fusion = bf16[8,1024,64]{1,2,0:T(8,128)(2,1)} fusion(bf16[8,256,4,64]{1,3,2,0:T(8,128)(2,1)} %reshape_reshape.7, f32[8,4,256,1024]{3,2,1,0:T(8,128)} %get-tuple-element.46, f32[8,4,256]{2,1,0:T(4,128)S(1)} %bitcast.217, pred[8,256,1024]{2,1,0:T(8,128)(4,1)} %broadcast_and_fusion), kind=kOutput, calls=%fused_computation.44 | convolution fusion | flops 1107820544 | bytes 37781504 | tf_op jit(solution)/shard_map/shqn,shqd->snd/dot_general | solution.py:523
  639.2 3.1 copy.176
  642.3 4.7 pad_maximum_fusion.refs_0_
  648.2 8.9 %multiply_convert_fusion.1 = bf16[8,256,2048]{2,1,0:T(8,128)(2,1)} fusion(bf16[8,256,2048]{2,1,0:T(8,128)(2,1)} %gather1.1, f32[2048]{0:T(1024)S(1)} %copy-done.49, f32[8,256]{1,0:T(8,128)S(1)} %copy-done.51), kind=kLoop, calls=%fused_computation.6 | loop fusion | flops 16777216 | bytes 16793600 | tf_op jit(solution)/shard_map/convert_element_type | solution.py:448
  657.1 6.8 convolution_convert_fusion.8.refs_0_
  663.9 25.4 %reduce-scatter.13.cloned.1.call-done.refs_1_ = bf16[8,256,128]{2,1,0:T(8,128)(2,1)} async-done(((bf16[8,1024,128]{2,1,0:T(8,128)(2,1)}), bf16[8,256,128]{2,1,0:T(8,128)(2,1)}) %reduce-scatter.13.cloned.1.call-update) | async-done | bytes 524304 | tf_op jit(solution)/shard_map/reduce_scatter | solution.py:525
  689.4 9.3 %fusion.18 = f32[8,4,256,64]{2,3,1,0:T(8,128)S(1)} fusion(bf16[8,4,256,1024]{3,2,1,0:T(8,128)(2,1)} %multiply_convert_fusion, bf16[8,1024,128]{2,1,0:T(8,128)(2,1)} %all-gather.10.cloned.1.call-done), kind=kOutput, calls=%fused_computation.60 | convolution fusion | flops 1073741824 | bytes 20971520 | tf_op jit(solution)/shard_map/shqn,snd->shqd/dot_general | solution.py:521
  700.2 2.3 copy.178
  704.4 8.6 convolution_convert_fusion.7
  714.4 12.2 %convolution_convert_fusion.1 = bf16[2048,2048]{1,0:T(8,128)(2,1)S(1)} fusion(bf16[2048,1024]{1,0:T(8,128)(2,1)} %get-tuple-element.29, bf16[1024,2048]{1,0:T(8,128)(2,1)} %all-gather.14.cloned.1.call-done), kind=kOutput, calls=%fused_computation.22 | convolution fusion | flops 8594128896 | bytes 16777216 | tf_op jit(solution)/shard_map/dot_general | solution.py:376
  726.6 40.3 %sum6.1 = bf16[256,2048]{1,0:T(8,128)(2,1)S(1)} custom-call(bf16[8,256,2048]{2,1,0:T(8,128)(2,1)S(1)} %bitcast.165), custom_call_target="tpu_custom_call" | custom-call | tf_op jit(solution)/shard_map/sum6/pallas_call | solution.py:181
  766.9 1.6 convert_element_type.271
  768.5 27.3 %swap11.1 = (bf16[64,8192]{1,0:T(8,128)(2,1)}, bf16[64,8192]{1,0:T(8,128)(2,1)}) custom-call(bf16[8,64,1024]{2,1,0:T(8,128)(2,1)} %reduce-scatter.11.cloned.1.call-done.refs_3_.refs_0_, bf16[8,64,1024]{2,1,0:T(8,128)(2,1)} %reduce-scatter.9.cloned.1.call-done.refs_2_.refs_1_), custom_call_target="tpu_custom_call" | custom-call | tf_op jit(solution)/shard_map/swap11/pallas_call | solution.py:335
  795.8 5.0 add_reduce_fusion
  801.4 4.8 convolution_convert_fusion
  806.2 40.2 %sum8.1 = bf16[256,2048]{1,0:T(8,128)(2,1)S(1)} custom-call(bf16[8,256,2048]{2,1,0:T(8,128)(2,1)S(1)} %bitcast.166), custom_call_target="tpu_custom_call" | custom-call | tf_op jit(solution)/shard_map/sum8/pallas_call | solution.py:181
  846.9 3.0 fusion.15
  850.0 12.5 %swap12.1 = (bf16[8,64,384]{2,1,0:T(8,128)(2,1)}, bf16[64,2048]{1,0:T(8,128)(2,1)}) custom-call(bf16[8,64,384]{2,1,0:T(8,128)(2,1)} %reduce-scatter.15.cloned.1.call-done.refs_0_, bf16[64,2048]{1,0:T(8,128)(2,1)} %reduce-scatter.17.cloned.1.call-done.refs_1_), custom_call_target="tpu_custom_call" | custom-call | tf_op jit(solution)/shard_map/swap12/pallas_call | solution.py:335
  (229 shorter events, 34.1 us)
Async XLA Ops:
  7.2 84.2 %all-gather.16.cloned.1.call-start = ((), (), s32[]{:S(2)}) async-start(), calls=%async_computation.15 | async-start | bytes 2621440 | tf_op jit(solution)/shard_map/all_gather | solution.py:389
  23.1 167.0 %all-gather.18.cloned.1.call-start = ((), (), s32[]{:S(2)}) async-start(), calls=%async_computation.16 | async-start | bytes 5242880 | tf_op jit(solution)/shard_map/all_gather | solution.py:389
  44.4 155.1 %all-gather.10.cloned.1.call-start = ((), (), s32[]{:S(2)}) async-start(), calls=%async_computation.6 | async-start | bytes 2621440 | tf_op jit(solution)/shard_map/all_gather | solution.py:465
  45.3 144.4 %copy-start.38 = (f32[256,32]{0,1:T(8,128)}, f32[256,32]{0,1:T(8,128)S(1)}, u32[]{:S(2)}) copy-start(f32[256,32]{0,1:T(8,128)S(1)} %get-tuple-element.44) | copy-start | bytes 98308
  45.4 56.1 %copy-start.35 = (f32[256,32]{1,0:T(8,128)}, f32[256,32]{1,0:T(8,128)S(1)}, u32[]{:S(2)}) copy-start(f32[256,32]{1,0:T(8,128)S(1)} %copy.163) | copy-start | bytes 98308
  91.3 2.5 copy-start.50
  93.2 7.8 copy-start.18
  93.8 7.2 copy-start.48
  93.8 199.3 %copy-start.46 = (f32[2048]{0:T(1024)}, f32[2048]{0:T(1024)S(1)}, u32[]{:S(2)}) copy-start(f32[2048]{0:T(1024)S(1)} %get-tuple-element.23) | copy-start | bytes 24580
  101.3 4.2 copy-start.59
  101.3 5.4 copy-start.57
  104.2 144.0 %all-gather.12.cloned.1.call-start = ((), (), s32[]{:S(2)}) async-start(), calls=%async_computation.7 | async-start | bytes 1310720 | tf_op jit(solution)/shard_map/all_gather | solution.py:468
  104.8 245.4 %all-gather.14.cloned.1.call-start = ((), (), s32[]{:S(2)}) async-start(), calls=%async_computation.8 | async-start | bytes 5242880 | tf_op jit(solution)/shard_map/all_gather | solution.py:470
  105.4 284.7 %all-gather.20.cloned.1.call-start = ((), (), s32[]{:S(2)}) async-start(), calls=%async_computation.17 | async-start | bytes 5242880 | tf_op jit(solution)/shard_map/all_gather | solution.py:389
  130.8 2.0 copy-start.21
  130.8 2.0 copy-start.23
  190.0 9.5 %copy-start.28 = (bf16[8,4,256,32]{2,3,1,0:T(8,128)(2,1)}, bf16[8,4,256,32]{2,3,1,0:T(8,128)(2,1)S(1)}, u32[]{:S(2)}) copy-start(bf16[8,4,256,32]{2,3,1,0:T(8,128)(2,1)S(1)} %get-tuple-element.34) | copy-start | bytes 1572868
  190.0 9.5 %copy-start.30 = (bf16[8,4,256,32]{2,3,1,0:T(8,128)(2,1)}, bf16[8,4,256,32]{2,3,1,0:T(8,128)(2,1)S(1)}, u32[]{:S(2)}) copy-start(bf16[8,4,256,32]{2,3,1,0:T(8,128)(2,1)S(1)} %get-tuple-element.35) | copy-start | bytes 1572868
  190.1 457.0 %reduce-scatter.9.cloned.1.call-start = ((), (), s32[]{:S(2)}) async-start(), calls=%async_computation.10 | async-start | bytes 5242880 | tf_op jit(solution)/shard_map/reduce_scatter | solution.py:395
  190.1 9.4 %copy-start.13 = (pred[8,256,1024]{2,1,0:T(8,128)(4,1)S(1)}, pred[8,256,1024]{2,1,0:T(8,128)(4,1)}, u32[]{:S(2)}) copy-start(pred[8,256,1024]{2,1,0:T(8,128)(4,1)} %broadcast_and_fusion) | copy-start | bytes 6291460
  215.8 15.5 %copy-start.27 = (bf16[8,1024,128]{2,1,0:T(8,128)(2,1)S(1)}, bf16[8,1024,128]{2,1,0:T(8,128)(2,1)}, u32[]{:S(2)}) copy-start(bf16[8,1024,128]{2,1,0:T(8,128)(2,1)} %all-gather.10.cloned.1.call-done) | copy-start | bytes 6291460
  231.2 14.4 %copy-start.52 = (f32[4,8,256]{2,1,0:T(8,128)}, f32[4,8,256]{2,1,0:T(8,128)S(1)}, u32[]{:S(2)}) copy-start(f32[4,8,256]{2,1,0:T(8,128)S(1)} %log_add_fusion) | copy-start | bytes 98308
  248.2 4.0 copy-start.11
  252.2 40.5 %copy-start.5 = (bf16[2,128,2048]{2,1,0:T(8,128)(2,1)S(1)}, bf16[2,128,2048]{2,1,0:T(8,128)(2,1)}, u32[]{:S(2)}) copy-start(bf16[2,128,2048]{2,1,0:T(8,128)(2,1)} %param.12) | copy-start | bytes 3145732
  350.2 14.1 %copy-start.14 = (bf16[8,256,2048]{2,1,0:T(8,128)(2,1)S(1)}, bf16[8,256,2048]{2,1,0:T(8,128)(2,1)}, u32[]{:S(2)}) copy-start(bf16[8,256,2048]{2,1,0:T(8,128)(2,1)} %gather2.1) | copy-start | bytes 25165828
  350.2 14.1 %copy-start.61 = (f32[2048,1024]{1,0:T(8,128)S(1)}, f32[2048,1024]{1,0:T(8,128)}, u32[]{:S(2)}) copy-start(f32[2048,1024]{1,0:T(8,128)} %fusion.37) | copy-start | bytes 25165828
  378.3 268.8 %reduce-scatter.11.cloned.1.call-start = ((), (), s32[]{:S(2)}) async-start(), calls=%async_computation.11 | async-start | bytes 5242880 | tf_op jit(solution)/shard_map/reduce_scatter | solution.py:395
  390.1 25.0 %slice-start = ((s8[8388608]{0:T(1024)(128)(4,1)}), s8[4194304]{0:T(1024)(128)(4,1)S(1)}, s32[]{:S(2)}) async-start(s8[8388608]{0:T(1024)(128)(4,1)} %bitcast.182), calls=%async_computation.18 | async-start | bytes 8388608
  393.0 22.1 %copy-start.25 = (bf16[4,4,2,64,1024]{4,3,2,1,0:T(8,128)(2,1)}, bf16[4,4,2,64,1024]{4,3,2,1,0:T(8,128)(2,1)S(1)}, u32[]{:S(2)}) copy-start(bf16[4,4,2,64,1024]{4,3,2,1,0:T(8,128)(2,1)S(1)} %copy.169) | copy-start | bytes 12582916
  393.0 22.1 %slice-start.1 = ((s8[8388608]{0:T(1024)(128)(4,1)}), s8[4194304]{0:T(1024)(128)(4,1)S(1)}, s32[]{:S(2)}) async-start(s8[8388608]{0:T(1024)(128)(4,1)} %bitcast.182), calls=%async_computation.19 | async-start | bytes 8388608
  428.8 218.3 %reduce-scatter.7.cloned.1.call-start = ((), (), s32[]{:S(2)}) async-start(), calls=%async_computation.9 | async-start | bytes 5242880 | tf_op jit(solution)/shard_map/reduce_scatter | solution.py:395
  429.0 15.5 %copy-start.60 = (bf16[2048,1024]{1,0:T(8,128)(2,1)S(1)}, bf16[2048,1024]{1,0:T(8,128)(2,1)}, u32[]{:S(2)}) copy-start(bf16[2048,1024]{1,0:T(8,128)(2,1)} %get-tuple-element.29) | copy-start | bytes 12582916
  457.4 231.9 %reduce-scatter.13.cloned.1.call-start = ((), (), s32[]{:S(2)}) async-start(), calls=%async_computation.12 | async-start | bytes 2621440 | tf_op jit(solution)/shard_map/reduce_scatter | solution.py:525
  478.3 2.2 copy-start.2
  480.5 2.2 copy-start.3
  482.7 2.2 copy-start.4
  484.9 40.9 %copy-start.1 = (bf16[256,2048]{1,0:T(8,128)(2,1)S(1)}, bf16[256,2048]{1,0:T(8,128)(2,1)}, u32[]{:S(2)}) copy-start(bf16[256,2048]{1,0:T(8,128)(2,1)} %copy-done) | copy-start | bytes 3145732
  484.9 40.9 %copy-start.6 = (bf16[2,128,2048]{2,1,0:T(8,128)(2,1)S(1)}, bf16[2,128,2048]{2,1,0:T(8,128)(2,1)}, u32[]{:S(2)}) copy-start(bf16[2,128,2048]{2,1,0:T(8,128)(2,1)} %param.12) | copy-start | bytes 3145732
  484.9 40.9 %copy-start.47 = (f32[2048]{0:T(1024)S(1)}, f32[2048]{0:T(1024)}, u32[]{:S(2)}) copy-start(f32[2048]{0:T(1024)} %copy-done.46) | copy-start | bytes 24580
  484.9 40.9 %copy-start.55 = (f32[256]{0:T(256)S(1)}, f32[256]{0:T(256)}, u32[]{:S(2)}) copy-start(f32[256]{0:T(256)} %copy-done.54) | copy-start | bytes 3076
  525.8 1.6 copy-start.9
  576.5 8.4 copy-start.53
  584.9 24.8 %copy-start.29 = (bf16[8,4,256,32]{2,3,1,0:T(8,128)(2,1)S(1)}, bf16[8,4,256,32]{2,3,1,0:T(8,128)(2,1)}, u32[]{:S(2)}) copy-start(bf16[8,4,256,32]{2,3,1,0:T(8,128)(2,1)} %copy-done.28) | copy-start | bytes 1572868
  584.9 24.8 %copy-start.31 = (bf16[8,4,256,32]{2,3,1,0:T(8,128)(2,1)S(1)}, bf16[8,4,256,32]{2,3,1,0:T(8,128)(2,1)}, u32[]{:S(2)}) copy-start(bf16[8,4,256,32]{2,3,1,0:T(8,128)(2,1)} %copy-done.30) | copy-start | bytes 1572868
  647.2 202.8 %reduce-scatter.17.cloned.1.call-start = ((), (), s32[]{:S(2)}) async-start(), calls=%async_computation.14 | async-start | bytes 1310720 | tf_op jit(solution)/shard_map/reduce_scatter | solution.py:395
  648.2 8.9 %copy-start.12 = (bf16[4,2,2,128,256]{4,3,1,2,0:T(8,128)(2,1)S(1)}, bf16[4,2,2,128,256]{4,3,1,2,0:T(8,128)(2,1)}, u32[]{:S(2)}) copy-start(bf16[4,2,2,128,256]{4,3,1,2,0:T(8,128)(2,1)} %copy-done.11) | copy-start | bytes 3145732
  689.3 9.4 %copy-start.39 = (f32[256,32]{0,1:T(8,128)S(1)}, f32[256,32]{0,1:T(8,128)}, u32[]{:S(2)}) copy-start(f32[256,32]{0,1:T(8,128)} %copy-done.38) | copy-start | bytes 98308
  689.3 160.7 %reduce-scatter.15.cloned.1.call-start = ((), (), s32[]{:S(2)}) async-start(), calls=%async_computation.13 | async-start | bytes 1966080 | tf_op jit(solution)/shard_map/reduce_scatter | solution.py:395
  698.7 3.7 copy-start.17
  699.1 3.6 copy-start.36
  704.4 8.6 copy-start.33
  726.6 40.3 %copy-start.24 = (bf16[256,2048]{1,0:T(8,128)(2,1)S(1)}, bf16[256,2048]{1,0:T(8,128)(2,1)}, u32[]{:S(2)}) copy-start(bf16[256,2048]{1,0:T(8,128)(2,1)} %reduce-scatter.7.cloned.1.call-done.refs_1_) | copy-start | bytes 3145732
  795.8 5.0 copy-start.58
  795.8 5.6 copy-start.19
  795.8 5.6 copy-start.34
  806.1 40.2 %copy-start.7 = (bf16[2,128,2048]{2,1,0:T(8,128)(2,1)S(1)}, bf16[2,128,2048]{2,1,0:T(8,128)(2,1)}, u32[]{:S(2)}) copy-start(bf16[2,128,2048]{2,1,0:T(8,128)(2,1)} %param.12) | copy-start | bytes 3145732
  806.2 40.8 %copy-start.10 = (f32[2,128,2048]{2,1,0:T(8,128)S(1)}, f32[2,128,2048]{2,1,0:T(8,128)}, u32[]{:S(2)}) copy-start(f32[2,128,2048]{2,1,0:T(8,128)} %copy-done.8) | copy-start | bytes 6291460
  850.0 14.2 %copy-start.37 = (bf16[64,2048]{1,0:T(8,128)(2,1)S(1)}, bf16[64,2048]{1,0:T(8,128)(2,1)}, u32[]{:S(2)}) copy-start(bf16[64,2048]{1,0:T(8,128)(2,1)} %param.16) | copy-start | bytes 786436
  850.0 15.5 %copy-start.44 = (bf16[64,512]{1,0:T(8,128)(2,1)S(1)}, bf16[64,512]{1,0:T(8,128)(2,1)}, u32[]{:S(2)}) copy-start(bf16[64,512]{1,0:T(8,128)(2,1)} %param.18) | copy-start | bytes 196612
  850.0 15.5 %copy-start.45 = (bf16[64,512]{1,0:T(8,128)(2,1)S(1)}, bf16[64,512]{1,0:T(8,128)(2,1)}, u32[]{:S(2)}) copy-start(bf16[64,512]{1,0:T(8,128)(2,1)} %param.17) | copy-start | bytes 196612
  862.6 2.1 copy-start.43
  862.6 3.1 copy-start.56
  864.2 2.0 copy-start.40
  864.2 2.0 copy-start.32
  (12 other events, 12.5 us)
Sparse Core Ops, SparseCore 0:
  23.2 48.4 all-gather.15
  73.3 79.5 all-gather.17
  155.1 44.4 all-gather.9
  201.0 26.6 all-gather.11
  229.1 80.2 all-gather.13
  310.8 79.2 all-gather.19
  392.4 75.2 reduce-scatter.8
  470.1 77.2 reduce-scatter.10
  549.7 77.2 reduce-scatter.6
  647.3 41.9 reduce-scatter.12
  691.6 26.4 reduce-scatter.16
  720.4 33.9 reduce-scatter.14

commit v3 on v1

v3 whole, which is shorter than its diff:
```python
import functools

import jax
import jax.numpy as jnp
from jax import lax
from jax.experimental import pallas as pl
from jax.experimental.pallas import tpu as pltpu
from jax.sharding import Mesh
from jax.sharding import PartitionSpec as P

HEADS = 32
KVH = 8
HD = 64
EPSILON = 1e-05
NEGATIVE = -1e30
BF = jnp.bfloat16
F32 = jnp.float32
GROUP = ("a", "core", "cl")
MESH = pl.DeviceIdType.MESH
ANY = pl.BlockSpec(memory_space=pl.ANY)
TILE = 32
MIB = 2**20


def dma(*shape):
    return pltpu.SemaphoreType.DMA(shape)


def places():
    return tuple(lax.axis_index(n) for n in GROUP)


def index_of(a, core, cl):
    return (a * 2 + core) * 2 + cl


def partners():
    a, core, cl = places()
    out = []
    for t in range(1, 8):
        at = (a ^ (t >> 2), core ^ ((t >> 1) & 1), cl ^ (t & 1))
        out.append((dict(zip(GROUP, at)), index_of(*at)))
    return out


def moved_to(c, nz):
    return lax.rem(c, nz), c // nz


def moved_from(c, nz):
    block = lax.rem(c, 2) * nz + c // 2
    return block // 2, lax.rem(block, 2)


def move_pair(nz, back):
    here = lax.axis_index("cm") * 2 + lax.axis_index("cl")
    pair = [dict(zip(("cm", "cl"), f(here, nz))) for f in (moved_to, moved_from)]
    if back:
        pair.reverse()
    return pair, pair[0]["cm"] * 2 + pair[0]["cl"] == here


def greet(whole, line, move, nz):
    barrier = pltpu.get_barrier_semaphore()

    def signal(device):
        pl.semaphore_signal(barrier, inc=1, device_id=device, device_id_type=MESH)

    if whole:
        base = [device for device, _ in partners()]
    else:
        base = [{n: 1 - lax.axis_index(n)} for n in GROUP]
    for device in base:
        signal(device)
    n = len(base)
    if line:
        z = lax.axis_index("cm")
        pl.when(z > 0)(lambda: signal({"cm": z - 1}))
        pl.when(z < nz - 1)(lambda: signal({"cm": z + 1}))
        edge = jnp.logical_or(z == 0, z == nz - 1)
        pl.when(edge)(lambda: pl.semaphore_wait(barrier, n + 1))
        pl.when(jnp.logical_not(edge))(lambda: pl.semaphore_wait(barrier, n + 2))
    elif move is not None:
        pair, stays = move_pair(nz, move)

        @pl.when(jnp.logical_not(stays))
        def _():
            for device in pair:
                signal(device)
            pl.semaphore_wait(barrier, n + 2)

        @pl.when(stays)
        def _():
            pl.semaphore_wait(barrier, n)

    else:
        pl.semaphore_wait(barrier, n)


def remote(src, dst, send, recv, device):
    if isinstance(device, str):
        device = {device: 1 - lax.axis_index(device)}
    return pltpu.make_async_remote_copy(
        src_ref=src, dst_ref=dst, send_sem=send, recv_sem=recv, device_id=device, device_id_type=MESH
    )


def gather_steps(x_ref, o_ref, local, ss, rs):
    a, core, cl = places()
    half = x_ref.shape[0] // 2
    lo, hi = pl.ds(0, half), pl.ds(half, half)
    me = index_of(a, core, cl)
    sx = index_of(1 - a, core, cl)
    sy = index_of(a, core, 1 - cl)
    sd = index_of(1 - a, core, 1 - cl)
    mine = pltpu.make_async_copy(x_ref, o_ref.at[me], local.at[0])

    def put(i, slot, part, name, src=None):
        src = o_ref.at[slot, part] if src is None else src
        return remote(src, o_ref.at[slot, part], ss.at[i], rs.at[i], name)

    sent = [
        put(0, me, lo, "a", x_ref.at[lo]),
        put(1, me, hi, "cl", x_ref.at[hi]),
        put(2, me, hi, "a", x_ref.at[hi]),
        put(3, me, lo, "cl", x_ref.at[lo]),
        put(4, me, pl.ds(0, 2 * half), "core", x_ref),
    ]
    for c in sent:
        c.start()
    mine.start()
    yield

    def on(i, slot, part, name):
        c = put(i, slot, part, name)
        c.start()
        sent.append(c)

    put(0, sx, lo, "a").wait_recv()
    on(5, sx, lo, "cl")
    on(6, sx, lo, "core")
    put(1, sy, hi, "cl").wait_recv()
    on(7, sy, hi, "a")
    on(8, sy, hi, "core")
    yield
    put(2, sx, hi, "a").wait_recv()
    on(9, sx, hi, "core")
    put(3, sy, lo, "cl").wait_recv()
    on(10, sy, lo, "core")
    yield
    put(5, sd, lo, "cl").wait_recv()
    on(11, sd, lo, "core")
    put(7, sd, hi, "a").wait_recv()
    on(12, sd, hi, "core")
    yield
    other = 2 - 4 * core
    put(4, me + other, pl.ds(0, 2 * half), "core").wait_recv()
    for i, slot, part in ((6, sx, lo), (8, sy, hi), (9, sx, hi), (10, sy, lo), (11, sd, lo), (12, sd, hi)):
        put(i, slot + other, part, "core").wait_recv()
    for c in sent:
        c.wait_send()
    mine.wait()


def add_rows(dst, sources, n):
    @pl.loop(0, n // TILE)
    def _(i):
        part = pl.ds(pl.multiple_of(i * TILE, TILE), TILE)
        total = sources[0][part, :].astype(F32)
        for s in sources[1:]:
            total = total + s[part, :].astype(F32)
        dst[part, :] = total.astype(dst.dtype)


def plane_chips():
    a, _, cl = places()
    return (a, cl), (1 - a, cl), (a, 1 - cl), (1 - a, 1 - cl)


def sum_steps(x_ref, o_ref, mine, theirs, first, last, lsem, cs, cr, ss, rs):
    core = lax.axis_index("core")
    out, loc = {}, {}
    for p in (3, 1, 2, 0):
        ca, cc = plane_chips()[p]
        out[p] = remote(x_ref.at[index_of(ca, 1 - core, cc)], theirs.at[p], cs.at[p], cr.at[p], "core")
        out[p].start()
        loc[p] = pltpu.make_async_copy(x_ref.at[index_of(ca, core, cc)], mine.at[p], lsem.at[p])
        loc[p].start()
    yield
    yield from sum_rest(o_ref, mine, theirs, first, last, lsem, out, loc, ss, rs)


def sum_rest(o_ref, mine, theirs, first, last, lsem, out, loc, ss, rs):
    rows = mine.shape[1]
    half = rows // 2
    lo, hi = pl.ds(0, half), pl.ds(half, half)

    def chip_sum(p):
        out[p].wait_recv()
        if p in loc:
            loc[p].wait()
        add_rows(mine.at[p], (mine.at[p], theirs.at[p]), rows)

    chip_sum(3)
    xd = remote(mine.at[3, lo], first.at[0], ss.at[0], rs.at[0], "a")
    yd = remote(mine.at[3, hi], first.at[1], ss.at[1], rs.at[1], "cl")
    xd.start()
    yd.start()
    chip_sum(1)
    xo = remote(mine.at[1, lo], first.at[2], ss.at[2], rs.at[2], "a")
    xo.start()
    chip_sum(2)
    yo = remote(mine.at[2, hi], first.at[3], ss.at[3], rs.at[3], "cl")
    yo.start()
    chip_sum(0)
    yield
    xd.wait_recv()
    add_rows(mine.at[2, lo], (mine.at[2, lo], first.at[0]), half)
    y2 = remote(mine.at[2, lo], last.at[0], ss.at[4], rs.at[4], "cl")
    y2.start()
    yd.wait_recv()
    add_rows(mine.at[1, hi], (mine.at[1, hi], first.at[1]), half)
    x2 = remote(mine.at[1, hi], last.at[1], ss.at[5], rs.at[5], "a")
    x2.start()
    yield
    xo.wait_recv()
    add_rows(mine.at[0, lo], (mine.at[0, lo], first.at[2]), half)
    yo.wait_recv()
    add_rows(mine.at[0, hi], (mine.at[0, hi], first.at[3]), half)
    yield
    y2.wait_recv()
    add_rows(mine.at[0, lo], (mine.at[0, lo], last.at[0]), half)
    x2.wait_recv()
    add_rows(mine.at[0, hi], (mine.at[0, hi], last.at[1]), half)
    done = pltpu.make_async_copy(mine.at[0], o_ref, lsem.at[4])
    done.start()
    for c in (*out.values(), xd, yd, xo, yo, y2, x2):
        c.wait_send()
    done.wait()


def swap_steps(kind, pieces, src, dst, lsem, ss, rs):
    me = index_of(*places())
    copies = []
    for p in range(pieces):

        def block(f, p=p):
            return ((f // 2) * pieces + p) * 2 + lax.rem(f, 2) if pieces > 1 else f

        width = (dst if kind == "cols" else src).shape[-1] // pieces

        def cut(ref, i, width=width):
            return ref.at[:, pl.ds(pl.multiple_of(i * width, width), width)]

        def part(ref, i, p=p, width=width):
            return ref.at[i] if pieces == 1 else ref.at[i, :, pl.ds(p * width, width)]

        def source(f, block=block, cut=cut, part=part):
            return cut(src, block(f)) if kind == "cols" else part(src, f)

        target = cut(dst, block(me)) if kind == "back" else part(dst, me)
        for t, (device, index) in enumerate(partners()):
            copies.append(remote(source(index), target, ss.at[p, t], rs.at[p, t], device))
            copies[-1].start()
        copies.append(pltpu.make_async_copy(source(me), target, lsem.at[p]))
        copies[-1].start()
    yield
    yield
    yield
    yield
    for copy in copies:
        copy.wait()


def move_steps(nz, back, src, dst, lsem, ss, rs):
    pair, stays = move_pair(nz, back)
    mine = pltpu.make_async_copy(src, dst, lsem.at[0])
    away = remote(src, dst, ss.at[0], rs.at[0], pair[0])
    pl.when(stays)(mine.start)
    pl.when(jnp.logical_not(stays))(away.start)
    yield
    yield
    yield
    yield
    pl.when(stays)(mine.wait)
    pl.when(jnp.logical_not(stays))(away.wait)


def up_steps(nz, x_ref, o_ref, lsem, ss, rs):
    z = lax.axis_index("cm")
    mine = pltpu.make_async_copy(x_ref, o_ref.at[z], lsem.at[0])
    mine.start()

    def send(j, src):
        return remote(src, o_ref.at[j], ss.at[j], rs.at[j], {"cm": jnp.minimum(z + 1, nz - 1)})

    @pl.when(z < nz - 1)
    def _():
        send(z, x_ref).start()

    yield
    for i in range(1, nz):

        @pl.when(z >= i)
        def _(i=i):
            j = z - i
            send(j, o_ref.at[j]).wait_recv()

            @pl.when(z < nz - 1)
            def _():
                send(j, o_ref.at[j]).start()

        yield
    for i in range(nz):

        @pl.when(jnp.logical_and(z >= i, z < nz - 1))
        def _(i=i):
            send(z - i, x_ref).wait_send()

    mine.wait()


def pass_steps(src, dst, lsem):
    copy = pltpu.make_async_copy(src, dst, lsem.at[0])
    copy.start()
    yield
    yield
    yield
    copy.wait()


def down_steps(nz, x_ref, o_ref, mine, came, lsem, ss, rs):
    z = lax.axis_index("cm")
    rows = x_ref.shape[1]

    def load(j):
        return pltpu.make_async_copy(x_ref.at[j], mine.at[j], lsem.at[j])

    def send(j):
        return remote(mine.at[j], came.at[j], ss.at[j], rs.at[j], {"cm": jnp.maximum(z - 1, 0)})

    for j in range(nz):
        pl.when(z >= j)(lambda j=j: load(j).start())
    yield
    for j in range(nz):

        @pl.when(z >= j)
        def _(j=j):
            load(j).wait()

            @pl.when(z < nz - 1)
            def _():
                send(j).wait_recv()
                add_rows(mine.at[j], (mine.at[j], came.at[j]), rows)

            @pl.when(z > j)
            def _():
                send(j).start()

        yield
    done = pltpu.make_async_copy(mine.at[z], o_ref, lsem.at[nz])
    done.start()
    for j in range(nz):
        pl.when(z > j)(lambda j=j: send(j).wait_send())
    done.wait()


def back_steps(nz, r, hid_ref, one_ref, two_ref, wone_ref, wtwo_ref, o_ref, out_one, out_two, *scratch):
    hid, g, w, out, stage, theirs, first, last, gsem, osem, lsem, cs, cr, ss, rs = scratch
    tiles, _, wide = hid.shape
    run = 2 * r
    per = wide // run
    core = lax.axis_index("core")
    rows, width = theirs.shape[1:]
    loads = [
        pltpu.make_async_copy(src, dst, gsem.at[n])
        for n, (src, dst) in enumerate(
            [(wone_ref, w.at[0]), (one_ref, g.at[0]), (wtwo_ref, w.at[1]), (two_ref, g.at[1])]
            + [(hid_ref.at[:, pl.ds(i * wide, wide)], hid.at[i]) for i in range(tiles)]
        )
    ]
    for c in loads:
        c.start()
    for c in loads[:4]:
        c.wait()

    @pl.loop(0, 8)
    def _(n):
        to = jnp.where(n < 4, 1 - core, core)
        turn = lax.rem(n, 4)
        a, _, cl = places()
        far_a = jnp.where(jnp.logical_or(turn == 0, turn == 1), 1 - a, a)
        far_cl = jnp.where(jnp.logical_or(turn == 0, turn == 2), 1 - cl, cl)
        p = jnp.where(turn == 0, 3, jnp.where(turn == 3, 0, turn))
        first_row = pl.multiple_of(index_of(far_a, to, far_cl) * rows, rows)
        for c in range(0, width, width // 2):
            part = pl.ds(c, width // 2)
            e = dot(g[0, pl.ds(first_row, rows), :], w[0, part, :], 1, 1)
            e += dot(g[1, pl.ds(first_row, rows), :], w[1, part, :], 1, 1)
            stage[n // 4, p, :, part] = e.astype(BF)

        @pl.when(n < 4)
        def _():
            remote(stage.at[0, p], theirs.at[p], cs.at[p], cr.at[p], "core").start()

    out_core = {p: remote(stage.at[0, p], theirs.at[p], cs.at[p], cr.at[p], "core") for p in range(4)}
    for c in loads[4:]:
        c.wait()

    def store(k, i, p):
        chunk = i * per + p
        at = (lax.rem(chunk, nz) * 4 + chunk // nz) * run
        target = (out_one, out_two)[k]
        return pltpu.make_async_copy(
            out.at[k, i, pl.ds(p * run, run)], target.at[pl.ds(pl.multiple_of(at, run), run)], osem.at[k, i, p]
        )

    def products(k, lo, hi):
        @pl.loop(lo, hi)
        def _(i):
            out[k, i] = dot(hid[i], g[k], 0, 0).astype(BF)
            for p in range(per):
                store(k, i, p).start()

    summing = sum_rest(o_ref, stage.at[1], theirs, first, last, lsem, out_core, {}, ss, rs)
    half = tiles // 2
    for k, lo, hi in ((1, 0, half), (1, half, tiles), (0, 0, half), (0, half, tiles)):
        next(summing, None)
        products(k, lo, hi)
    for _ in summing:
        pass
    for k in range(2):

        @pl.loop(0, tiles)
        def _(i, k=k):
            for p in range(per):
                store(k, i, p).wait()

    yield


def product_steps(a_ref, b_ref, o_ref, a, b, out, lsem, osem):
    tiles, rows, _ = out.shape
    loads = [pltpu.make_async_copy(a_ref, a, lsem.at[0]), pltpu.make_async_copy(b_ref, b, lsem.at[1])]
    for c in loads:
        c.start()
    for c in loads:
        c.wait()

    def store(i):
        return pltpu.make_async_copy(out.at[i], o_ref.at[pl.ds(pl.multiple_of(i * rows, rows), rows)], osem.at[i])

    half = b.shape[1] // 2
    for lo, hi in ((0, tiles // 2), (tiles // 2, tiles)):

        @pl.loop(lo, hi)
        def _(i):
            left = a[pl.ds(pl.multiple_of(i * rows, rows), rows), :]
            for c in (0, half):
                out[i, :, c : c + half] = dot(left, b[:, c : c + half]).astype(BF)
            store(i).start()

        yield

    @pl.loop(0, tiles)
    def _(i):
        store(i).wait()


def heads_steps(x_ref, wo_ref, low_ref, heads_ref, g_ref, buf, wo, low, heads, total, g, lsem, local, ss, rs):
    loads = [pltpu.make_async_copy(wo_ref, wo, lsem.at[0]), pltpu.make_async_copy(low_ref, low, lsem.at[1])]
    for c in loads:
        c.start()
    yield from gather_steps(x_ref, buf, local, ss, rs)
    for c in loads:
        c.wait()
    total[...] = jnp.zeros_like(total)
    rows = buf.shape[1]

    @pl.loop(0, 8)
    def _(i):
        block = buf[i]
        part = pl.ds(pl.multiple_of(i * rows, rows), rows)
        heads[part, :] = dot(block, wo[...], 1, 1).astype(BF)
        total[...] += dot(low[part, :], block, 0, 0)

    g[...] = total[...].astype(BF)
    stores = [pltpu.make_async_copy(heads, heads_ref, lsem.at[2]), pltpu.make_async_copy(g, g_ref, lsem.at[3])]
    for c in stores:
        c.start()
    for c in stores:
        c.wait()


def part(kind, *xs, **how):
    nz = lax.axis_size("cm")
    x = xs[0]
    like = lambda *shape: jax.ShapeDtypeStruct(shape, x.dtype)
    vmem = lambda *shape: pltpu.VMEM(shape, x.dtype)
    if kind == "gather":
        rows, cols = x.shape
        return kind, gather_steps, xs, [like(8, rows, cols)], [dma(1), dma(13), dma(13)]
    if kind == "sum":
        rows, cols = x.shape[0] // 8, x.shape[1]
        scratch = [vmem(n, m, cols) for n, m in ((4, rows), (4, rows), (4, rows // 2), (2, rows // 2))]
        scratch += [dma(5), dma(4), dma(4), dma(6), dma(6)]
        return kind, sum_steps, [x.reshape(8, rows, cols)], [like(rows, cols)], scratch
    if kind == "up":
        return kind, functools.partial(up_steps, nz), xs, [like(nz, *x.shape)], [dma(1), dma(nz), dma(nz)]
    if kind == "pass":
        return kind, pass_steps, xs, [like(*x.shape)], [dma(1)]
    if kind == "down":
        scratch = [vmem(*x.shape)] * 2 + [dma(nz + 1), dma(nz), dma(nz)]
        return kind, functools.partial(down_steps, nz), xs, [like(*x.shape[1:])], scratch
    if kind in ("move", "home"):
        return kind, functools.partial(move_steps, nz, kind == "home"), xs, [like(*x.shape)], [dma(1), dma(1), dma(1)]
    if kind == "mlp":
        rows, width = x.shape
        cols = xs[1].shape[1]
        r = width // (8 * nz)
        wide = 256
        tiles = width // wide
        block = rows // 8
        scratch = [vmem(tiles, rows, wide), vmem(2, rows, cols), vmem(2, width, cols), vmem(2, tiles, wide, cols)]
        scratch += [vmem(2, 4, block, width), vmem(4, block, width), vmem(4, block // 2, width)]
        scratch += [vmem(2, block // 2, width), dma(4 + tiles), dma(2, tiles, wide // (2 * r))]
        scratch += [dma(5), dma(4), dma(4), dma(6), dma(6)]
        outs = [like(block, width), like(width, cols), like(width, cols)]
        return kind, functools.partial(back_steps, nz, r), xs, outs, scratch
    if kind == "product":
        rows, cols = x.shape[0], xs[1].shape[1]
        scratch = [vmem(*x.shape), vmem(*xs[1].shape), vmem(8, rows // 8, cols), dma(2), dma(8)]
        return kind, product_steps, xs, [like(rows, cols)], scratch
    if kind == "heads":
        rows, cols = x.shape
        wide = xs[1].shape[0]
        scratch = [vmem(8, rows, cols), vmem(wide, cols), vmem(8 * rows, wide), vmem(8 * rows, wide)]
        scratch += [pltpu.VMEM((wide, cols), F32), vmem(wide, cols), dma(4), dma(1), dma(13), dma(13)]
        return kind, heads_steps, xs, [like(8 * rows, wide), like(wide, cols)], scratch
    pieces = how.get("pieces", 1)
    shape = x.shape
    if kind == "cols":
        shape = (8, x.shape[0], x.shape[1] // 8)
    elif kind == "back":
        shape = (x.shape[1], 8 * x.shape[2])
    scratch = [dma(pieces), dma(pieces, 7), dma(pieces, 7)]
    return kind, functools.partial(swap_steps, kind, pieces), xs, [like(*shape)], scratch


def transfer(cid, parts, deps=()):
    nz = lax.axis_size("cm")
    kinds = [p[0] for p in parts]
    operands = [x for p in parts for x in p[2]]
    results = [o for p in parts for o in p[3]]
    moves = [k == "home" for k in kinds if k in ("move", "home")]
    whole = any(k in ("slab", "cols", "back") for k in kinds)
    line = any(k in ("up", "down") for k in kinds)

    def kernel(*refs):
        ins = list(refs[: len(operands)])
        rest = list(refs[len(operands) + len(deps) :])
        outs, scratch = rest[: len(results)], rest[len(results) :]

        def take(refs, n):
            out = refs[:n]
            del refs[:n]
            return out

        greet(whole, line, moves[0] if moves else None, nz)
        running = []
        for _, steps, xs, shapes, own in parts:
            running.append(steps(*take(ins, len(xs)), *take(outs, len(shapes)), *take(scratch, len(own))))
        while running:
            still = []
            for steps in running:
                try:
                    next(steps)
                except StopIteration:
                    continue
                still.append(steps)
            running = still

    return pl.pallas_call(
        kernel,
        out_shape=results,
        in_specs=[ANY] * (len(operands) + len(deps)),
        out_specs=[ANY] * len(results),
        scratch_shapes=[s for p in parts for s in p[4]],
        compiler_params=pltpu.CompilerParams(
            collective_id=cid, has_side_effects=True, vmem_limit_bytes=56 * MIB
        ),
        name="_".join(kinds) + str(cid),
    )(*operands, *deps)


def after(x, deps):
    return pl.pallas_call(
        lambda *refs: None,
        out_shape=jax.ShapeDtypeStruct(x.shape, x.dtype),
        in_specs=[ANY] * (1 + len(deps)),
        out_specs=ANY,
        input_output_aliases={0: 0},
        name="after",
    )(x, *deps)


def sum_planes(g):
    return lax.psum_scatter(g, "cm", scatter_dimension=0, tiled=True)


def gather_planes(x):
    return lax.all_gather(x, "cm", axis=0, tiled=True)


def dot(a, b, left=1, right=0):
    return lax.dot_general(a, b, (((left,), (right,)), ((), ())), preferred_element_type=F32)


def rope(u, cos, sin):
    width = u.shape[-1]
    lane = lax.broadcasted_iota(jnp.int32, u.shape, 1)
    other = jnp.where(lane % HD < HD // 2, pltpu.roll(u, width - HD // 2, 1), pltpu.roll(u, HD // 2, 1))
    return u * cos + other * sin


def tables(positions):
    lane = jnp.arange(2 * HD)
    frequency = 500000.0 ** (-(lane % (HD // 2)).astype(F32) * 2.0 / HD)
    angles = positions.astype(F32)[..., None] * frequency
    return jnp.cos(angles), jnp.where(lane % HD < HD // 2, -1.0, 1.0) * jnp.sin(angles)


def project_kernel(x_ref, gain_ref, w_ref, cos_ref, sin_ref, hid_ref, q_ref, kv_ref):
    x = x_ref[...].astype(F32)
    hid = (x * lax.rsqrt(jnp.mean(x * x, -1, keepdims=True) + EPSILON) * gain_ref[...]).astype(BF)
    hid_ref[...] = hid
    u = dot(hid, w_ref[...])
    times = x.shape[0] // cos_ref.shape[1]
    cos = jnp.concatenate([cos_ref[0]] * times, 0)
    sin = jnp.concatenate([sin_ref[0]] * times, 0)
    wide = q_ref.shape[-1]
    copies = wide // (2 * HD)
    q_ref[...] = rope(u[:, :wide], jnp.concatenate([cos] * copies, 1), jnp.concatenate([sin] * copies, 1)).astype(BF)
    kv = u[:, wide:]
    lane = lax.broadcasted_iota(jnp.int32, kv.shape, 1)
    kv_ref[...] = jnp.where(lane < HD, rope(kv, cos, sin), kv).astype(BF)


def project(x, gain, w, wide, cos, sin):
    rows, width = x.shape
    step = rows // 8
    block = cos.shape[1]
    table = pl.BlockSpec((1, block, 2 * HD), lambda g: (g % 2, 0, 0))
    return pl.pallas_call(
        project_kernel,
        grid=(8,),
        out_shape=[jax.ShapeDtypeStruct((rows, c), BF) for c in (width, wide, 2 * HD)],
        in_specs=[
            pl.BlockSpec((step, width), lambda g: (g, 0)),
            pl.BlockSpec((1, width), lambda g: (0, 0)),
            pl.BlockSpec((width, wide + 2 * HD), lambda g: (0, 0)),
            table,
            table,
        ],
        out_specs=[pl.BlockSpec((step, c), lambda g: (g, 0)) for c in (width, wide, 2 * HD)],
        compiler_params=pltpu.CompilerParams(vmem_limit_bytes=48 * MIB),
        name="project",
    )(x, gain, w, cos, sin)


def project_back_kernel(dq_ref, dkv_ref, hid_ref, w_ref, cos_ref, sin_ref, e_ref, g_ref, total):
    step = pl.program_id(0)

    @pl.when(step == 0)
    def _():
        total[...] = jnp.zeros_like(total)

    dq = dq_ref[...]
    times = dq.shape[0] // cos_ref.shape[1]
    cos = jnp.concatenate([cos_ref[0]] * times, 0)
    sin = -jnp.concatenate([sin_ref[0]] * times, 0)
    copies = dq.shape[1] // (2 * HD)
    dq = rope(dq, jnp.concatenate([cos] * copies, 1), jnp.concatenate([sin] * copies, 1))
    dkv = dkv_ref[...].astype(F32)
    lane = lax.broadcasted_iota(jnp.int32, dkv.shape, 1)
    dkv = jnp.where(lane < HD, rope(dkv, cos, sin), dkv)
    rows = jnp.concatenate([dq.astype(BF), dkv.astype(BF)], 1)
    e_ref[...] = dot(rows, w_ref[...], 1, 1).astype(BF)
    total[...] += dot(hid_ref[...], rows, 0, 0)

    @pl.when(step == pl.num_programs(0) - 1)
    def _():
        g_ref[...] = total[...].astype(BF)


def project_back(dq, dkv, hid, w, cos, sin):
    rows, width = hid.shape
    step = rows // 8
    shape = (width, dq.shape[1] + 2 * HD)
    block = cos.shape[1]
    table = pl.BlockSpec((1, block, 2 * HD), lambda g: (g % 2, 0, 0))
    return pl.pallas_call(
        project_back_kernel,
        grid=(8,),
        out_shape=[jax.ShapeDtypeStruct((rows, width), BF), jax.ShapeDtypeStruct(shape, BF)],
        in_specs=[
            pl.BlockSpec((step, dq.shape[1]), lambda g: (g, 0)),
            pl.BlockSpec((step, 2 * HD), lambda g: (g, 0)),
            pl.BlockSpec((step, width), lambda g: (g, 0)),
            pl.BlockSpec(shape, lambda g: (0, 0)),
            table,
            table,
        ],
        out_specs=[pl.BlockSpec((step, width), lambda g: (g, 0)), pl.BlockSpec(shape, lambda g: (0, 0))],
        scratch_shapes=[pltpu.VMEM(shape, F32)],
        compiler_params=pltpu.CompilerParams(vmem_limit_bytes=48 * MIB),
        name="project_back",
    )(dq, dkv, hid, w, cos, sin)


def flat(ref):
    x = ref[...]
    return x.reshape(x.shape[-4] * x.shape[-2], x.shape[-1])


def heads_of(x):
    return [x[:, h * HD : (h + 1) * HD] for h in range(x.shape[1] // HD)]


def seen(n, j, z, slots):
    col = lax.broadcasted_iota(jnp.int32, (slots, slots), 0) + j * slots
    row = lax.broadcasted_iota(jnp.int32, (slots, slots), 1) + z * slots
    return jnp.logical_and(col <= row, col < n)


def attend_kernel(lens, q_ref, kv_ref, att_ref, low_ref, log_ref, scores, top, sums, acc):
    z = lax.axis_index("cm")
    n = lens[pl.program_id(0) * pl.num_programs(1) + pl.program_id(1)]
    q = flat(q_ref)
    slots = q.shape[0]
    qs = heads_of((q.astype(F32) * HD ** (-0.5)).astype(BF))
    top[...] = jnp.full_like(top, NEGATIVE)
    sums[...] = jnp.zeros_like(sums)
    acc[...] = jnp.zeros_like(acc)

    def score(j, _):
        k = flat(kv_ref.at[j])[:, :HD]
        mask = seen(n, j, z, slots)
        for h, qh in enumerate(qs):
            s = jnp.where(mask, dot(k, qh, 1, 1), NEGATIVE)
            scores[j, h] = s
            top[h : h + 1] = jnp.maximum(top[h : h + 1], jnp.max(s, 0, keepdims=True))
        return 0

    blocks = jnp.minimum(z + 1, (n + slots - 1) // slots)
    lax.fori_loop(0, blocks, score, 0)

    def weigh(j, _):
        v = flat(kv_ref.at[j])[:, HD:]
        for h in range(len(qs)):
            p = jnp.exp(scores[j, h] - top[h : h + 1])
            sums[h : h + 1] += jnp.sum(p, 0, keepdims=True)
            acc[h * HD : (h + 1) * HD] += dot(v, p.astype(BF), 0, 0)
        return 0

    lax.fori_loop(0, blocks, weigh, 0)
    out = jnp.concatenate([acc[h * HD : (h + 1) * HD] / sums[h : h + 1] for h in range(len(qs))], 0)
    att_ref[0, 0] = out
    low_ref[...] = out.T.astype(BF).reshape(low_ref.shape)
    log_ref[0, 0] = top[...] + jnp.log(sums[...])


def attend_back_kernel(lens, q_ref, kv_ref, do_ref, att_ref, log_ref, dq_ref, dkv_ref, acc):
    z = lax.axis_index("cm")
    n = lens[pl.program_id(0) * pl.num_programs(1) + pl.program_id(1)]
    q = flat(q_ref)
    slots = q.shape[0]
    qs = heads_of((q.astype(F32) * HD ** (-0.5)).astype(BF))
    do = flat(do_ref)
    dos = heads_of(do)
    both = do.astype(F32).T * att_ref[0, 0]
    deltas = [jnp.sum(both[h * HD : (h + 1) * HD], 0, keepdims=True) for h in range(len(qs))]
    acc[...] = jnp.zeros_like(acc)

    def step(j, _):
        kv = flat(kv_ref.at[j])
        k, v = kv[:, :HD], kv[:, HD:]
        mask = seen(n, j, z, slots)
        dk = jnp.zeros((slots, HD), F32)
        dv = jnp.zeros((slots, HD), F32)
        for h, qh in enumerate(qs):
            s = jnp.where(mask, dot(k, qh, 1, 1), NEGATIVE)
            p = jnp.exp(s - log_ref[0, 0, h : h + 1])
            ds = (p * (dot(v, dos[h], 1, 1) - deltas[h])).astype(BF)
            acc[h * HD : (h + 1) * HD] += dot(k, ds, 0, 0)
            dk += dot(ds, qh)
            dv += dot(p.astype(BF), dos[h])
        out = jnp.concatenate([dk, dv], 1).astype(BF)
        dkv_ref[j] = out.reshape(dkv_ref.shape[1:])
        return 0

    live = jnp.where(z * slots < n, z + 1, 0)
    lax.fori_loop(0, live, step, 0)

    def nothing(j, _):
        dkv_ref[j] = jnp.zeros(dkv_ref.shape[1:], BF)
        return 0

    lax.fori_loop(live, z + 1, nothing, 0)
    dq_ref[...] = (acc[...] * HD ** (-0.5)).T.reshape(dq_ref.shape)


def attention_specs(seqs, block, wide, nz):
    own = lambda c: pl.BlockSpec((1, 2, 1, block, c), lambda f, s: (f, 0, s, 0, 0))
    every = pl.BlockSpec((nz, 1, 2, 1, block, 2 * HD), lambda f, s: (0, f, 0, s, 0, 0))
    turned = lambda c: pl.BlockSpec((1, 1, c, 2 * block), lambda f, s: (f, s, 0, 0))
    return own(wide), every, turned(wide), turned(wide // HD)


def attend(lens, q, kv, seqs, block):
    nz, rows, _ = kv.shape
    wide = q.shape[1]
    heads = wide // HD
    own, every, turned, logs = attention_specs(seqs, block, wide, nz)
    view = (4, 2, seqs, block)
    att, low, log = pl.pallas_call(
        attend_kernel,
        grid=(4, seqs),
        out_shape=[
            jax.ShapeDtypeStruct((4, seqs, wide, 2 * block), F32),
            jax.ShapeDtypeStruct((*view, wide), BF),
            jax.ShapeDtypeStruct((4, seqs, heads, 2 * block), F32),
        ],
        in_specs=[pl.BlockSpec(memory_space=pltpu.SMEM), own, every],
        out_specs=[turned, own, logs],
        scratch_shapes=[
            pltpu.VMEM((nz, heads, 2 * block, 2 * block), F32),
            pltpu.VMEM((heads, 2 * block), F32),
            pltpu.VMEM((heads, 2 * block), F32),
            pltpu.VMEM((wide, 2 * block), F32),
        ],
        compiler_params=pltpu.CompilerParams(vmem_limit_bytes=48 * MIB),
        name="attend",
    )(lens, q.reshape(*view, wide), kv.reshape(nz, *view, 2 * HD))
    return att, low.reshape(rows, wide), log


def attend_back(lens, q, kv, do, att, log, seqs, block):
    nz, rows, _ = kv.shape
    wide = q.shape[1]
    own, every, turned, logs = attention_specs(seqs, block, wide, nz)
    view = (4, 2, seqs, block)
    dq, dkv = pl.pallas_call(
        attend_back_kernel,
        grid=(4, seqs),
        out_shape=[
            jax.ShapeDtypeStruct((*view, wide), F32),
            jax.ShapeDtypeStruct((nz, *view, 2 * HD), BF),
        ],
        in_specs=[pl.BlockSpec(memory_space=pltpu.SMEM), own, every, own, turned, logs],
        out_specs=[own, every],
        scratch_shapes=[pltpu.VMEM((wide, 2 * block), F32)],
        compiler_params=pltpu.CompilerParams(vmem_limit_bytes=48 * MIB),
        name="attend_back",
    )(lens, q.reshape(*view, wide), kv.reshape(nz, *view, 2 * HD), do.reshape(*view, wide), att, log)
    return dq.reshape(rows, wide), dkv.reshape(nz, rows, 2 * HD)


def rms_scale(field):
    return lax.rsqrt(jnp.mean(field * field, -1, keepdims=True) + EPSILON)


def norm_back(grad_normed, normed, scale_rows):
    return scale_rows * (grad_normed - normed * jnp.mean(grad_normed * normed, -1, keepdims=True))


def rows_of(x):
    nz = lax.axis_size("cm")
    _, r, c = x.shape
    x = gather_planes(x)
    return x.reshape(nz, 4, 2, r, c).transpose(1, 0, 2, 3, 4).reshape(nz * 8 * r, c)


def rows_first(g):
    nz = lax.axis_size("cm")
    rows, c = g.shape
    r = rows // (8 * nz)
    return g.astype(BF).reshape(4, nz, 2, r, c).transpose(1, 0, 2, 3, 4).reshape(nz * 8, r, c)


def on_device(
    tokens, lengths, cotangent, attn_gain, w_query, w_key, w_value, w_out, mlp_gain, w_gate, w_up, w_down
):
    seqs, block, width = tokens.shape
    nz = lax.axis_size("cm")
    rows = seqs * block
    r = w_query.shape[0]
    wide = HEADS // 8 * HD
    cm = lax.axis_index("cm")
    cl = lax.axis_index("cl")
    gain_two = mlp_gain.astype(F32)[:, None]
    pieces = nz if w_down.shape[0] % 128 == 0 else 1
    perm = [(c, (c % nz) * 2 + c // nz) for c in range(2 * nz)]
    home = [(t, s) for s, t in perm]

    def gained(w):
        return (w.astype(F32) * gain_two).astype(BF)

    pack = [w.reshape(r, 8, -1) for w in (w_query, w_key, w_value)]
    pack.append(jnp.broadcast_to(attn_gain[:, None, None], (r, 8, 2 * HD)))
    pack = jnp.concatenate(pack, -1).transpose(1, 0, 2)
    lens = jnp.broadcast_to(jnp.pad(lengths, (0, 128 - seqs))[None, None], (8, 8, 128))
    pack, lens = transfer(1, [part("slab", pack), part("slab", lens)])
    lens = lens[::2, 0, :seqs].reshape(-1)
    wg, wo = transfer(2, [part("cols", gained(w_gate), pieces=pieces), part("move", w_out)], (pack,))
    own = tokens.reshape(rows, width)
    tok_all, wu = transfer(3, [part("gather", own), part("cols", gained(w_up), pieces=pieces)], (wg,))
    pack = rows_of(pack)
    gain_row = pack[:, wide + 2 * HD].astype(F32)[None]
    wg = rows_of(wg)
    wo = gather_planes(wo)

    slot = cm * 2 * block + jnp.arange(2 * block, dtype=jnp.int32).reshape(2, block)
    cos, sin = tables(slot)
    hidden_one, q, kv = project(tok_all.reshape(8 * rows, width), gain_row, pack, wide, cos, sin)
    own_pos = cm * 2 * block + cl * block + jnp.arange(block, dtype=jnp.int32)
    valid = (own_pos[None, :] < lengths[:, None]).astype(F32)
    grad_out = (cotangent.astype(F32) * valid[..., None]).reshape(rows, width)
    grad_low, kv_all, down = transfer(
        4,
        [
            part("gather", grad_out.astype(BF)),
            part("up", kv),
            part("pass", w_down),
        ],
    )
    grad_low = grad_low.reshape(8 * rows, width)
    wu = rows_of(wu)
    att, att_low, log = attend(lens, q, kv_all, seqs, block)

    resid_in = own.astype(F32)
    (mid,) = transfer(5, [part("sum", dot(att_low, wo).astype(BF))], (wg,))
    wd = gather_planes(down if pieces > 1 else lax.ppermute(down, ("cm", "cl"), perm))
    resid_mid = resid_in + mid.astype(F32)
    scale_two = rms_scale(resid_mid)
    normed_two = resid_mid * scale_two
    (hidden_two,) = transfer(6, [part("gather", normed_two.astype(BF))], (wu,))
    hidden_two = hidden_two.reshape(8 * rows, width)
    gate_pre = dot(hidden_two, wg)
    up_pre = dot(hidden_two, wu)
    sig = jax.nn.sigmoid(gate_pre)
    act = gate_pre * sig
    inner = (act * up_pre).astype(BF)
    grad_wd = dot(inner, grad_low, 0, 0).astype(BF)
    wd = after(wd, (grad_wd,))
    grad_inner = dot(grad_low, wd, 1, 1).astype(BF).astype(F32)
    grad_gate = (grad_inner * up_pre * (sig * (1.0 + gate_pre * (1.0 - sig)))).astype(BF)
    grad_up = (grad_inner * act).astype(BF)
    e_two, grad_wg, grad_wu = transfer(7, [part("mlp", hidden_two, grad_gate, grad_up, wg, wu)])
    by_owner = lambda g: sum_planes(g.reshape(8 * nz, r, -1))
    grad_wd, grad_wu, grad_wg = sum_planes(grad_wd), by_owner(grad_wu), by_owner(grad_wg)
    grad_mid = grad_out + norm_back(e_two.astype(F32), normed_two, scale_two)
    grad_heads, grad_wo, out_part = transfer(
        8, [part("heads", grad_mid.astype(BF), wo, att_low), part("product", inner, wd)], (grad_wd,)
    )
    dq, dkv = attend_back(lens, q, kv_all, grad_heads, att, log, seqs, block)
    dkv, out_sum, grad_wu = transfer(
        9, [part("down", dkv), part("sum", out_part), part("back", grad_wu, pieces=pieces)]
    )
    layer_out = (resid_mid + out_sum.astype(F32)).astype(BF)
    e_one, grad_qkv = project_back(dq, dkv, hidden_one, pack, cos, sin)
    e_one, grad_wg = transfer(10, [part("sum", e_one), part("back", grad_wg, pieces=pieces)])
    grad_wo = sum_planes(grad_wo)
    grad_qkv = sum_planes(rows_first(grad_qkv))
    scale_one = rms_scale(resid_in)
    grad_tokens = grad_mid + norm_back(e_one.astype(F32) * gain_row, resid_in * scale_one, scale_one)
    grad_qkv, grad_wo = transfer(11, [part("slab", grad_qkv), part("home", grad_wo)], (e_one,))
    if pieces == 1:
        grad_wd = lax.ppermute(grad_wd, ("cm", "cl"), home)
    grad_qkv = grad_qkv.transpose(1, 0, 2).astype(F32)
    grad_wq = grad_qkv[..., :wide].reshape(r, 8 * wide)
    grad_wk = grad_qkv[..., wide : wide + HD].reshape(r, 8 * HD)
    grad_wv = grad_qkv[..., wide + HD :].reshape(r, 8 * HD)
    grad_wg, grad_wu = grad_wg.astype(F32), grad_wu.astype(F32)

    def gain_grad(pairs):
        return sum(jnp.sum(w.astype(F32) * g, -1) for w, g in pairs)

    gain_grad_one = gain_grad(((w_query, grad_wq), (w_key, grad_wk), (w_value, grad_wv))) / attn_gain.astype(F32)
    gain_grad_two = gain_grad(((w_gate, grad_wg), (w_up, grad_wu)))
    return (
        layer_out.reshape(seqs, block, width),
        grad_tokens.reshape(seqs, block, width).astype(BF),
        gain_grad_one,
        grad_wq,
        grad_wk,
        grad_wv,
        grad_wo.astype(F32),
        gain_grad_two,
        grad_wg * gain_two,
        grad_wu * gain_two,
        grad_wd.astype(F32),
    )


def solution(mesh):
    fsdp, ctx = mesh.devices.shape
    fine = Mesh(mesh.devices.reshape(fsdp // 2, 2, ctx // 2, 2), ("a", "core", "cm", "cl"))
    token = P(("a", "core"), ("cm", "cl"), None)
    vector = P(("a", "core", "cm", "cl"))
    matrix = P(("a", "core", "cm", "cl"), None)
    return jax.shard_map(
        on_device,
        mesh=fine,
        in_specs=(
            token,
            P(("a", "core")),
            token,
            vector,
            matrix,
            matrix,
            matrix,
            matrix,
            vector,
            matrix,
            matrix,
            matrix,
        ),
        out_specs=(token, token, vector, matrix, matrix, matrix, matrix, vector, matrix, matrix, matrix),
        check_vma=False,
    )
```

time: 1480 us -> 789 us (0.53)
  waiting for transfers between devices: 962 us -> 36.3 us
  Pallas kernels: 0 us -> 609 us
  matrix products: 267 us -> 69.7 us
  blocking collectives: 66.9 us -> 0 us
  local copies, waits for them, and re-layouts: 74.4 us -> 29.2 us
  other arithmetic: 66.9 us -> 24.7 us
  starting transfers between devices: 18 us -> 0.62 us
    pallas_call x0 -> x16, Pallas kernels: none -> 609 us  [the longest x11 556 us: transfer(): pl.pallas_call(kernel, out_shape=results, in_specs=[ANY] * (len(operands)...]
    all_gather x10 -> x5, waiting for transfers between devices: 519 us -> 14.8 us  [gather_planes(): return lax.all_gather(x, 'cm', axis=0, tiled=True)]
    reduce_scatter x10 -> x5, waiting for transfers between devices: 438 us -> 20 us  [sum_planes(): return lax.psum_scatter(g, 'cm', scatter_dimension=0, tiled=True)]
    dot_general x21 -> x5, matrix products: 267 us -> 69.7 us  [dot(): lax.dot_general(a, b, (((left,), (right,)), ((), ())), preferred_element_...]
    all_to_all x3 -> x0, blocking collectives: 62 us -> none  [swap_group(): return lax.all_to_all(x, GROUP, 0, 0, tiled=True)]
    reduce_sum x5 -> x3, other arithmetic: 22.6 us -> 0.39 us  [gain_grad(): return sum((jnp.sum(w.astype(F32) * g, -1) for w, g in pairs))]
    convert_element_type x7 -> x0, local copies, waits for them, and re-layouts: 20.2 us -> none  [the longest x6 19.7 us: ff_back(): g.reshape(4, 2, r, nz, fb).transpose(2, 0, 3, 1, 4).reshape(r, 8 * nz * fb)]
    transpose x6 -> x0, local copies, waits for them, and re-layouts: 16.2 us -> none  [the longest x3 11.6 us: rows_of(): x.reshape(nz, 4, 2, r, c).transpose(1, 0, 2, 3, 4).reshape(nz * 8 * r, c)]
  transfers between devices with their start and end apart: 25 -> 10, of which waited for: 19 -> 2; matrix products, arithmetic and copies ran while one was open for 16% -> 13% of each run, Pallas kernels for 0% -> 75%
where the time goes in v3:
time: 789 us; the launch traced here: 784 us
  Pallas kernels  609 us (77%)
  matrix products  69.7 us (9%)
  waiting for transfers between devices  36.3 us (5%)
  local copies, waits for them, and re-layouts  29.2 us (4%)
  other arithmetic  24.7 us (3%)
  between operations  15 us (2%)
    pallas_call x11, Pallas kernels, transfer(): pl.pallas_call(kernel, out_shape=results, in_specs=[ANY] * (len(operands)...  556 us
    dot_general x5, matrix products, dot(): lax.dot_general(a, b, (((left,), (right,)), ((), ())), preferred_element_...  69.7 us
    reduce_scatter x5, waiting for transfers between devices, sum_planes(): return lax.psum_scatter(g, 'cm', scatter_dimension=0, tiled=True)  20 us
  transfers between devices with their start and end apart: 10, of which 2 were waited for; matrix products, arithmetic and copies ran while one was open for 13% of the time, Pallas kernels for 75%

profile of v3, /device:TPU:0, one launch (start us, length us, event | category | flops | bytes accessed | tf_op | source)
XLA Modules:
  0.0 784.4 jit_solution(14792170511984057832)
XLA Ops:
  7.3 1.1 copy.51
  8.4 1.0 reshape.246
  9.4 1.0 reshape.247
  10.4 0.7 pad.4
  11.1 0.7 broadcast_in_dim.10
  11.8 0.9 maximum_bitcast_fusion.refs_0_
  12.7 0.6 broadcast_in_dim.11.refs_1_
  13.4 11.9 %slab_slab1.1 = (bf16[8,64,512]{2,1,0:T(8,128)(2,1)}, s32[8,8,128]{2,1,0:T(8,128)}) custom-call(bf16[8,64,512]{2,1,0:T(8,128)(2,1)} %maximum_bitcast_fusion.refs_0_, s32[8,8,128]{2,1,0:T(8,128)} %broadcast_in_dim.11.refs_1_), custom_call_target="tpu_custom_call" | custom-call | tf_op jit(solution)/shard_map/slab_slab1/pallas_call | solution.py:583
  25.4 1.8 fusion.12
  27.2 20.6 %cols_move2.1 = (bf16[8,64,1024]{2,1,0:T(8,128)(2,1)}, bf16[64,2048]{1,0:T(8,128)(2,1)}) custom-call(bf16[64,8192]{1,0:T(8,128)(2,1)} %get-tuple-element.89.refs_0_, bf16[64,2048]{1,0:T(8,128)(2,1)} %refs_1_.1, bf16[8,64,512]{2,1,0:T(8,128)(2,1)} %get-tuple-element.44.refs_2_), custom_call_target="tpu_custom_call" | custom-call | tf_op jit(solution)/shard_map/cols_move2/pallas_call | solution.py:583
  47.9 0.7 all-gather.10.cloned.1.call-update
  48.7 52.7 %gather_cols3.1 = (bf16[8,256,2048]{2,1,0:T(8,128)(2,1)}, bf16[8,64,1024]{2,1,0:T(8,128)(2,1)}) custom-call(bf16[256,2048]{1,0:T(8,128)(2,1)} %bitcast.86, bf16[64,8192]{1,0:T(8,128)(2,1)} %get-tuple-element.90.refs_1_, bf16[8,64,1024]{2,1,0:T(8,128)(2,1)} %get-tuple-element.45.refs_2_), custom_call_target="tpu_custom_call" | custom-call | tf_op jit(solution)/shard_map/gather_cols3/pallas_call | solution.py:583
  101.5 0.7 slice_reduce_fusion
  102.4 0.5 fusion.20
  103.0 0.2 convert_multiply_fusion.11
  103.2 1.3 copy-done.13
  104.5 1.1 bitcast_convert_fusion.refs_0_
  105.6 1.8 copy.41
  107.4 0.2 convert_reduce_fusion
  107.7 13.6 %project.1 = (bf16[2048,2048]{1,0:T(8,128)(2,1)}, bf16[2048,256]{1,0:T(8,128)(2,1)S(1)}, bf16[2048,128]{1,0:T(8,128)(2,1)S(1)}) custom-call(bf16[2048,2048]{1,0:T(8,128)(2,1)} %bitcast.100, f32[1,2048]{1,0:T(1,128)S(1)} %bitcast.85, bf16[2048,512]{1,0:T(8,128)(2,1)S(1)} %bitcast.76, f32[2,128,128]{2,1,0:T(8,128)S(1)} %get-tuple-element.86.cos_ref, ...), custom_call_target="tpu_custom_call" | custom-call | tf_op jit(solution)/shard_map/project/pallas_call | solution.py:654
  121.3 0.8 copy-done.5
  122.1 84.2 %gather_up_pass4.1 = (bf16[8,256,2048]{2,1,0:T(8,128)(2,1)}, bf16[4,2048,128]{2,1,0:T(8,128)(2,1)}, bf16[256,2048]{1,0:T(8,128)(2,1)}) custom-call(bf16[256,2048]{1,0:T(8,128)(2,1)} %bitcast_convert_fusion.refs_0_, bf16[2048,128]{1,0:T(8,128)(2,1)} %copy-done.5, bf16[256,2048]{1,0:T(8,128)(2,1)} %refs_2_.1), custom_call_target="tpu_custom_call" | custom-call | tf_op jit(solution)/shard_map/gather_up_pass4/pallas_call | solution.py:583
  206.3 0.3 reduce-scatter.6.cloned.1.call-start
  206.6 8.4 %attend.1 = (f32[4,2,256,256]{3,2,1,0:T(8,128)S(1)}, bf16[4,2,2,128,256]{4,3,2,1,0:T(8,128)(2,1)S(1)}, f32[4,2,4,256]{3,2,1,0:T(4,128)S(1)}) custom-call(s32[8]{0:T(128)S(1)} %reshape_squeeze.3.lens, bf16[4,2,2,128,256]{4,3,2,1,0:T(8,128)(2,1)S(1)} %bitcast.80, bf16[4,4,2,2,128,128]{5,4,3,2,1,0:T(8,128)(2,1)} %bitcast.97), custom_call_target="tpu_custom_call" | custom-call | tf_op jit(solution)/shard_map/attend/pallas_call | solution.py:826
  215.0 1.3 copy-done.2
  216.4 7.3 convolution_convert_fusion
  223.7 4.9 copy.42
  228.6 41.2 %sum5.1 = bf16[256,2048]{1,0:T(8,128)(2,1)} custom-call(bf16[8,256,2048]{2,1,0:T(8,128)(2,1)} %bitcast.87, bf16[2048,1024]{1,0:T(8,128)(2,1)} %bitcast.88), custom_call_target="tpu_custom_call" | custom-call | tf_op jit(solution)/shard_map/sum5/pallas_call | solution.py:583
  269.8 1.7 multiply_reduce_fusion.1
  271.5 1.4 fusion.19.refs_0_
  272.9 14.8 %all-gather.12.cloned.1.call-done = bf16[32,64,1024]{2,1,0:T(8,128)(2,1)} async-done(((bf16[8,64,1024]{2,1,0:T(8,128)(2,1)}), bf16[32,64,1024]{2,1,0:T(8,128)(2,1)}) %all-gather.12.cloned.1.call-update) | async-done | bytes 4194320 | tf_op jit(solution)/shard_map/all_gather | solution.py:612
  287.7 4.9 copy.43
  292.6 40.2 %gather6.1 = bf16[8,256,2048]{2,1,0:T(8,128)(2,1)} custom-call(bf16[256,2048]{1,0:T(8,128)(2,1)} %fusion.19.refs_0_, bf16[2048,1024]{1,0:T(8,128)(2,1)} %bitcast.91), custom_call_target="tpu_custom_call" | custom-call | tf_op jit(solution)/shard_map/gather6/pallas_call | solution.py:583
  332.9 13.4 %fusion.27 = f32[2048,1024]{1,0:T(8,128)} fusion(bf16[2048,2048]{1,0:T(8,128)(2,1)} %bitcast.94, bf16[2048,1024]{1,0:T(8,128)(2,1)S(1)} %bitcast.90), kind=kOutput, calls=%fused_computation.72 | convolution fusion | flops 8589934592 | bytes 20971520 | tf_op jit(solution)/shard_map/dot_general | solution.py:616
  346.3 13.2 %multiply_convert_fusion = (bf16[2048,1024]{1,0:T(8,128)(2,1)S(1)}, f32[2048,1024]{1,0:T(8,128)}) fusion(f32[2048,1024]{1,0:T(8,128)} %fusion.27, bf16[2048,2048]{1,0:T(8,128)(2,1)S(1)} %bitcast.96, bf16[2048,1024]{1,0:T(8,128)(2,1)S(1)} %bitcast.93), kind=kOutput, calls=%fused_computation.5 | convolution fusion | flops 8602517504 | bytes 33554432 | tf_op jit(solution)/shard_map/dot_general | solution.py:616
  359.5 2.0 copy-done.19
  361.5 13.2 %convolution_convert_fusion.2.refs_1_ = bf16[1024,2048]{1,0:T(8,128)(2,1)} fusion(bf16[2048,1024]{1,0:T(8,128)(2,1)S(1)} %get-tuple-element.91.refs_3_, bf16[2048,2048]{1,0:T(8,128)(2,1)} %bitcast.115), kind=kOutput, calls=%fused_computation.10 | convolution fusion | flops 8592031744 | bytes 16777216 | tf_op jit(solution)/shard_map/dot_general | solution.py:616
  374.8 22.6 %fusion.2 = (bf16[2048,1024]{1,0:T(8,128)(2,1)}, bf16[2048,1024]{1,0:T(8,128)(2,1)}) fusion(f32[2048,1024]{1,0:T(8,128)} %fusion.27, f32[2048,1024]{1,0:T(8,128)} %get-tuple-element.92, bf16[2048,2048]{1,0:T(8,128)(2,1)} %bitcast.116, bf16[1024,2048]{1,0:T(8,128)(2,1)} %after.1.refs_4_), kind=kOutput, calls=%fused_computation.4 | convolution fusion | flops 8621391872 | bytes 37748736 | tf_op jit(solution)/shard_map/dot_general | solution.py:616
  397.4 70.0 %mlp7.1 = (bf16[256,2048]{1,0:T(8,128)(2,1)}, bf16[2048,1024]{1,0:T(8,128)(2,1)}, bf16[2048,1024]{1,0:T(8,128)(2,1)}) custom-call(bf16[2048,2048]{1,0:T(8,128)(2,1)} %bitcast.95, bf16[2048,1024]{1,0:T(8,128)(2,1)} %get-tuple-element.76.refs_1_, bf16[2048,1024]{1,0:T(8,128)(2,1)} %get-tuple-element.75.refs_2_, bf16[2048,1024]{1,0:T(8,128)(2,1)} %bitcast.89, ...), custom_call_target="tpu_custom_call" | custom-call | tf_op jit(solution)/shard_map/mlp7/pallas_call | solution.py:583
  467.5 0.7 reduce-scatter.10.cloned.1.call-update
  468.2 2.0 fusion.13
  470.4 1.7 fusion.25.refs_0_
  472.1 46.6 %heads_product8.1 = (bf16[2048,256]{1,0:T(8,128)(2,1)}, bf16[256,2048]{1,0:T(8,128)(2,1)}, bf16[2048,2048]{1,0:T(8,128)(2,1)}) custom-call(bf16[256,2048]{1,0:T(8,128)(2,1)} %fusion.25.refs_0_, bf16[256,2048]{1,0:T(8,128)(2,1)} %all-gather.8.cloned.1.call-done.refs_1_, bf16[2048,256]{1,0:T(8,128)(2,1)} %bitcast.79, bf16[2048,1024]{1,0:T(8,128)(2,1)} %copy-done.19, ...), custom_call_target="tpu_custom_call" | custom-call | tf_op jit(solution)/shard_map/heads_product8/pallas_call | solution.py:583
  518.8 1.2 copy-done.3
  520.1 15.6 %attend_back.1 = (f32[4,2,2,128,256]{4,3,2,1,0:T(8,128)S(1)}, bf16[4,4,2,2,128,128]{5,4,3,2,1,0:T(8,128)(2,1)}) custom-call(s32[8]{0:T(128)S(1)} %reshape_squeeze.3.lens, bf16[4,2,2,128,256]{4,3,2,1,0:T(8,128)(2,1)S(1)} %bitcast.81, bf16[4,4,2,2,128,128]{5,4,3,2,1,0:T(8,128)(2,1)} %bitcast.98, bf16[4,2,2,128,256]{4,3,2,1,0:T(8,128)(2,1)S(1)} %bitcast.84, ...), custom_call_target="tpu_custom_call" | custom-call | tf_op jit(solution)/shard_map/attend_back/pallas_call | solution.py:853
  535.7 20.0 %reduce-scatter.8.cloned.1.call-done.refs_2_ = bf16[8,64,1024]{2,1,0:T(8,128)(2,1)} async-done(((bf16[32,64,1024]{2,1,0:T(8,128)(2,1)}), bf16[8,64,1024]{2,1,0:T(8,128)(2,1)}) %reduce-scatter.8.cloned.1.call-update) | async-done | bytes 1048592 | tf_op jit(solution)/shard_map/reduce_scatter | solution.py:608
  555.7 122.9 %down_sum_back9.1 = (bf16[2048,128]{1,0:T(8,128)(2,1)}, bf16[256,2048]{1,0:T(8,128)(2,1)}, bf16[64,8192]{1,0:T(8,128)(2,1)}) custom-call(bf16[4,2048,128]{2,1,0:T(8,128)(2,1)} %bitcast.110, bf16[8,256,2048]{2,1,0:T(8,128)(2,1)} %bitcast.101, bf16[8,64,1024]{2,1,0:T(8,128)(2,1)} %reduce-scatter.8.cloned.1.call-done.refs_2_), custom_call_target="tpu_custom_call" | custom-call | tf_op jit(solution)/shard_map/down_sum_back9/pallas_call | solution.py:583
  678.6 1.0 copy-done.4
  679.7 15.0 %project_back.1 = (bf16[2048,2048]{1,0:T(8,128)(2,1)}, bf16[2048,384]{1,0:T(8,128)(2,1)S(1)}) custom-call(f32[2048,256]{1,0:T(8,128)S(1)} %bitcast.82, bf16[2048,128]{1,0:T(8,128)(2,1)S(1)} %copy-done.4, bf16[2048,2048]{1,0:T(8,128)(2,1)} %get-tuple-element.65.hid_ref, bf16[2048,512]{1,0:T(8,128)(2,1)} %bitcast.77, ...), custom_call_target="tpu_custom_call" | custom-call | tf_op jit(solution)/shard_map/project_back/pallas_call | solution.py:702
  694.7 1.4 copy.44
  696.1 0.3 multiply_reduce_fusion
  696.4 0.9 copy-done.24
  697.3 1.6 convert_element_type.188
  698.9 53.7 %sum_back10.1 = (bf16[256,2048]{1,0:T(8,128)(2,1)}, bf16[64,8192]{1,0:T(8,128)(2,1)}) custom-call(bf16[8,256,2048]{2,1,0:T(8,128)(2,1)} %bitcast.99, bf16[8,64,1024]{2,1,0:T(8,128)(2,1)} %reduce-scatter.10.cloned.1.call-done.refs_1_), custom_call_target="tpu_custom_call" | custom-call | tf_op jit(solution)/shard_map/sum_back10/pallas_call | solution.py:583
  752.6 4.2 convert_multiply_fusion.2
  756.8 0.5 add.119
  757.4 0.6 fusion.6
  758.1 0.3 copy-done.18
  758.4 3.0 fusion.10
  761.4 12.0 %slab_home11.1 = (bf16[8,64,384]{2,1,0:T(8,128)(2,1)}, bf16[64,2048]{1,0:T(8,128)(2,1)}) custom-call(bf16[8,64,384]{2,1,0:T(8,128)(2,1)} %reduce-scatter.12.cloned.1.call-done.refs_0_, bf16[64,2048]{1,0:T(8,128)(2,1)} %reduce-scatter.14.cloned.1.call-done.refs_1_, bf16[256,2048]{1,0:T(8,128)(2,1)} %get-tuple-element.68.refs_2_), custom_call_target="tpu_custom_call" | custom-call | tf_op jit(solution)/shard_map/slab_home11/pallas_call | solution.py:583
  773.5 1.1 convert_bitcast_fusion
  774.8 0.2 multiply_reduce_fusion.2
  776.0 0.8 convert_element_type.185
  776.8 0.5 convert_divide_fusion
  (115 shorter events, 2.3 us)
Async XLA Ops:
  7.2 18.2 %copy-start.37 = (bf16[64]{0:T(256)(128)(2,1)S(1)}, bf16[64]{0:T(256)(128)(2,1)}, u32[]{:S(2)}) copy-start(bf16[64]{0:T(256)(128)(2,1)} %param.20) | copy-start | bytes 388
  7.2 18.2 %copy-start.20 = (bf16[64,8192]{1,0:T(8,128)(2,1)S(1)}, bf16[64,8192]{1,0:T(8,128)(2,1)}, u32[]{:S(2)}) copy-start(bf16[64,8192]{1,0:T(8,128)(2,1)} %param.21) | copy-start | bytes 3145732
  7.2 18.2 %copy-start.22 = (bf16[64,8192]{1,0:T(8,128)(2,1)S(1)}, bf16[64,8192]{1,0:T(8,128)(2,1)}, u32[]{:S(2)}) copy-start(bf16[64,8192]{1,0:T(8,128)(2,1)} %param.22) | copy-start | bytes 3145732
  7.2 98.4 %all-gather.6.cloned.1.call-start = ((), (), s32[]{:S(2)}) async-start(), calls=%async_computation.5 | async-start | bytes 2621440 | tf_op jit(solution)/shard_map/all_gather | solution.py:612
  25.3 191.0 %all-gather.8.cloned.1.call-start = ((), (), s32[]{:S(2)}) async-start(), calls=%async_computation.6 | async-start | bytes 1310720 | tf_op jit(solution)/shard_map/all_gather | solution.py:612
  47.9 175.8 %all-gather.10.cloned.1.call-start = ((), (), s32[]{:S(2)}) async-start(), calls=%async_computation.7 | async-start | bytes 5242880 | tf_op jit(solution)/shard_map/all_gather | solution.py:612
  48.6 239.0 %all-gather.12.cloned.1.call-start = ((), (), s32[]{:S(2)}) async-start(), calls=%async_computation.8 | async-start | bytes 5242880 | tf_op jit(solution)/shard_map/all_gather | solution.py:612
  48.7 53.7 %copy-start.36 = (s32[2]{0:T(128)S(1)}, s32[2]{0:T(128)}, u32[]{:S(2)}) copy-start(s32[2]{0:T(128)} %param.13) | copy-start | bytes 28
  48.7 54.3 %copy-start.28 = (bf16[2,128,2048]{2,1,0:T(8,128)(2,1)S(1)}, bf16[2,128,2048]{2,1,0:T(8,128)(2,1)}, u32[]{:S(2)}) copy-start(bf16[2,128,2048]{2,1,0:T(8,128)(2,1)} %param.14) | copy-start | bytes 3145732
  101.5 273.3 %all-gather.14.cloned.1.call-start = ((), (), s32[]{:S(2)}) async-start(), calls=%async_computation.9 | async-start | bytes 5242880 | tf_op jit(solution)/shard_map/all_gather | solution.py:612
  103.2 1.4 copy-start.13
  107.4 13.8 %copy-start = (bf16[4,4,2,64,512]{4,3,2,0,1:T(8,128)(2,1)}, bf16[4,4,2,64,512]{4,3,2,0,1:T(8,128)(2,1)S(1)}, u32[]{:S(2)}) copy-start(bf16[4,4,2,64,512]{4,3,2,0,1:T(8,128)(2,1)S(1)} %copy.41) | copy-start | bytes 6291460
  121.3 0.8 copy-start.5
  206.3 265.8 %reduce-scatter.6.cloned.1.call-start = ((), (), s32[]{:S(2)}) async-start(), calls=%async_computation.10 | async-start | bytes 5242880 | tf_op jit(solution)/shard_map/reduce_scatter | solution.py:608
  215.0 1.3 copy-start.2
  216.4 7.3 copy-start.1
  228.6 41.2 %copy-start.6 = (bf16[2,128,2048]{2,1,0:T(8,128)(2,1)S(1)}, bf16[2,128,2048]{2,1,0:T(8,128)(2,1)}, u32[]{:S(2)}) copy-start(bf16[2,128,2048]{2,1,0:T(8,128)(2,1)} %param.12) | copy-start | bytes 3145732
  269.8 1.8 copy-start.10
  292.6 40.3 %copy-start.8 = (bf16[4,4,2,64,1024]{4,3,2,0,1:T(8,128)(2,1)S(1)}, bf16[4,4,2,64,1024]{4,3,2,0,1:T(8,128)(2,1)}, u32[]{:S(2)}) copy-start(bf16[4,4,2,64,1024]{4,3,2,0,1:T(8,128)(2,1)} %copy.42) | copy-start | bytes 12582916
  332.9 13.4 %copy-start.9 = (bf16[4,4,2,64,1024]{4,3,2,0,1:T(8,128)(2,1)S(1)}, bf16[4,4,2,64,1024]{4,3,2,0,1:T(8,128)(2,1)}, u32[]{:S(2)}) copy-start(bf16[4,4,2,64,1024]{4,3,2,0,1:T(8,128)(2,1)} %copy.43) | copy-start | bytes 12582916
  332.9 13.4 %copy-start.12 = (bf16[8,256,2048]{2,1,0:T(8,128)(2,1)S(1)}, bf16[8,256,2048]{2,1,0:T(8,128)(2,1)}, u32[]{:S(2)}) copy-start(bf16[8,256,2048]{2,1,0:T(8,128)(2,1)} %gather6.1) | copy-start | bytes 25165828
  359.5 2.0 copy-start.19
  374.7 181.0 %reduce-scatter.8.cloned.1.call-start = ((), (), s32[]{:S(2)}) async-start(), calls=%async_computation.11 | async-start | bytes 5242880 | tf_op jit(solution)/shard_map/reduce_scatter | solution.py:608
  467.4 231.5 %reduce-scatter.10.cloned.1.call-start = ((), (), s32[]{:S(2)}) async-start(), calls=%async_computation.12 | async-start | bytes 5242880 | tf_op jit(solution)/shard_map/reduce_scatter | solution.py:608
  468.2 293.3 %reduce-scatter.14.cloned.1.call-start = ((), (), s32[]{:S(2)}) async-start(), calls=%async_computation.14 | async-start | bytes 1310720 | tf_op jit(solution)/shard_map/reduce_scatter | solution.py:608
  468.2 2.0 copy-start.14
  468.2 2.2 copy-start.17
  518.8 242.7 %reduce-scatter.12.cloned.1.call-start = ((), (), s32[]{:S(2)}) async-start(), calls=%async_computation.13 | async-start | bytes 1966080 | tf_op jit(solution)/shard_map/reduce_scatter | solution.py:608
  518.8 1.3 copy-start.3
  678.6 1.0 copy-start.4
  694.7 1.4 copy-start.7
  696.1 1.2 copy-start.24
  698.9 53.7 %copy-start.21 = (bf16[64,8192]{1,0:T(8,128)(2,1)S(1)}, bf16[64,8192]{1,0:T(8,128)(2,1)}, u32[]{:S(2)}) copy-start(bf16[64,8192]{1,0:T(8,128)(2,1)} %param.21) | copy-start | bytes 3145732
  698.9 53.7 %copy-start.23 = (bf16[64,8192]{1,0:T(8,128)(2,1)S(1)}, bf16[64,8192]{1,0:T(8,128)(2,1)}, u32[]{:S(2)}) copy-start(bf16[64,8192]{1,0:T(8,128)(2,1)} %param.22) | copy-start | bytes 3145732
  698.9 53.7 %copy-start.27 = (bf16[64,8192]{1,0:T(8,128)(2,1)S(1)}, bf16[64,8192]{1,0:T(8,128)(2,1)}, u32[]{:S(2)}) copy-start(bf16[64,8192]{1,0:T(8,128)(2,1)} %get-tuple-element.74) | copy-start | bytes 3145732
  752.6 4.8 copy-start.16
  752.6 5.4 copy-start.15
  752.6 5.4 copy-start.26
  756.8 1.2 copy-start.11
  756.8 1.5 copy-start.18
  773.4 1.4 copy-start.29
  774.6 0.8 copy-start.33
  774.7 1.1 copy-start.34
  774.8 1.2 copy-start.32
  774.8 2.5 copy-start.25
  774.8 2.0 copy-start.35
  775.4 1.9 copy-start.30
  775.8 1.5 copy-start.31
Sparse Core Ops, SparseCore 0:
  25.5 49.4 all-gather.5
  76.5 26.5 all-gather.7
  104.7 87.5 all-gather.9
  193.6 94.0 all-gather.11
  289.1 79.2 all-gather.13
  374.8 87.4 reduce-scatter.5
  467.5 88.1 reduce-scatter.7
  558.0 110.3 reduce-scatter.9
  670.8 27.8 reduce-scatter.13
  700.9 33.9 reduce-scatter.11

commit v4 on v3

--- a/solution.py
+++ b/solution.py
@@ -105,14 +105,16 @@
     )
 
 
-def gather_steps(x_ref, o_ref, local, ss, rs):
+def gather_steps(x_ref, o_ref, local, ss, rs, ready=None):
+    ready = ready or (lambda i: None)
     a, core, cl = places()
     half = x_ref.shape[0] // 2
-    lo, hi = pl.ds(0, half), pl.ds(half, half)
+    lo, hi, both = pl.ds(0, half), pl.ds(half, half), pl.ds(0, 2 * half)
     me = index_of(a, core, cl)
     sx = index_of(1 - a, core, cl)
     sy = index_of(a, core, 1 - cl)
     sd = index_of(1 - a, core, 1 - cl)
+    other = 2 - 4 * core
     mine = pltpu.make_async_copy(x_ref, o_ref.at[me], local.at[0])
 
     def put(i, slot, part, name, src=None):
@@ -124,12 +126,14 @@
         put(1, me, hi, "cl", x_ref.at[hi]),
         put(2, me, hi, "a", x_ref.at[hi]),
         put(3, me, lo, "cl", x_ref.at[lo]),
-        put(4, me, pl.ds(0, 2 * half), "core", x_ref),
+        put(4, me, both, "core", x_ref),
     ]
     for c in sent:
         c.start()
     mine.start()
     yield
+    mine.wait()
+    ready(me)
 
     def on(i, slot, part, name):
         c = put(i, slot, part, name)
@@ -142,24 +146,33 @@
     put(1, sy, hi, "cl").wait_recv()
     on(7, sy, hi, "a")
     on(8, sy, hi, "core")
+    put(4, me + other, both, "core").wait_recv()
+    ready(me + other)
     yield
     put(2, sx, hi, "a").wait_recv()
     on(9, sx, hi, "core")
     put(3, sy, lo, "cl").wait_recv()
     on(10, sy, lo, "core")
-    yield
+    ready(sx)
+    ready(sy)
+    yield
+    for i, slot, part in ((6, sx, lo), (9, sx, hi)):
+        put(i, slot + other, part, "core").wait_recv()
+    ready(sx + other)
     put(5, sd, lo, "cl").wait_recv()
     on(11, sd, lo, "core")
     put(7, sd, hi, "a").wait_recv()
     on(12, sd, hi, "core")
     yield
-    other = 2 - 4 * core
-    put(4, me + other, pl.ds(0, 2 * half), "core").wait_recv()
-    for i, slot, part in ((6, sx, lo), (8, sy, hi), (9, sx, hi), (10, sy, lo), (11, sd, lo), (12, sd, hi)):
+    for i, slot, part in ((8, sy, hi), (10, sy, lo)):
         put(i, slot + other, part, "core").wait_recv()
+    ready(sy + other)
+    ready(sd)
+    for i, slot, part in ((11, sd, lo), (12, sd, hi)):
+        put(i, slot + other, part, "core").wait_recv()
+    ready(sd + other)
     for c in sent:
         c.wait_send()
-    mine.wait()
 
 
 def add_rows(dst, sources, n):
@@ -341,23 +354,27 @@
 
     for j in range(nz):
         pl.when(z >= j)(lambda j=j: load(j).start())
-    yield
-    for j in range(nz):
-
-        @pl.when(z >= j)
+
+    @pl.when(z == nz - 1)
+    def _():
+        for j in range(nz):
+            load(j).wait()
+            if j < nz - 1:
+                send(j).start()
+
+    yield
+    yield
+    yield
+    for j in range(nz - 1):
+
+        @pl.when(jnp.logical_and(z >= j, z < nz - 1))
         def _(j=j):
             load(j).wait()
-
-            @pl.when(z < nz - 1)
-            def _():
-                send(j).wait_recv()
-                add_rows(mine.at[j], (mine.at[j], came.at[j]), rows)
-
-            @pl.when(z > j)
-            def _():
-                send(j).start()
-
-        yield
+            send(j).wait_recv()
+            add_rows(mine.at[j], (mine.at[j], came.at[j]), rows)
+            pl.when(z > j)(send(j).start)
+
+    yield
     done = pltpu.make_async_copy(mine.at[z], o_ref, lsem.at[nz])
     done.start()
     for j in range(nz):
@@ -365,23 +382,30 @@
     done.wait()
 
 
-def back_steps(nz, r, hid_ref, one_ref, two_ref, wone_ref, wtwo_ref, o_ref, out_one, out_two, *scratch):
-    hid, g, w, out, stage, theirs, first, last, gsem, osem, lsem, cs, cr, ss, rs = scratch
+def row_loads(nz, src, dst, sems):
+    run = dst.shape[0] // (4 * nz)
+    copies = []
+    for c in range(4 * nz):
+        at = (c % nz * 4 + c // nz) * run
+        copies.append(pltpu.make_async_copy(src.at[pl.ds(at, run)], dst.at[pl.ds(c * run, run)], sems.at[c]))
+    return copies
+
+
+def back_steps(nz, r, hid_ref, one_ref, two_ref, wone_ref, wtwo_ref, o_ref, out_ref, *scratch):
+    hid, g, w, out, stage, theirs, first, last, gsem, wsem, osem, lsem, cs, cr, ss, rs = scratch
     tiles, _, wide = hid.shape
     run = 2 * r
     per = wide // run
     core = lax.axis_index("core")
     rows, width = theirs.shape[1:]
-    loads = [
-        pltpu.make_async_copy(src, dst, gsem.at[n])
-        for n, (src, dst) in enumerate(
-            [(wone_ref, w.at[0]), (one_ref, g.at[0]), (wtwo_ref, w.at[1]), (two_ref, g.at[1])]
-            + [(hid_ref.at[:, pl.ds(i * wide, wide)], hid.at[i]) for i in range(tiles)]
-        )
+    loads = [pltpu.make_async_copy(one_ref, g.at[0], gsem.at[0]), pltpu.make_async_copy(two_ref, g.at[1], gsem.at[1])]
+    loads += row_loads(nz, wone_ref, w.at[0], wsem.at[0]) + row_loads(nz, wtwo_ref, w.at[1], wsem.at[1])
+    later = [
+        pltpu.make_async_copy(hid_ref.at[:, pl.ds(i * wide, wide)], hid.at[i], gsem.at[2 + i]) for i in range(tiles)
     ]
+    for c in loads + later:
+        c.start()
     for c in loads:
-        c.start()
-    for c in loads[:4]:
         c.wait()
 
     @pl.loop(0, 8)
@@ -404,38 +428,92 @@
             remote(stage.at[0, p], theirs.at[p], cs.at[p], cr.at[p], "core").start()
 
     out_core = {p: remote(stage.at[0, p], theirs.at[p], cs.at[p], cr.at[p], "core") for p in range(4)}
-    for c in loads[4:]:
+    for c in later:
         c.wait()
 
-    def store(k, i, p):
+    def store(i, p):
         chunk = i * per + p
         at = (lax.rem(chunk, nz) * 4 + chunk // nz) * run
-        target = (out_one, out_two)[k]
         return pltpu.make_async_copy(
-            out.at[k, i, pl.ds(p * run, run)], target.at[pl.ds(pl.multiple_of(at, run), run)], osem.at[k, i, p]
+            out.at[i, pl.ds(p * run, run)], out_ref.at[pl.ds(pl.multiple_of(at, run), run)], osem.at[i, p]
         )
 
-    def products(k, lo, hi):
+    def products(lo, hi):
         @pl.loop(lo, hi)
         def _(i):
-            out[k, i] = dot(hid[i], g[k], 0, 0).astype(BF)
+            out[i] = dot(hid[i], g[0], 0, 0).astype(BF)
             for p in range(per):
-                store(k, i, p).start()
+                store(i, p).start()
 
     summing = sum_rest(o_ref, stage.at[1], theirs, first, last, lsem, out_core, {}, ss, rs)
-    half = tiles // 2
-    for k, lo, hi in ((1, 0, half), (1, half, tiles), (0, 0, half), (0, half, tiles)):
+    for n in range(4):
         next(summing, None)
-        products(k, lo, hi)
+        products(n * tiles // 4, (n + 1) * tiles // 4)
     for _ in summing:
         pass
-    for k in range(2):
-
-        @pl.loop(0, tiles)
-        def _(i, k=k):
-            for p in range(per):
-                store(k, i, p).wait()
-
+
+    @pl.loop(0, tiles)
+    def _(i):
+        for p in range(per):
+            store(i, p).wait()
+
+    yield
+
+
+def forward_steps(nz, x_ref, wone_ref, wtwo_ref, low_ref, all_ref, gate_ref, up_ref, in_ref, *rest):
+    g_refs, scratch = rest[:2], rest[2:]
+    buf, w, low, inner, stage, out, wsem, asem, gsem, osem, local, ss, rs = scratch
+    rows = buf.shape[1]
+    loads = row_loads(nz, wone_ref, w.at[0], wsem.at[0]) + row_loads(nz, wtwo_ref, w.at[1], wsem.at[1])
+    load_low = pltpu.make_async_copy(low_ref, low, osem.at[0])
+    done = []
+
+    def keep(src, dst, sem):
+        done.append(pltpu.make_async_copy(src, dst, sem))
+        done[-1].start()
+
+    def ready(i):
+        n = len(done) // 4
+        if n == 0:
+            for c in loads:
+                c.wait()
+        block = buf[i]
+        part = pl.ds(pl.multiple_of(i * rows, rows), rows)
+        gate = dot(block, w[0])
+        up = dot(block, w[1])
+        stage[n, 0] = gate
+        stage[n, 1] = up
+        inner[part, :] = (gate * jax.nn.sigmoid(gate) * up).astype(BF)
+        keep(buf.at[i], all_ref.at[i], asem.at[n])
+        keep(stage.at[n, 0], gate_ref.at[part], gsem.at[n, 0])
+        keep(stage.at[n, 1], up_ref.at[part], gsem.at[n, 1])
+        keep(inner.at[part], in_ref.at[part], gsem.at[n, 2])
+
+    first = gather_steps(x_ref, buf, local, ss, rs, ready)
+    next(first)
+    for c in (*loads, load_low):
+        c.start()
+    for _ in first:
+        pass
+    load_low.wait()
+    tiles, wide, width = out.shape
+    half = width // 2
+
+    def store(t, n):
+        return pltpu.make_async_copy(
+            out.at[t, :, pl.ds(n * half, half)], g_refs[n].at[pl.ds(t * wide, wide)], osem.at[1 + t * 2 + n]
+        )
+
+    for t in range(tiles):
+        left = inner[:, t * wide : (t + 1) * wide]
+        for n in range(2):
+            out[t, :, n * half : (n + 1) * half] = dot(left, low[:, n * half : (n + 1) * half], 0, 0).astype(BF)
+            store(t, n).start()
+    for t in range(tiles):
+        for n in range(2):
+            store(t, n).wait()
+    for c in done:
+        c.wait()
     yield
 
 
@@ -521,12 +599,22 @@
         wide = 256
         tiles = width // wide
         block = rows // 8
-        scratch = [vmem(tiles, rows, wide), vmem(2, rows, cols), vmem(2, width, cols), vmem(2, tiles, wide, cols)]
+        scratch = [vmem(tiles, rows, wide), vmem(2, rows, cols), vmem(2, width, cols), vmem(tiles, wide, cols)]
         scratch += [vmem(2, 4, block, width), vmem(4, block, width), vmem(4, block // 2, width)]
-        scratch += [vmem(2, block // 2, width), dma(4 + tiles), dma(2, tiles, wide // (2 * r))]
+        scratch += [vmem(2, block // 2, width), dma(2 + tiles), dma(2, 4 * nz), dma(tiles, wide // (2 * r))]
         scratch += [dma(5), dma(4), dma(4), dma(6), dma(6)]
-        outs = [like(block, width), like(width, cols), like(width, cols)]
-        return kind, functools.partial(back_steps, nz, r), xs, outs, scratch
+        return kind, functools.partial(back_steps, nz, r), xs, [like(block, width), like(width, cols)], scratch
+    if kind == "forward":
+        rows, width = x.shape
+        cols = xs[1].shape[1]
+        wide = min(256, cols)
+        tiles = cols // wide
+        full = [jax.ShapeDtypeStruct((8 * rows, cols), F32)] * 2
+        outs = [like(8, rows, width), *full, like(8 * rows, cols), *[like(cols, width // 2)] * 2]
+        scratch = [vmem(8, rows, width), vmem(2, width, cols), vmem(8 * rows, width), vmem(8 * rows, cols)]
+        scratch += [pltpu.VMEM((8, 2, rows, cols), F32), vmem(tiles, wide, width)]
+        scratch += [dma(2, 4 * nz), dma(8), dma(8, 3), dma(1 + 2 * tiles), dma(1), dma(13), dma(13)]
+        return kind, functools.partial(forward_steps, nz), xs, outs, scratch
     if kind == "product":
         rows, cols = x.shape[0], xs[1].shape[1]
         scratch = [vmem(*x.shape), vmem(*xs[1].shape), vmem(8, rows // 8, cols), dma(2), dma(8)]
@@ -587,7 +675,7 @@
         out_specs=[ANY] * len(results),
         scratch_shapes=[s for p in parts for s in p[4]],
         compiler_params=pltpu.CompilerParams(
-            collective_id=cid, has_side_effects=True, vmem_limit_bytes=56 * MIB
+            collective_id=cid, has_side_effects=True, vmem_limit_bytes=60 * MIB
         ),
         name="_".join(kinds) + str(cid),
     )(*operands, *deps)
@@ -668,7 +756,8 @@
     )(x, gain, w, cos, sin)
 
 
-def project_back_kernel(dq_ref, dkv_ref, hid_ref, w_ref, cos_ref, sin_ref, e_ref, g_ref, total):
+def project_back_kernel(dq_ref, dkv_ref, hid_ref, w_ref, cos_ref, sin_ref, *rest):
+    e_ref, g_ref, total = rest[-3:]
     step = pl.program_id(0)
 
     @pl.when(step == 0)
@@ -693,7 +782,7 @@
         g_ref[...] = total[...].astype(BF)
 
 
-def project_back(dq, dkv, hid, w, cos, sin):
+def project_back(dq, dkv, hid, w, cos, sin, deps):
     rows, width = hid.shape
     step = rows // 8
     shape = (width, dq.shape[1] + 2 * HD)
@@ -710,12 +799,75 @@
             pl.BlockSpec(shape, lambda g: (0, 0)),
             table,
             table,
-        ],
+        ]
+        + [ANY] * len(deps),
         out_specs=[pl.BlockSpec((step, width), lambda g: (g, 0)), pl.BlockSpec(shape, lambda g: (0, 0))],
         scratch_shapes=[pltpu.VMEM(shape, F32)],
         compiler_params=pltpu.CompilerParams(vmem_limit_bytes=48 * MIB),
         name="project_back",
-    )(dq, dkv, hid, w, cos, sin)
+    )(dq, dkv, hid, w, cos, sin, *deps)
+
+
+def inner_back_kernel(nz, r, low_ref, gate_ref, up_ref, wd_ref, hid_ref, gg_ref, gu_ref, out_ref, hid, gu, sems):
+    step = pl.program_id(0)
+    tiles, _, wide = hid.shape
+    loads = [
+        pltpu.make_async_copy(hid_ref.at[:, pl.ds(i * wide, wide)], hid.at[i], sems.at[i]) for i in range(tiles)
+    ]
+
+    @pl.when(step == 0)
+    def _():
+        for c in loads:
+            c.start()
+
+    inner = dot(low_ref[...], wd_ref[...], 1, 1).astype(BF).astype(F32)
+    gate = gate_ref[...]
+    sig = jax.nn.sigmoid(gate)
+    act = gate * sig
+    gg_ref[...] = (inner * up_ref[...] * (sig * (1.0 + gate * (1.0 - sig)))).astype(BF)
+    up = (inner * act).astype(BF)
+    gu_ref[...] = up
+    rows = up.shape[0]
+    gu[pl.ds(pl.multiple_of(step * rows, rows), rows), :] = up
+
+    @pl.when(step == pl.num_programs(0) - 1)
+    def _():
+        for c in loads:
+            c.wait()
+        run = 2 * r
+        per = wide // run
+
+        @pl.loop(0, tiles)
+        def _(i):
+            product = dot(hid[i], gu[...], 0, 0).astype(BF)
+            for p in range(per):
+                chunk = i * per + p
+                at = (lax.rem(chunk, nz) * 4 + chunk // nz) * run
+                out_ref[pl.ds(pl.multiple_of(at, run), run), :] = product[p * run : (p + 1) * run]
+
+
+def inner_back(low, gate, up, wd, hid):
+    nz = lax.axis_size("cm")
+    rows, width = low.shape
+    cols = gate.shape[1]
+    step = rows // 8
+    wide = 256
+    tiles = width // wide
+    block = lambda c: pl.BlockSpec((step, c), lambda g: (g, 0))
+    return pl.pallas_call(
+        functools.partial(inner_back_kernel, nz, width // (8 * nz)),
+        grid=(8,),
+        out_shape=[
+            jax.ShapeDtypeStruct((rows, cols), BF),
+            jax.ShapeDtypeStruct((rows, cols), BF),
+            jax.ShapeDtypeStruct((width, cols), BF),
+        ],
+        in_specs=[block(width), block(cols), block(cols), pl.BlockSpec(wd.shape, lambda g: (0, 0)), ANY],
+        out_specs=[block(cols), block(cols), pl.BlockSpec((width, cols), lambda g: (0, 0))],
+        scratch_shapes=[pltpu.VMEM((tiles, rows, wide), BF), pltpu.VMEM((rows, cols), BF), dma(tiles)],
+        compiler_params=pltpu.CompilerParams(vmem_limit_bytes=60 * MIB),
+        name="inner_back",
+    )(low, gate, up, wd, hid)
 
 
 def flat(ref):
@@ -770,7 +922,8 @@
     log_ref[0, 0] = top[...] + jnp.log(sums[...])
 
 
-def attend_back_kernel(lens, q_ref, kv_ref, do_ref, att_ref, log_ref, dq_ref, dkv_ref, acc):
+def attend_back_kernel(lens, q_ref, kv_ref, do_ref, att_ref, log_ref, *rest):
+    dq_ref, dkv_ref, acc = rest[-3:]
     z = lax.axis_index("cm")
     n = lens[pl.program_id(0) * pl.num_programs(1) + pl.program_id(1)]
     q = flat(q_ref)
@@ -845,7 +998,7 @@
     return att, low.reshape(rows, wide), log
 
 
-def attend_back(lens, q, kv, do, att, log, seqs, block):
+def attend_back(lens, q, kv, do, att, log, seqs, block, deps):
     nz, rows, _ = kv.shape
     wide = q.shape[1]
     own, every, turned, logs = attention_specs(seqs, block, wide, nz)
@@ -857,12 +1010,12 @@
             jax.ShapeDtypeStruct((*view, wide), F32),
             jax.ShapeDtypeStruct((nz, *view, 2 * HD), BF),
         ],
-        in_specs=[pl.BlockSpec(memory_space=pltpu.SMEM), own, every, own, turned, logs],
+        in_specs=[pl.BlockSpec(memory_space=pltpu.SMEM), own, every, own, turned, logs] + [ANY] * len(deps),
         out_specs=[own, every],
         scratch_shapes=[pltpu.VMEM((wide, 2 * block), F32)],
         compiler_params=pltpu.CompilerParams(vmem_limit_bytes=48 * MIB),
         name="attend_back",
-    )(lens, q.reshape(*view, wide), kv.reshape(nz, *view, 2 * HD), do.reshape(*view, wide), att, log)
+    )(lens, q.reshape(*view, wide), kv.reshape(nz, *view, 2 * HD), do.reshape(*view, wide), att, log, *deps)
     return dq.reshape(rows, wide), dkv.reshape(nz, rows, 2 * HD)
 
 
@@ -917,7 +1070,7 @@
     tok_all, wu = transfer(3, [part("gather", own), part("cols", gained(w_up), pieces=pieces)], (wg,))
     pack = rows_of(pack)
     gain_row = pack[:, wide + 2 * HD].astype(F32)[None]
-    wg = rows_of(wg)
+    wg = gather_planes(wg).reshape(width, -1)
     wo = gather_planes(wo)
 
     slot = cm * 2 * block + jnp.arange(2 * block, dtype=jnp.int32).reshape(2, block)
@@ -926,55 +1079,51 @@
     own_pos = cm * 2 * block + cl * block + jnp.arange(block, dtype=jnp.int32)
     valid = (own_pos[None, :] < lengths[:, None]).astype(F32)
     grad_out = (cotangent.astype(F32) * valid[..., None]).reshape(rows, width)
-    grad_low, kv_all, down = transfer(
+    grad_low, kv_all = transfer(
         4,
         [
             part("gather", grad_out.astype(BF)),
             part("up", kv),
-            part("pass", w_down),
         ],
     )
     grad_low = grad_low.reshape(8 * rows, width)
-    wu = rows_of(wu)
+    wu = gather_planes(wu).reshape(width, -1)
     att, att_low, log = attend(lens, q, kv_all, seqs, block)
 
     resid_in = own.astype(F32)
-    (mid,) = transfer(5, [part("sum", dot(att_low, wo).astype(BF))], (wg,))
+    mid, down = transfer(5, [part("sum", dot(att_low, wo).astype(BF)), part("pass", w_down)], (wg,))
     wd = gather_planes(down if pieces > 1 else lax.ppermute(down, ("cm", "cl"), perm))
     resid_mid = resid_in + mid.astype(F32)
     scale_two = rms_scale(resid_mid)
     normed_two = resid_mid * scale_two
-    (hidden_two,) = transfer(6, [part("gather", normed_two.astype(BF))], (wu,))
+    hidden_two, gate_pre, up_pre, inner, wd_left, wd_right = transfer(
+        6, [part("forward", normed_two.astype(BF), wg, wu, grad_low)]
+    )
     hidden_two = hidden_two.reshape(8 * rows, width)
-    gate_pre = dot(hidden_two, wg)
-    up_pre = dot(hidden_two, wu)
-    sig = jax.nn.sigmoid(gate_pre)
-    act = gate_pre * sig
-    inner = (act * up_pre).astype(BF)
-    grad_wd = dot(inner, grad_low, 0, 0).astype(BF)
-    wd = after(wd, (grad_wd,))
-    grad_inner = dot(grad_low, wd, 1, 1).astype(BF).astype(F32)
-    grad_gate = (grad_inner * up_pre * (sig * (1.0 + gate_pre * (1.0 - sig)))).astype(BF)
-    grad_up = (grad_inner * act).astype(BF)
-    e_two, grad_wg, grad_wu = transfer(7, [part("mlp", hidden_two, grad_gate, grad_up, wg, wu)])
+    wd = after(wd, (wd_left,))
+    grad_gate, grad_up, grad_wu = inner_back(grad_low, gate_pre, up_pre, wd, hidden_two)
+    e_two, grad_wg = transfer(7, [part("mlp", hidden_two, grad_gate, grad_up, wg, wu)], (grad_wu,))
     by_owner = lambda g: sum_planes(g.reshape(8 * nz, r, -1))
-    grad_wd, grad_wu, grad_wg = sum_planes(grad_wd), by_owner(grad_wu), by_owner(grad_wg)
+    wd_left, grad_wu, grad_wg = sum_planes(wd_left), by_owner(grad_wu), by_owner(grad_wg)
     grad_mid = grad_out + norm_back(e_two.astype(F32), normed_two, scale_two)
     grad_heads, grad_wo, out_part = transfer(
-        8, [part("heads", grad_mid.astype(BF), wo, att_low), part("product", inner, wd)], (grad_wd,)
+        8, [part("heads", grad_mid.astype(BF), wo, att_low), part("product", inner, wd)], (wd_left,)
     )
-    dq, dkv = attend_back(lens, q, kv_all, grad_heads, att, log, seqs, block)
+    dq, dkv = attend_back(lens, q, kv_all, grad_heads, att, log, seqs, block, (grad_wu,))
     dkv, out_sum, grad_wu = transfer(
         9, [part("down", dkv), part("sum", out_part), part("back", grad_wu, pieces=pieces)]
     )
+    wd_right = after(wd_right, (dkv,))
     layer_out = (resid_mid + out_sum.astype(F32)).astype(BF)
-    e_one, grad_qkv = project_back(dq, dkv, hidden_one, pack, cos, sin)
+    e_one, grad_qkv = project_back(dq, dkv, hidden_one, pack, cos, sin, (wd_right,))
+    wd_right = sum_planes(wd_right)
     e_one, grad_wg = transfer(10, [part("sum", e_one), part("back", grad_wg, pieces=pieces)])
     grad_wo = sum_planes(grad_wo)
     grad_qkv = sum_planes(rows_first(grad_qkv))
     scale_one = rms_scale(resid_in)
     grad_tokens = grad_mid + norm_back(e_one.astype(F32) * gain_row, resid_in * scale_one, scale_one)
     grad_qkv, grad_wo = transfer(11, [part("slab", grad_qkv), part("home", grad_wo)], (e_one,))
+    grad_wd = jnp.concatenate([wd_left, wd_right], 1)
     if pieces == 1:
         grad_wd = lax.ppermute(grad_wd, ("cm", "cl"), home)
     grad_qkv = grad_qkv.transpose(1, 0, 2).astype(F32)

time: 789 us -> 757 us (0.959)
  matrix products: 69.7 us -> 7.23 us
  waiting for transfers between devices: 36.3 us -> 87.1 us
  Pallas kernels: 609 us -> 591 us
  local copies, waits for them, and re-layouts: 29.2 us -> 18.1 us
    all_gather x5, waiting for transfers between devices: 14.8 us -> 79.4 us  [gather_planes(): return lax.all_gather(x, 'cm', axis=0, tiled=True)]
    dot_general x5 -> x1, matrix products: 69.7 us -> 7.23 us  [dot(): lax.dot_general(a, b, (((left,), (right,)), ((), ())), preferred_element_...]
    pallas_call x11, Pallas kernels: 556 us -> 505 us  [transfer(): pl.pallas_call(kernel, out_shape=results, in_specs=[ANY] * (len(operands)...]
    pallas_call x0 -> x1, Pallas kernels: none -> 33.3 us  [inner_back(): pl.pallas_call(functools.partial(inner_back_kernel, nz, width // (8 * nz)...]
    reduce_scatter x5 -> x6, waiting for transfers between devices: 20 us -> 6.15 us  [sum_planes(): return lax.psum_scatter(g, 'cm', scatter_dimension=0, tiled=True)]
    reshape x3 -> x1, local copies, waits for them, and re-layouts: 11.6 us -> 1.8 us  [rows_of(): x.reshape(nz, 4, 2, r, c).transpose(1, 0, 2, 3, 4).reshape(nz * 8 * r, c)]
  transfers between devices with their start and end apart: 10 -> 11, of which waited for: 2 -> 4; matrix products, arithmetic and copies ran while one was open for 13% -> 5% of each run, Pallas kernels for 75% -> 78%
where the time goes in v4:
time: 757 us; the launch traced here: 746 us
  Pallas kernels  591 us (78%)
  waiting for transfers between devices  87.1 us (12%)
  other arithmetic  25.9 us (3%)
  local copies, waits for them, and re-layouts  18.1 us (2%)
  between operations  14.9 us (2%)
    pallas_call x11, Pallas kernels, transfer(): pl.pallas_call(kernel, out_shape=results, in_specs=[ANY] * (len(operands)...  505 us
    all_gather x5, waiting for transfers between devices, gather_planes(): return lax.all_gather(x, 'cm', axis=0, tiled=True)  79.4 us
    pallas_call x1, Pallas kernels, inner_back(): pl.pallas_call(functools.partial(inner_back_kernel, nz, width // (8 * nz)...  33.3 us
    pallas_call x1, Pallas kernels, attend_back(): pl.pallas_call(attend_back_kernel, grid=(4, seqs), out_shape=[jax.ShapeDt...  15.6 us
  transfers between devices with their start and end apart: 11, of which 4 were waited for; matrix products, arithmetic and copies ran while one was open for 5% of the time, Pallas kernels for 78%

profile of v4, /device:TPU:0, one launch (start us, length us, event | category | flops | bytes accessed | tf_op | source)
XLA Modules:
  0.0 745.7 jit_solution(4494151936779212861)
XLA Ops:
  7.3 1.1 copy.46
  8.4 1.0 reshape.240
  9.4 1.0 reshape.241
  10.4 0.7 pad.4
  11.1 0.7 broadcast_in_dim.10
  11.8 0.9 maximum_bitcast_fusion.refs_0_
  12.7 0.6 broadcast_in_dim.11.refs_1_
  13.4 11.9 %slab_slab1.1 = (bf16[8,64,512]{2,1,0:T(8,128)(2,1)}, s32[8,8,128]{2,1,0:T(8,128)}) custom-call(bf16[8,64,512]{2,1,0:T(8,128)(2,1)} %maximum_bitcast_fusion.refs_0_, s32[8,8,128]{2,1,0:T(8,128)} %broadcast_in_dim.11.refs_1_), custom_call_target="tpu_custom_call" | custom-call | tf_op jit(solution)/shard_map/slab_slab1/pallas_call | solution.py:671
  25.4 1.8 fusion.8
  27.2 20.6 %cols_move2.1 = (bf16[8,64,1024]{2,1,0:T(8,128)(2,1)}, bf16[64,2048]{1,0:T(8,128)(2,1)}) custom-call(bf16[64,8192]{1,0:T(8,128)(2,1)} %get-tuple-element.105.refs_0_, bf16[64,2048]{1,0:T(8,128)(2,1)} %refs_1_.2, bf16[8,64,512]{2,1,0:T(8,128)(2,1)} %get-tuple-element.53.refs_2_), custom_call_target="tpu_custom_call" | custom-call | tf_op jit(solution)/shard_map/cols_move2/pallas_call | solution.py:671
  47.9 0.7 all-gather.10.cloned.1.call-update
  48.7 52.8 %gather_cols3.1 = (bf16[8,256,2048]{2,1,0:T(8,128)(2,1)}, bf16[8,64,1024]{2,1,0:T(8,128)(2,1)}) custom-call(bf16[256,2048]{1,0:T(8,128)(2,1)} %bitcast.72, bf16[64,8192]{1,0:T(8,128)(2,1)} %get-tuple-element.106.refs_1_, bf16[8,64,1024]{2,1,0:T(8,128)(2,1)} %get-tuple-element.54.refs_2_), custom_call_target="tpu_custom_call" | custom-call | tf_op jit(solution)/shard_map/gather_cols3/pallas_call | solution.py:671
  101.6 0.7 slice_reduce_fusion
  102.5 0.5 fusion.16
  103.1 0.2 convert_multiply_fusion.9
  103.3 1.3 copy-done.9
  104.6 1.1 bitcast_convert_fusion.refs_0_
  105.7 1.8 copy.38
  107.5 0.2 convert_reduce_fusion
  107.7 13.6 %project.1 = (bf16[2048,2048]{1,0:T(8,128)(2,1)}, bf16[2048,256]{1,0:T(8,128)(2,1)S(1)}, bf16[2048,128]{1,0:T(8,128)(2,1)S(1)}) custom-call(bf16[2048,2048]{1,0:T(8,128)(2,1)} %bitcast.85, f32[1,2048]{1,0:T(1,128)S(1)} %bitcast.71, bf16[2048,512]{1,0:T(8,128)(2,1)S(1)} %bitcast.62, f32[2,128,128]{2,1,0:T(8,128)S(1)} %get-tuple-element.102.cos_ref, ...), custom_call_target="tpu_custom_call" | custom-call | tf_op jit(solution)/shard_map/project/pallas_call | solution.py:742
  121.3 0.8 copy-done.6
  122.1 52.4 %gather_up4.1 = (bf16[8,256,2048]{2,1,0:T(8,128)(2,1)}, bf16[4,2048,128]{2,1,0:T(8,128)(2,1)}) custom-call(bf16[256,2048]{1,0:T(8,128)(2,1)} %bitcast_convert_fusion.refs_0_, bf16[2048,128]{1,0:T(8,128)(2,1)} %copy-done.6), custom_call_target="tpu_custom_call" | custom-call | tf_op jit(solution)/shard_map/gather_up4/pallas_call | solution.py:671
  174.4 8.4 %attend.1 = (f32[4,2,256,256]{3,2,1,0:T(8,128)S(1)}, bf16[4,2,2,128,256]{4,3,2,1,0:T(8,128)(2,1)S(1)}, f32[4,2,4,256]{3,2,1,0:T(4,128)S(1)}) custom-call(s32[8]{0:T(128)S(1)} %reshape_squeeze.3.lens, bf16[4,2,2,128,256]{4,3,2,1,0:T(8,128)(2,1)S(1)} %bitcast.66, bf16[4,4,2,2,128,128]{5,4,3,2,1,0:T(8,128)(2,1)} %bitcast.87), custom_call_target="tpu_custom_call" | custom-call | tf_op jit(solution)/shard_map/attend/pallas_call | solution.py:979
  182.9 1.3 copy-done.3
  184.2 7.2 convolution_convert_fusion
  191.4 0.8 all-gather.10.cloned.1.call-done
  192.2 41.9 %sum_pass5.1 = (bf16[256,2048]{1,0:T(8,128)(2,1)}, bf16[256,2048]{1,0:T(8,128)(2,1)}) custom-call(bf16[8,256,2048]{2,1,0:T(8,128)(2,1)} %bitcast.73, bf16[256,2048]{1,0:T(8,128)(2,1)} %refs_1_.3, bf16[2048,1024]{1,0:T(8,128)(2,1)} %bitcast.74), custom_call_target="tpu_custom_call" | custom-call | tf_op jit(solution)/shard_map/sum_pass5/pallas_call | solution.py:671
  234.1 0.5 reduce-scatter.7.cloned.1.call-start
  234.7 1.6 multiply_reduce_fusion.1
  236.3 1.4 fusion.15.refs_0_
  237.7 50.0 %all-gather.12.cloned.1.call-done = bf16[32,64,1024]{2,1,0:T(8,128)(2,1)} async-done(((bf16[8,64,1024]{2,1,0:T(8,128)(2,1)}), bf16[32,64,1024]{2,1,0:T(8,128)(2,1)}) %all-gather.12.cloned.1.call-update) | async-done | bytes 4194320 | tf_op jit(solution)/shard_map/all_gather | solution.py:700
  287.7 55.1 %forward6.1 = (bf16[8,256,2048]{2,1,0:T(8,128)(2,1)}, f32[2048,1024]{1,0:T(8,128)}, f32[2048,1024]{1,0:T(8,128)}, bf16[2048,1024]{1,0:T(8,128)(2,1)}, bf16[1024,...) custom-call(bf16[256,2048]{1,0:T(8,128)(2,1)} %fusion.15.refs_0_, bf16[2048,1024]{1,0:T(8,128)(2,1)} %bitcast.75, ...), custom_call_target="tpu_custom_call" | custom-call | tf_op jit(solution)/shard_map/forward6/pallas_call | solution.py:671
  342.8 28.6 %all-gather.14.cloned.1.call-done.refs_0_ = bf16[1024,2048]{1,0:T(8,128)(2,1)} async-done(((bf16[256,2048]{1,0:T(8,128)(2,1)}), bf16[1024,2048]{1,0:T(8,128)(2,1)}) %all-gather.14.cloned.1.call-update) | async-done | bytes 4194320 | tf_op jit(solution)/shard_map/all_gather | solution.py:700
  371.5 33.3 %inner_back.1 = (bf16[2048,1024]{1,0:T(8,128)(2,1)}, bf16[2048,1024]{1,0:T(8,128)(2,1)}, bf16[2048,1024]{1,0:T(8,128)(2,1)}) custom-call(bf16[2048,2048]{1,0:T(8,128)(2,1)} %bitcast.80, f32[2048,1024]{1,0:T(8,128)} %get-tuple-element.65.gate_ref, f32[2048,1024]{1,0:T(8,128)} %get-tuple-element.66.up_ref, bf16[1024,2048]{1,0:T(8,128)(2,1)} %after.2.wd_ref.refs_4_, ...), custom_call_target="tpu_custom_call" | custom-call | tf_op jit(solution)/shard_map/inner_back/pallas_call | solution.py:857
  404.8 0.3 reduce-scatter.11.cloned.1.call-start
  405.1 69.8 %mlp7.1 = (bf16[256,2048]{1,0:T(8,128)(2,1)}, bf16[2048,1024]{1,0:T(8,128)(2,1)}) custom-call(bf16[2048,2048]{1,0:T(8,128)(2,1)} %bitcast.78, bf16[2048,1024]{1,0:T(8,128)(2,1)} %get-tuple-element.69.refs_1_, bf16[2048,1024]{1,0:T(8,128)(2,1)} %get-tuple-element.70.refs_2_, bf16[2048,1024]{1,0:T(8,128)(2,1)} %bitcast.76, bf16[2048,1024]{1,0:T(8,128)(2,1)} %bitcast.82, ...), custom_call_target="tpu_custom_call" | custom-call | tf_op jit(solution)/shard_map/mlp7/pallas_call | solution.py:671
  474.9 2.0 fusion.9
  477.1 1.7 fusion.21.refs_0_
  478.8 46.6 %heads_product8.1 = (bf16[2048,256]{1,0:T(8,128)(2,1)}, bf16[256,2048]{1,0:T(8,128)(2,1)}, bf16[2048,2048]{1,0:T(8,128)(2,1)}) custom-call(bf16[256,2048]{1,0:T(8,128)(2,1)} %fusion.21.refs_0_, bf16[256,2048]{1,0:T(8,128)(2,1)} %all-gather.8.cloned.1.call-done.refs_1_, bf16[2048,256]{1,0:T(8,128)(2,1)} %bitcast.65, ...), custom_call_target="tpu_custom_call" | custom-call | tf_op jit(solution)/shard_map/heads_product8/pallas_call | solution.py:671
  525.5 0.3 reduce-scatter.13.cloned.1.call-start
  525.8 1.2 copy-done.2
  527.0 1.2 copy-done.5
  528.2 15.6 %attend_back.1 = (f32[4,2,2,128,256]{4,3,2,1,0:T(8,128)S(1)}, bf16[4,4,2,2,128,128]{5,4,3,2,1,0:T(8,128)(2,1)}) custom-call(s32[8]{0:T(128)S(1)} %reshape_squeeze.3.lens, bf16[4,2,2,128,256]{4,3,2,1,0:T(8,128)(2,1)S(1)} %bitcast.67, bf16[4,4,2,2,128,128]{5,4,3,2,1,0:T(8,128)(2,1)} %bitcast.88, bf16[4,2,2,128,256]{4,3,2,1,0:T(8,128)(2,1)S(1)} %bitcast.70, ...), custom_call_target="tpu_custom_call" | custom-call | tf_op jit(solution)/shard_map/attend_back/pallas_call | solution.py:1006
  543.8 91.0 %down_sum_back9.1 = (bf16[2048,128]{1,0:T(8,128)(2,1)}, bf16[256,2048]{1,0:T(8,128)(2,1)}, bf16[64,8192]{1,0:T(8,128)(2,1)}) custom-call(bf16[4,2048,128]{2,1,0:T(8,128)(2,1)} %bitcast.94, bf16[8,256,2048]{2,1,0:T(8,128)(2,1)} %bitcast.86, bf16[8,64,1024]{2,1,0:T(8,128)(2,1)} %reduce-scatter.9.cloned.1.call-done.rest_0_.refs_2_), custom_call_target="tpu_custom_call" | custom-call | tf_op jit(solution)/shard_map/down_sum_back9/pallas_call | solution.py:671
  634.9 1.0 copy-done.4
  635.9 15.0 %project_back.1 = (bf16[2048,2048]{1,0:T(8,128)(2,1)}, bf16[2048,384]{1,0:T(8,128)(2,1)S(1)}) custom-call(f32[2048,256]{1,0:T(8,128)S(1)} %bitcast.68, bf16[2048,128]{1,0:T(8,128)(2,1)S(1)} %copy-done.4, bf16[2048,2048]{1,0:T(8,128)(2,1)} %get-tuple-element.82.hid_ref, bf16[2048,512]{1,0:T(8,128)(2,1)} %bitcast.63, ...), custom_call_target="tpu_custom_call" | custom-call | tf_op jit(solution)/shard_map/project_back/pallas_call | solution.py:791
  650.9 1.4 copy.39
  652.4 0.7 reduce-scatter.17.cloned.1.call-update
  653.1 0.5 copy-done.8
  653.5 0.3 multiply_reduce_fusion
  653.9 50.8 %sum_back10.1 = (bf16[256,2048]{1,0:T(8,128)(2,1)}, bf16[64,8192]{1,0:T(8,128)(2,1)}) custom-call(bf16[8,256,2048]{2,1,0:T(8,128)(2,1)} %bitcast.84, bf16[8,64,1024]{2,1,0:T(8,128)(2,1)} %reduce-scatter.11.cloned.1.call-done.refs_1_), custom_call_target="tpu_custom_call" | custom-call | tf_op jit(solution)/shard_map/sum_back10/pallas_call | solution.py:671
  704.8 4.5 convert_multiply_fusion
  709.3 0.5 add.113
  709.9 0.6 fusion.2
  710.5 0.5 copy-done.11
  710.9 3.0 fusion.6
  713.9 12.3 %slab_home11.1 = (bf16[8,64,384]{2,1,0:T(8,128)(2,1)}, bf16[64,2048]{1,0:T(8,128)(2,1)}) custom-call(bf16[8,64,384]{2,1,0:T(8,128)(2,1)} %reduce-scatter.13.cloned.1.call-done.refs_0_, bf16[64,2048]{1,0:T(8,128)(2,1)} %reduce-scatter.15.cloned.1.call-done.refs_1_, bf16[256,2048]{1,0:T(8,128)(2,1)} %get-tuple-element.86.refs_2_), custom_call_target="tpu_custom_call" | custom-call | tf_op jit(solution)/shard_map/slab_home11/pallas_call | solution.py:671
  726.2 1.1 convert_bitcast_fusion
  727.6 0.2 copy.42
  727.9 0.2 copy.41
  728.3 0.8 convert_element_type.161
  729.5 0.5 convert_divide_fusion
  730.0 6.1 reduce-scatter.17.cloned.1.call-done
  736.1 2.6 maximum_convert_fusion
  (106 shorter events, 2.0 us)
Async XLA Ops:
  7.2 18.2 %copy-start.33 = (bf16[64]{0:T(256)(128)(2,1)S(1)}, bf16[64]{0:T(256)(128)(2,1)}, u32[]{:S(2)}) copy-start(bf16[64]{0:T(256)(128)(2,1)} %param.20) | copy-start | bytes 388
  7.2 18.2 %copy-start.17 = (bf16[64,8192]{1,0:T(8,128)(2,1)S(1)}, bf16[64,8192]{1,0:T(8,128)(2,1)}, u32[]{:S(2)}) copy-start(bf16[64,8192]{1,0:T(8,128)(2,1)} %param.21) | copy-start | bytes 3145732
  7.2 18.2 %copy-start.19 = (bf16[64,8192]{1,0:T(8,128)(2,1)S(1)}, bf16[64,8192]{1,0:T(8,128)(2,1)}, u32[]{:S(2)}) copy-start(bf16[64,8192]{1,0:T(8,128)(2,1)} %param.22) | copy-start | bytes 3145732
  7.2 98.5 %all-gather.6.cloned.1.call-start = ((), (), s32[]{:S(2)}) async-start(), calls=%async_computation.6 | async-start | bytes 2621440 | tf_op jit(solution)/shard_map/all_gather | solution.py:700
  25.3 158.8 %all-gather.8.cloned.1.call-start = ((), (), s32[]{:S(2)}) async-start(), calls=%async_computation.7 | async-start | bytes 1310720 | tf_op jit(solution)/shard_map/all_gather | solution.py:700
  47.9 144.3 %all-gather.10.cloned.1.call-start = ((), (), s32[]{:S(2)}) async-start(), calls=%async_computation.8 | async-start | bytes 5242880 | tf_op jit(solution)/shard_map/all_gather | solution.py:700
  48.6 239.0 %all-gather.12.cloned.1.call-start = ((), (), s32[]{:S(2)}) async-start(), calls=%async_computation.9 | async-start | bytes 5242880 | tf_op jit(solution)/shard_map/all_gather | solution.py:700
  48.7 53.7 %copy-start.32 = (s32[2]{0:T(128)S(1)}, s32[2]{0:T(128)}, u32[]{:S(2)}) copy-start(s32[2]{0:T(128)} %param.13) | copy-start | bytes 28
  48.7 54.3 %copy-start.24 = (bf16[2,128,2048]{2,1,0:T(8,128)(2,1)S(1)}, bf16[2,128,2048]{2,1,0:T(8,128)(2,1)}, u32[]{:S(2)}) copy-start(bf16[2,128,2048]{2,1,0:T(8,128)(2,1)} %param.14) | copy-start | bytes 3145732
  101.5 269.9 %all-gather.14.cloned.1.call-start = ((), (), s32[]{:S(2)}) async-start(), calls=%async_computation.10 | async-start | bytes 5242880 | tf_op jit(solution)/shard_map/all_gather | solution.py:700
  103.3 1.3 copy-start.9
  107.5 13.8 %copy-start = (bf16[4,4,2,64,512]{4,3,2,0,1:T(8,128)(2,1)}, bf16[4,4,2,64,512]{4,3,2,0,1:T(8,128)(2,1)S(1)}, u32[]{:S(2)}) copy-start(bf16[4,4,2,64,512]{4,3,2,0,1:T(8,128)(2,1)S(1)} %copy.38) | copy-start | bytes 6291460
  121.3 0.8 copy-start.6
  182.9 1.3 copy-start.3
  184.2 7.2 copy-start.1
  192.2 42.4 %copy-start.7 = (bf16[2,128,2048]{2,1,0:T(8,128)(2,1)S(1)}, bf16[2,128,2048]{2,1,0:T(8,128)(2,1)}, u32[]{:S(2)}) copy-start(bf16[2,128,2048]{2,1,0:T(8,128)(2,1)} %param.12) | copy-start | bytes 3145732
  234.1 2.2 copy-start.12
  234.1 244.6 %reduce-scatter.7.cloned.1.call-start = ((), (), s32[]{:S(2)}) async-start(), calls=%async_computation.11 | async-start | bytes 2621440 | tf_op jit(solution)/shard_map/reduce_scatter | solution.py:696
  342.8 183.0 %reduce-scatter.9.cloned.1.call-start = ((), (), s32[]{:S(2)}) async-start(), calls=%async_computation.12 | async-start | bytes 5242880 | tf_op jit(solution)/shard_map/reduce_scatter | solution.py:696
  404.8 249.0 %reduce-scatter.11.cloned.1.call-start = ((), (), s32[]{:S(2)}) async-start(), calls=%async_computation.13 | async-start | bytes 5242880 | tf_op jit(solution)/shard_map/reduce_scatter | solution.py:696
  474.9 239.1 %reduce-scatter.15.cloned.1.call-start = ((), (), s32[]{:S(2)}) async-start(), calls=%async_computation.15 | async-start | bytes 1310720 | tf_op jit(solution)/shard_map/reduce_scatter | solution.py:696
  474.9 2.0 copy-start.10
  474.9 2.2 copy-start.15
  525.5 188.5 %reduce-scatter.13.cloned.1.call-start = ((), (), s32[]{:S(2)}) async-start(), calls=%async_computation.14 | async-start | bytes 1966080 | tf_op jit(solution)/shard_map/reduce_scatter | solution.py:696
  525.8 1.2 copy-start.2
  527.0 1.2 copy-start.5
  634.9 1.0 copy-start.4
  652.3 1.2 copy-start.8
  652.3 83.8 %reduce-scatter.17.cloned.1.call-start = ((), (), s32[]{:S(2)}) async-start(), calls=%async_computation.16 | async-start | bytes 2621440 | tf_op jit(solution)/shard_map/reduce_scatter | solution.py:696
  653.9 50.9 %copy-start.18 = (bf16[64,8192]{1,0:T(8,128)(2,1)S(1)}, bf16[64,8192]{1,0:T(8,128)(2,1)}, u32[]{:S(2)}) copy-start(bf16[64,8192]{1,0:T(8,128)(2,1)} %param.21) | copy-start | bytes 3145732
  653.9 50.9 %copy-start.20 = (bf16[64,8192]{1,0:T(8,128)(2,1)S(1)}, bf16[64,8192]{1,0:T(8,128)(2,1)}, u32[]{:S(2)}) copy-start(bf16[64,8192]{1,0:T(8,128)(2,1)} %param.22) | copy-start | bytes 3145732
  704.7 5.1 copy-start.14
  704.8 5.7 copy-start.13
  704.8 5.7 copy-start.16
  704.8 5.7 copy-start.23
  709.3 1.6 copy-start.11
  727.3 1.0 copy-start.28
  727.4 2.1 copy-start.22
  727.4 1.7 copy-start.29
  727.4 1.8 copy-start.30
  727.4 1.9 copy-start.25
  727.6 1.9 copy-start.31
  727.6 8.6 %copy-start.21 = (bf16[256,1024]{1,0:T(8,128)(2,1)S(1)}, bf16[256,1024]{1,0:T(8,128)(2,1)}, u32[]{:S(2)}) copy-start(bf16[256,1024]{1,0:T(8,128)(2,1)} %reduce-scatter.7.cloned.1.call-done.refs_5_) | copy-start | bytes 1572868
  727.9 10.9 %copy-start.26 = (f32[64,512]{1,0:T(8,128)}, f32[64,512]{1,0:T(8,128)S(1)}, u32[]{:S(2)}) copy-start(f32[64,512]{1,0:T(8,128)S(1)} %reshape.269) | copy-start | bytes 393220
  728.1 10.6 %copy-start.27 = (f32[64,512]{1,0:T(8,128)}, f32[64,512]{1,0:T(8,128)S(1)}, u32[]{:S(2)}) copy-start(f32[64,512]{1,0:T(8,128)S(1)} %reshape.268) | copy-start | bytes 393220
Sparse Core Ops, SparseCore 0:
  25.5 49.4 all-gather.5
  76.5 26.5 all-gather.7
  104.7 87.5 all-gather.9
  193.6 94.0 all-gather.11
  289.1 82.3 all-gather.13
  373.6 42.3 reduce-scatter.6
  418.4 76.0 reduce-scatter.8
  496.8 77.2 reduce-scatter.10
  576.5 43.6 reduce-scatter.14
  652.5 32.9 reduce-scatter.12
  687.7 48.3 reduce-scatter.16

commit v5 on v4

--- a/solution.py
+++ b/solution.py
@@ -203,12 +203,14 @@
     yield from sum_rest(o_ref, mine, theirs, first, last, lsem, out, loc, ss, rs)
 
 
-def sum_rest(o_ref, mine, theirs, first, last, lsem, out, loc, ss, rs):
+def sum_rest(o_ref, mine, theirs, first, last, lsem, out, loc, ss, rs, make=None):
     rows = mine.shape[1]
     half = rows // 2
     lo, hi = pl.ds(0, half), pl.ds(half, half)
 
     def chip_sum(p):
+        if make is not None:
+            make(p)
         out[p].wait_recv()
         if p in loc:
             loc[p].wait()
@@ -355,16 +357,17 @@
     for j in range(nz):
         pl.when(z >= j)(lambda j=j: load(j).start())
 
-    @pl.when(z == nz - 1)
-    def _():
-        for j in range(nz):
-            load(j).wait()
-            if j < nz - 1:
-                send(j).start()
-
-    yield
-    yield
-    yield
+    ends = [0, 1, 2, nz]
+    for first, end in zip(ends, ends[1:]):
+
+        @pl.when(z == nz - 1)
+        def _(first=first, end=end):
+            for j in range(first, end):
+                load(j).wait()
+                if j < nz - 1:
+                    send(j).start()
+
+        yield
     for j in range(nz - 1):
 
         @pl.when(jnp.logical_and(z >= j, z < nz - 1))
@@ -408,28 +411,24 @@
     for c in loads:
         c.wait()
 
-    @pl.loop(0, 8)
-    def _(n):
-        to = jnp.where(n < 4, 1 - core, core)
-        turn = lax.rem(n, 4)
-        a, _, cl = places()
-        far_a = jnp.where(jnp.logical_or(turn == 0, turn == 1), 1 - a, a)
-        far_cl = jnp.where(jnp.logical_or(turn == 0, turn == 2), 1 - cl, cl)
-        p = jnp.where(turn == 0, 3, jnp.where(turn == 3, 0, turn))
-        first_row = pl.multiple_of(index_of(far_a, to, far_cl) * rows, rows)
-        for c in range(0, width, width // 2):
-            part = pl.ds(c, width // 2)
-            e = dot(g[0, pl.ds(first_row, rows), :], w[0, part, :], 1, 1)
-            e += dot(g[1, pl.ds(first_row, rows), :], w[1, part, :], 1, 1)
-            stage[n // 4, p, :, part] = e.astype(BF)
-
-        @pl.when(n < 4)
-        def _():
-            remote(stage.at[0, p], theirs.at[p], cs.at[p], cr.at[p], "core").start()
+    def blocks(p):
+        ca, cc = plane_chips()[p]
+
+        @pl.loop(0, 2)
+        def _(n):
+            to = jnp.where(n == 0, 1 - core, core)
+            first_row = pl.multiple_of(index_of(ca, to, cc) * rows, rows)
+            for c in range(0, width, width // 2):
+                part = pl.ds(c, width // 2)
+                e = dot(g[0, pl.ds(first_row, rows), :], w[0, part, :], 1, 1)
+                e += dot(g[1, pl.ds(first_row, rows), :], w[1, part, :], 1, 1)
+                stage[n, p, :, part] = e.astype(BF)
+
+            @pl.when(n == 0)
+            def _():
+                out_core[p].start()
 
     out_core = {p: remote(stage.at[0, p], theirs.at[p], cs.at[p], cr.at[p], "core") for p in range(4)}
-    for c in later:
-        c.wait()
 
     def store(i, p):
         chunk = i * per + p
@@ -445,9 +444,12 @@
             for p in range(per):
                 store(i, p).start()
 
-    summing = sum_rest(o_ref, stage.at[1], theirs, first, last, lsem, out_core, {}, ss, rs)
+    summing = sum_rest(o_ref, stage.at[1], theirs, first, last, lsem, out_core, {}, ss, rs, blocks)
     for n in range(4):
         next(summing, None)
+        if n == 0:
+            for c in later:
+                c.wait()
         products(n * tiles // 4, (n + 1) * tiles // 4)
     for _ in summing:
         pass
@@ -517,9 +519,14 @@
     yield
 
 
-def product_steps(a_ref, b_ref, o_ref, a, b, out, lsem, osem):
+def product_steps(a_ref, left_ref, right_ref, o_ref, a, b, out, lsem, osem):
+    half = b.shape[1] // 2
     tiles, rows, _ = out.shape
-    loads = [pltpu.make_async_copy(a_ref, a, lsem.at[0]), pltpu.make_async_copy(b_ref, b, lsem.at[1])]
+    loads = [
+        pltpu.make_async_copy(a_ref, a, lsem.at[0]),
+        pltpu.make_async_copy(left_ref, b.at[:, pl.ds(0, left_ref.shape[1])], lsem.at[1]),
+        pltpu.make_async_copy(right_ref, b.at[:, pl.ds(left_ref.shape[1], right_ref.shape[1])], lsem.at[2]),
+    ]
     for c in loads:
         c.start()
     for c in loads:
@@ -528,7 +535,6 @@
     def store(i):
         return pltpu.make_async_copy(out.at[i], o_ref.at[pl.ds(pl.multiple_of(i * rows, rows), rows)], osem.at[i])
 
-    half = b.shape[1] // 2
     for lo, hi in ((0, tiles // 2), (tiles // 2, tiles)):
 
         @pl.loop(lo, hi)
@@ -549,19 +555,21 @@
     loads = [pltpu.make_async_copy(wo_ref, wo, lsem.at[0]), pltpu.make_async_copy(low_ref, low, lsem.at[1])]
     for c in loads:
         c.start()
-    yield from gather_steps(x_ref, buf, local, ss, rs)
-    for c in loads:
-        c.wait()
-    total[...] = jnp.zeros_like(total)
     rows = buf.shape[1]
-
-    @pl.loop(0, 8)
-    def _(i):
+    seen_blocks = []
+
+    def ready(i):
+        if not seen_blocks:
+            for c in loads:
+                c.wait()
+            total[...] = jnp.zeros_like(total)
+        seen_blocks.append(i)
         block = buf[i]
         part = pl.ds(pl.multiple_of(i * rows, rows), rows)
         heads[part, :] = dot(block, wo[...], 1, 1).astype(BF)
         total[...] += dot(low[part, :], block, 0, 0)
 
+    yield from gather_steps(x_ref, buf, local, ss, rs, ready)
     g[...] = total[...].astype(BF)
     stores = [pltpu.make_async_copy(heads, heads_ref, lsem.at[2]), pltpu.make_async_copy(g, g_ref, lsem.at[3])]
     for c in stores:
@@ -616,8 +624,8 @@
         scratch += [dma(2, 4 * nz), dma(8), dma(8, 3), dma(1 + 2 * tiles), dma(1), dma(13), dma(13)]
         return kind, functools.partial(forward_steps, nz), xs, outs, scratch
     if kind == "product":
-        rows, cols = x.shape[0], xs[1].shape[1]
-        scratch = [vmem(*x.shape), vmem(*xs[1].shape), vmem(8, rows // 8, cols), dma(2), dma(8)]
+        rows, cols = x.shape[0], xs[1].shape[1] + xs[2].shape[1]
+        scratch = [vmem(*x.shape), vmem(x.shape[1], cols), vmem(8, rows // 8, cols), dma(3), dma(8)]
         return kind, product_steps, xs, [like(rows, cols)], scratch
     if kind == "heads":
         rows, cols = x.shape
@@ -808,7 +816,7 @@
     )(dq, dkv, hid, w, cos, sin, *deps)
 
 
-def inner_back_kernel(nz, r, low_ref, gate_ref, up_ref, wd_ref, hid_ref, gg_ref, gu_ref, out_ref, hid, gu, sems):
+def inner_back_kernel(nz, r, low_ref, gate_ref, up_ref, wl_ref, wr_ref, hid_ref, gg_ref, gu_ref, out_ref, hid, gu, sems):
     step = pl.program_id(0)
     tiles, _, wide = hid.shape
     loads = [
@@ -820,7 +828,9 @@
         for c in loads:
             c.start()
 
-    inner = dot(low_ref[...], wd_ref[...], 1, 1).astype(BF).astype(F32)
+    half = wl_ref.shape[1]
+    inner = dot(low_ref[:, :half], wl_ref[...], 1, 1) + dot(low_ref[:, half:], wr_ref[...], 1, 1)
+    inner = inner.astype(BF).astype(F32)
     gate = gate_ref[...]
     sig = jax.nn.sigmoid(gate)
     act = gate * sig
@@ -846,7 +856,7 @@
                 out_ref[pl.ds(pl.multiple_of(at, run), run), :] = product[p * run : (p + 1) * run]
 
 
-def inner_back(low, gate, up, wd, hid):
+def inner_back(low, gate, up, wl, wr, hid):
     nz = lax.axis_size("cm")
     rows, width = low.shape
     cols = gate.shape[1]
@@ -862,12 +872,12 @@
             jax.ShapeDtypeStruct((rows, cols), BF),
             jax.ShapeDtypeStruct((width, cols), BF),
         ],
-        in_specs=[block(width), block(cols), block(cols), pl.BlockSpec(wd.shape, lambda g: (0, 0)), ANY],
+        in_specs=[block(width), block(cols), block(cols)] + [pl.BlockSpec(w.shape, lambda g: (0, 0)) for w in (wl, wr)] + [ANY],
         out_specs=[block(cols), block(cols), pl.BlockSpec((width, cols), lambda g: (0, 0))],
         scratch_shapes=[pltpu.VMEM((tiles, rows, wide), BF), pltpu.VMEM((rows, cols), BF), dma(tiles)],
         compiler_params=pltpu.CompilerParams(vmem_limit_bytes=60 * MIB),
         name="inner_back",
-    )(low, gate, up, wd, hid)
+    )(low, gate, up, wl, wr, hid)
 
 
 def flat(ref):
@@ -1027,13 +1037,6 @@
     return scale_rows * (grad_normed - normed * jnp.mean(grad_normed * normed, -1, keepdims=True))
 
 
-def rows_of(x):
-    nz = lax.axis_size("cm")
-    _, r, c = x.shape
-    x = gather_planes(x)
-    return x.reshape(nz, 4, 2, r, c).transpose(1, 0, 2, 3, 4).reshape(nz * 8 * r, c)
-
-
 def rows_first(g):
     nz = lax.axis_size("cm")
     rows, c = g.shape
@@ -1059,6 +1062,8 @@
     def gained(w):
         return (w.astype(F32) * gain_two).astype(BF)
 
+    down = w_down if pieces > 1 else lax.ppermute(w_down, ("cm", "cl"), perm)
+    wd_one = gather_planes(down[:, : width // 4])
     pack = [w.reshape(r, 8, -1) for w in (w_query, w_key, w_value)]
     pack.append(jnp.broadcast_to(attn_gain[:, None, None], (r, 8, 2 * HD)))
     pack = jnp.concatenate(pack, -1).transpose(1, 0, 2)
@@ -1067,8 +1072,10 @@
     lens = lens[::2, 0, :seqs].reshape(-1)
     wg, wo = transfer(2, [part("cols", gained(w_gate), pieces=pieces), part("move", w_out)], (pack,))
     own = tokens.reshape(rows, width)
-    tok_all, wu = transfer(3, [part("gather", own), part("cols", gained(w_up), pieces=pieces)], (wg,))
-    pack = rows_of(pack)
+    tok_all, wu = transfer(
+        3, [part("gather", own), part("cols", gained(w_up), pieces=pieces)], (wg, wd_one)
+    )
+    pack = gather_planes(pack).reshape(nz, 4, 2 * r, -1).transpose(1, 0, 2, 3).reshape(width, -1)
     gain_row = pack[:, wide + 2 * HD].astype(F32)[None]
     wg = gather_planes(wg).reshape(width, -1)
     wo = gather_planes(wo)
@@ -1091,8 +1098,8 @@
     att, att_low, log = attend(lens, q, kv_all, seqs, block)
 
     resid_in = own.astype(F32)
-    mid, down = transfer(5, [part("sum", dot(att_low, wo).astype(BF)), part("pass", w_down)], (wg,))
-    wd = gather_planes(down if pieces > 1 else lax.ppermute(down, ("cm", "cl"), perm))
+    mid, down = transfer(5, [part("sum", dot(att_low, wo).astype(BF)), part("pass", down[:, width // 4 :])], (wg,))
+    wd_two = gather_planes(down)
     resid_mid = resid_in + mid.astype(F32)
     scale_two = rms_scale(resid_mid)
     normed_two = resid_mid * scale_two
@@ -1100,14 +1107,14 @@
         6, [part("forward", normed_two.astype(BF), wg, wu, grad_low)]
     )
     hidden_two = hidden_two.reshape(8 * rows, width)
-    wd = after(wd, (wd_left,))
-    grad_gate, grad_up, grad_wu = inner_back(grad_low, gate_pre, up_pre, wd, hidden_two)
+    wd_two = after(wd_two, (wd_left,))
+    grad_gate, grad_up, grad_wu = inner_back(grad_low, gate_pre, up_pre, wd_one, wd_two, hidden_two)
     e_two, grad_wg = transfer(7, [part("mlp", hidden_two, grad_gate, grad_up, wg, wu)], (grad_wu,))
     by_owner = lambda g: sum_planes(g.reshape(8 * nz, r, -1))
     wd_left, grad_wu, grad_wg = sum_planes(wd_left), by_owner(grad_wu), by_owner(grad_wg)
     grad_mid = grad_out + norm_back(e_two.astype(F32), normed_two, scale_two)
     grad_heads, grad_wo, out_part = transfer(
-        8, [part("heads", grad_mid.astype(BF), wo, att_low), part("product", inner, wd)], (wd_left,)
+        8, [part("heads", grad_mid.astype(BF), wo, att_low), part("product", inner, wd_one, wd_two)], (wd_left,)
     )
     dq, dkv = attend_back(lens, q, kv_all, grad_heads, att, log, seqs, block, (grad_wu,))
     dkv, out_sum, grad_wu = transfer(

time: 757 us -> 735 us (0.971)
  Pallas kernels: 591 us -> 564 us
    pallas_call x11, Pallas kernels: 505 us -> 478 us  [transfer(): pl.pallas_call(kernel, out_shape=results, in_specs=[ANY] * (len(operands)...]
    reduce_scatter x6, waiting for transfers between devices: 6.15 us -> 17.2 us  [sum_planes(): return lax.psum_scatter(g, 'cm', scatter_dimension=0, tiled=True)]
    all_gather x5 -> x6, waiting for transfers between devices: 79.4 us -> 71.9 us  [gather_planes(): return lax.all_gather(x, 'cm', axis=0, tiled=True)]
  transfers between devices with their start and end apart: 11 -> 12, of which waited for: 4 -> 4; matrix products, arithmetic and copies ran while one was open for 5% -> 6% of each run, Pallas kernels for 78% -> 78%
where the time goes in v5:
time: 735 us; the launch traced here: 723 us
  Pallas kernels  564 us (77%)
  waiting for transfers between devices  90.4 us (12%)
  other arithmetic  26 us (4%)
  local copies, waits for them, and re-layouts  19.6 us (3%)
  between operations  15.3 us (2%)
    pallas_call x11, Pallas kernels, transfer(): pl.pallas_call(kernel, out_shape=results, in_specs=[ANY] * (len(operands)...  478 us
    all_gather x6, waiting for transfers between devices, gather_planes(): return lax.all_gather(x, 'cm', axis=0, tiled=True)  71.9 us
    pallas_call x1, Pallas kernels, inner_back(): pl.pallas_call(functools.partial(inner_back_kernel, nz, width // (8 * nz)...  33.5 us
    reduce_scatter x6, waiting for transfers between devices, sum_planes(): return lax.psum_scatter(g, 'cm', scatter_dimension=0, tiled=True)  17.2 us
    pallas_call x1, Pallas kernels, attend_back(): pl.pallas_call(attend_back_kernel, grid=(4, seqs), out_shape=[jax.ShapeDt...  15.6 us
    pallas_call x1, Pallas kernels, project_back(): pl.pallas_call(project_back_kernel, grid=(8,), out_shape=[jax.ShapeDtypeS...  15 us
  transfers between devices with their start and end apart: 12, of which 4 were waited for; matrix products, arithmetic and copies ran while one was open for 6% of the time, Pallas kernels for 78%

profile of v5, /device:TPU:0, one launch (start us, length us, event | category | flops | bytes accessed | tf_op | source)
XLA Modules:
  0.0 723.2 jit_solution(10206293821365979337)
XLA Ops:
  7.2 1.7 slice.22
  9.0 1.1 copy.46
  10.1 1.0 reshape.240
  11.1 1.0 reshape.241
  12.3 0.9 maximum_bitcast_fusion.refs_0_
  13.2 0.6 broadcast_in_dim.11.refs_1_
  13.8 11.9 %slab_slab1.1 = (bf16[8,64,512]{2,1,0:T(8,128)(2,1)}, s32[8,8,128]{2,1,0:T(8,128)}) custom-call(bf16[8,64,512]{2,1,0:T(8,128)(2,1)} %maximum_bitcast_fusion.refs_0_, s32[8,8,128]{2,1,0:T(8,128)} %broadcast_in_dim.11.refs_1_), custom_call_target="tpu_custom_call" | custom-call | tf_op jit(solution)/shard_map/slab_slab1/pallas_call | solution.py:679
  25.9 1.8 fusion.8
  27.7 20.6 %cols_move2.1 = (bf16[8,64,1024]{2,1,0:T(8,128)(2,1)}, bf16[64,2048]{1,0:T(8,128)(2,1)}) custom-call(bf16[64,8192]{1,0:T(8,128)(2,1)} %get-tuple-element.105.refs_0_, bf16[64,2048]{1,0:T(8,128)(2,1)} %refs_1_.1, bf16[8,64,512]{2,1,0:T(8,128)(2,1)} %get-tuple-element.53.refs_2_), custom_call_target="tpu_custom_call" | custom-call | tf_op jit(solution)/shard_map/cols_move2/pallas_call | solution.py:679
  48.4 0.5 all-gather.13.cloned.1.call-update
  49.0 52.7 %gather_cols3.1 = (bf16[8,256,2048]{2,1,0:T(8,128)(2,1)}, bf16[8,64,1024]{2,1,0:T(8,128)(2,1)}) custom-call(bf16[256,2048]{1,0:T(8,128)(2,1)} %bitcast.72, bf16[64,8192]{1,0:T(8,128)(2,1)} %get-tuple-element.106.refs_1_, bf16[8,64,1024]{2,1,0:T(8,128)(2,1)} %get-tuple-element.54.refs_2_, bf16[1024,512]{1,0:T(8,128)(2,1)} %all-gather.7.cloned.1.call-done.refs_3_.wl_ref.refs_4_), custom_call_target="tpu_custom_call" | custom-call | tf_op jit(solution)/shard_map/gather_cols3/pallas_call | solution.py:679
  101.9 0.9 slice.24.refs_1_
  102.8 0.7 slice_reduce_fusion
  103.7 0.5 fusion.16
  104.3 0.2 convert_multiply_fusion.9
  104.5 1.3 copy-done.9
  105.8 1.1 bitcast_convert_fusion.refs_0_
  106.9 1.8 copy.38
  108.7 0.2 convert_reduce_fusion
  108.9 13.5 %project.1 = (bf16[2048,2048]{1,0:T(8,128)(2,1)}, bf16[2048,256]{1,0:T(8,128)(2,1)S(1)}, bf16[2048,128]{1,0:T(8,128)(2,1)S(1)}) custom-call(bf16[2048,2048]{1,0:T(8,128)(2,1)} %bitcast.85, f32[1,2048]{1,0:T(1,128)S(1)} %bitcast.71, bf16[2048,512]{1,0:T(8,128)(2,1)S(1)} %bitcast.62, f32[2,128,128]{2,1,0:T(8,128)S(1)} %get-tuple-element.102.cos_ref, ...), custom_call_target="tpu_custom_call" | custom-call | tf_op jit(solution)/shard_map/project/pallas_call | solution.py:750
  122.4 0.8 copy-done.6
  123.2 52.4 %gather_up4.1 = (bf16[8,256,2048]{2,1,0:T(8,128)(2,1)}, bf16[4,2048,128]{2,1,0:T(8,128)(2,1)}) custom-call(bf16[256,2048]{1,0:T(8,128)(2,1)} %bitcast_convert_fusion.refs_0_, bf16[2048,128]{1,0:T(8,128)(2,1)} %copy-done.6), custom_call_target="tpu_custom_call" | custom-call | tf_op jit(solution)/shard_map/gather_up4/pallas_call | solution.py:679
  175.6 8.4 %attend.1 = (f32[4,2,256,256]{3,2,1,0:T(8,128)S(1)}, bf16[4,2,2,128,256]{4,3,2,1,0:T(8,128)(2,1)S(1)}, f32[4,2,4,256]{3,2,1,0:T(4,128)S(1)}) custom-call(s32[8]{0:T(128)S(1)} %reshape_squeeze.3.lens, bf16[4,2,2,128,256]{4,3,2,1,0:T(8,128)(2,1)S(1)} %bitcast.66, bf16[4,4,2,2,128,128]{5,4,3,2,1,0:T(8,128)(2,1)} %bitcast.87), custom_call_target="tpu_custom_call" | custom-call | tf_op jit(solution)/shard_map/attend/pallas_call | solution.py:989
  184.0 1.3 copy-done.3
  185.3 7.2 %convolution_convert_fusion = bf16[2048,2048]{1,0:T(8,128)(2,1)} fusion(bf16[2048,256]{1,0:T(8,128)(2,1)S(1)} %bitcast.64, bf16[256,2048]{1,0:T(8,128)(2,1)} %all-gather.11.cloned.1.call-done.refs_1_), kind=kOutput, calls=%fused_computation | convolution fusion | flops 2151677952 | bytes 10485760 | tf_op jit(solution)/shard_map/dot_general | solution.py:712
  192.6 13.8 %all-gather.13.cloned.1.call-done = bf16[32,64,1024]{2,1,0:T(8,128)(2,1)} async-done(((bf16[8,64,1024]{2,1,0:T(8,128)(2,1)}), bf16[32,64,1024]{2,1,0:T(8,128)(2,1)}) %all-gather.13.cloned.1.call-update) | async-done | bytes 4194320 | tf_op jit(solution)/shard_map/all_gather | solution.py:708
  206.4 41.2 %sum_pass5.1 = (bf16[256,2048]{1,0:T(8,128)(2,1)}, bf16[256,1536]{1,0:T(8,128)(2,1)}) custom-call(bf16[8,256,2048]{2,1,0:T(8,128)(2,1)} %bitcast.73, bf16[256,1536]{1,0:T(8,128)(2,1)} %slice.24.refs_1_, bf16[2048,1024]{1,0:T(8,128)(2,1)} %bitcast.74), custom_call_target="tpu_custom_call" | custom-call | tf_op jit(solution)/shard_map/sum_pass5/pallas_call | solution.py:679
  247.6 0.3 reduce-scatter.7.cloned.1.call-start
  247.9 1.7 multiply_reduce_fusion.1
  249.6 1.4 fusion.15.refs_0_
  251.0 49.1 %all-gather.15.cloned.1.call-done = bf16[32,64,1024]{2,1,0:T(8,128)(2,1)} async-done(((bf16[8,64,1024]{2,1,0:T(8,128)(2,1)}), bf16[32,64,1024]{2,1,0:T(8,128)(2,1)}) %all-gather.15.cloned.1.call-update) | async-done | bytes 4194320 | tf_op jit(solution)/shard_map/all_gather | solution.py:708
  300.1 55.3 %forward6.1 = (bf16[8,256,2048]{2,1,0:T(8,128)(2,1)}, f32[2048,1024]{1,0:T(8,128)}, f32[2048,1024]{1,0:T(8,128)}, bf16[2048,1024]{1,0:T(8,128)(2,1)}, bf16[1024,...) custom-call(bf16[256,2048]{1,0:T(8,128)(2,1)} %fusion.15.refs_0_, bf16[2048,1024]{1,0:T(8,128)(2,1)} %bitcast.75, ...), custom_call_target="tpu_custom_call" | custom-call | tf_op jit(solution)/shard_map/forward6/pallas_call | solution.py:679
  355.4 9.0 %all-gather.17.cloned.1.call-done.refs_0_ = bf16[1024,1536]{1,0:T(8,128)(2,1)} async-done(((bf16[256,1536]{1,0:T(8,128)(2,1)}), bf16[1024,1536]{1,0:T(8,128)(2,1)}) %all-gather.17.cloned.1.call-update) | async-done | bytes 3145744 | tf_op jit(solution)/shard_map/all_gather | solution.py:708
  364.4 33.5 %inner_back.1 = (bf16[2048,1024]{1,0:T(8,128)(2,1)}, bf16[2048,1024]{1,0:T(8,128)(2,1)}, bf16[2048,1024]{1,0:T(8,128)(2,1)}) custom-call(bf16[2048,2048]{1,0:T(8,128)(2,1)} %bitcast.80, f32[2048,1024]{1,0:T(8,128)} %get-tuple-element.65.gate_ref, f32[2048,1024]{1,0:T(8,128)} %get-tuple-element.66.up_ref, ...), custom_call_target="tpu_custom_call" | custom-call | tf_op jit(solution)/shard_map/inner_back/pallas_call | solution.py:867
  397.9 0.2 reduce-scatter.11.cloned.1.call-start
  398.2 56.2 %mlp7.1 = (bf16[256,2048]{1,0:T(8,128)(2,1)}, bf16[2048,1024]{1,0:T(8,128)(2,1)}) custom-call(bf16[2048,2048]{1,0:T(8,128)(2,1)} %bitcast.78, bf16[2048,1024]{1,0:T(8,128)(2,1)} %get-tuple-element.69.refs_1_, bf16[2048,1024]{1,0:T(8,128)(2,1)} %get-tuple-element.70.refs_2_, bf16[2048,1024]{1,0:T(8,128)(2,1)} %bitcast.76, bf16[2048,1024]{1,0:T(8,128)(2,1)} %bitcast.82, ...), custom_call_target="tpu_custom_call" | custom-call | tf_op jit(solution)/shard_map/mlp7/pallas_call | solution.py:679
  454.4 0.3 reduce-scatter.15.cloned.1.call-start
  454.7 2.0 fusion.9
  456.9 1.7 fusion.21.refs_0_
  458.6 40.4 %heads_product8.1 = (bf16[2048,256]{1,0:T(8,128)(2,1)}, bf16[256,2048]{1,0:T(8,128)(2,1)}, bf16[2048,2048]{1,0:T(8,128)(2,1)}) custom-call(bf16[256,2048]{1,0:T(8,128)(2,1)} %fusion.21.refs_0_, bf16[256,2048]{1,0:T(8,128)(2,1)} %all-gather.11.cloned.1.call-done.refs_1_, bf16[2048,256]{1,0:T(8,128)(2,1)} %bitcast.65, ...), custom_call_target="tpu_custom_call" | custom-call | tf_op jit(solution)/shard_map/heads_product8/pallas_call | solution.py:679
  499.1 1.2 copy-done.2
  500.3 1.2 copy-done.5
  501.5 15.6 %attend_back.1 = (f32[4,2,2,128,256]{4,3,2,1,0:T(8,128)S(1)}, bf16[4,4,2,2,128,128]{5,4,3,2,1,0:T(8,128)(2,1)}) custom-call(s32[8]{0:T(128)S(1)} %reshape_squeeze.3.lens, bf16[4,2,2,128,256]{4,3,2,1,0:T(8,128)(2,1)S(1)} %bitcast.67, bf16[4,4,2,2,128,128]{5,4,3,2,1,0:T(8,128)(2,1)} %bitcast.88, bf16[4,2,2,128,256]{4,3,2,1,0:T(8,128)(2,1)S(1)} %bitcast.70, ...), custom_call_target="tpu_custom_call" | custom-call | tf_op jit(solution)/shard_map/attend_back/pallas_call | solution.py:1016
  517.1 82.7 %down_sum_back9.1 = (bf16[2048,128]{1,0:T(8,128)(2,1)}, bf16[256,2048]{1,0:T(8,128)(2,1)}, bf16[64,8192]{1,0:T(8,128)(2,1)}) custom-call(bf16[4,2048,128]{2,1,0:T(8,128)(2,1)} %bitcast.94, bf16[8,256,2048]{2,1,0:T(8,128)(2,1)} %bitcast.86, bf16[8,64,1024]{2,1,0:T(8,128)(2,1)} %reduce-scatter.9.cloned.1.call-done.rest_0_.refs_2_), custom_call_target="tpu_custom_call" | custom-call | tf_op jit(solution)/shard_map/down_sum_back9/pallas_call | solution.py:679
  599.8 1.0 copy-done.4
  600.9 15.0 %project_back.1 = (bf16[2048,2048]{1,0:T(8,128)(2,1)}, bf16[2048,384]{1,0:T(8,128)(2,1)S(1)}) custom-call(f32[2048,256]{1,0:T(8,128)S(1)} %bitcast.68, bf16[2048,128]{1,0:T(8,128)(2,1)S(1)} %copy-done.4, bf16[2048,2048]{1,0:T(8,128)(2,1)} %get-tuple-element.82.hid_ref, bf16[2048,512]{1,0:T(8,128)(2,1)} %bitcast.63, ...), custom_call_target="tpu_custom_call" | custom-call | tf_op jit(solution)/shard_map/project_back/pallas_call | solution.py:799
  615.9 1.4 copy.39
  617.4 0.5 reduce-scatter.17.cloned.1.call-update
  617.9 0.6 copy-done.8
  618.5 0.3 multiply_reduce_fusion
  618.9 51.1 %sum_back10.1 = (bf16[256,2048]{1,0:T(8,128)(2,1)}, bf16[64,8192]{1,0:T(8,128)(2,1)}) custom-call(bf16[8,256,2048]{2,1,0:T(8,128)(2,1)} %bitcast.84, bf16[8,64,1024]{2,1,0:T(8,128)(2,1)} %reduce-scatter.11.cloned.1.call-done.refs_1_), custom_call_target="tpu_custom_call" | custom-call | tf_op jit(solution)/shard_map/sum_back10/pallas_call | solution.py:679
  670.0 4.5 convert_multiply_fusion
  674.6 0.5 add.113
  675.1 0.6 fusion.2
  675.7 0.5 copy-done.11
  676.1 3.0 fusion.6
  679.1 13.1 %slab_home11.1 = (bf16[8,64,384]{2,1,0:T(8,128)(2,1)}, bf16[64,2048]{1,0:T(8,128)(2,1)}) custom-call(bf16[8,64,384]{2,1,0:T(8,128)(2,1)} %reduce-scatter.13.cloned.1.call-done.refs_0_, bf16[64,2048]{1,0:T(8,128)(2,1)} %reduce-scatter.15.cloned.1.call-done.refs_1_, bf16[256,2048]{1,0:T(8,128)(2,1)} %get-tuple-element.86.refs_2_), custom_call_target="tpu_custom_call" | custom-call | tf_op jit(solution)/shard_map/slab_home11/pallas_call | solution.py:679
  692.3 1.1 convert_bitcast_fusion
  693.6 0.2 copy.42
  693.9 0.2 copy.41
  694.3 0.8 convert_element_type.161
  695.6 0.5 convert_divide_fusion
  696.1 17.2 %reduce-scatter.17.cloned.1.call-done = bf16[256,1024]{1,0:T(8,128)(2,1)} async-done(((bf16[1024,1024]{1,0:T(8,128)(2,1)}), bf16[256,1024]{1,0:T(8,128)(2,1)}) %reduce-scatter.17.cloned.1.call-update) | async-done | bytes 524304 | tf_op jit(solution)/shard_map/reduce_scatter | solution.py:704
  713.3 2.6 maximum_convert_fusion
  (113 shorter events, 2.2 us)
Async XLA Ops:
  7.2 5.0 copy-start.33
  7.2 5.0 copy-start.32
  7.2 41.8 %all-gather.7.cloned.1.call-start = ((), (), s32[]{:S(2)}) async-start(), calls=%async_computation.6 | async-start | bytes 1310720 | tf_op jit(solution)/shard_map/all_gather | solution.py:708
  8.9 16.9 %copy-start.34 = (bf16[64]{0:T(256)(128)(2,1)S(1)}, bf16[64]{0:T(256)(128)(2,1)}, u32[]{:S(2)}) copy-start(bf16[64]{0:T(256)(128)(2,1)} %param.20) | copy-start | bytes 388
  8.9 16.9 %copy-start.17 = (bf16[64,8192]{1,0:T(8,128)(2,1)S(1)}, bf16[64,8192]{1,0:T(8,128)(2,1)}, u32[]{:S(2)}) copy-start(bf16[64,8192]{1,0:T(8,128)(2,1)} %param.21) | copy-start | bytes 3145732
  8.9 17.0 %copy-start.19 = (bf16[64,8192]{1,0:T(8,128)(2,1)S(1)}, bf16[64,8192]{1,0:T(8,128)(2,1)}, u32[]{:S(2)}) copy-start(bf16[64,8192]{1,0:T(8,128)(2,1)} %param.22) | copy-start | bytes 3145732
  8.9 97.9 %all-gather.9.cloned.1.call-start = ((), (), s32[]{:S(2)}) async-start(), calls=%async_computation.7 | async-start | bytes 2621440 | tf_op jit(solution)/shard_map/all_gather | solution.py:708
  25.8 159.5 %all-gather.11.cloned.1.call-start = ((), (), s32[]{:S(2)}) async-start(), calls=%async_computation.8 | async-start | bytes 1310720 | tf_op jit(solution)/shard_map/all_gather | solution.py:708
  48.4 158.0 %all-gather.13.cloned.1.call-start = ((), (), s32[]{:S(2)}) async-start(), calls=%async_computation.9 | async-start | bytes 5242880 | tf_op jit(solution)/shard_map/all_gather | solution.py:708
  48.9 251.1 %all-gather.15.cloned.1.call-start = ((), (), s32[]{:S(2)}) async-start(), calls=%async_computation.10 | async-start | bytes 5242880 | tf_op jit(solution)/shard_map/all_gather | solution.py:708
  49.0 52.9 %copy-start.24 = (bf16[256,2048]{1,0:T(8,128)(2,1)S(1)}, bf16[256,2048]{1,0:T(8,128)(2,1)}, u32[]{:S(2)}) copy-start(bf16[256,2048]{1,0:T(8,128)(2,1)} %param.23) | copy-start | bytes 3145732
  101.8 2.5 copy-start.25
  101.8 262.6 %all-gather.17.cloned.1.call-start = ((), (), s32[]{:S(2)}) async-start(), calls=%async_computation.11 | async-start | bytes 3932160 | tf_op jit(solution)/shard_map/all_gather | solution.py:708
  104.5 1.3 copy-start.9
  108.7 13.7 %copy-start = (bf16[4,4,128,512]{3,2,0,1:T(8,128)(2,1)}, bf16[4,4,128,512]{3,2,0,1:T(8,128)(2,1)S(1)}, u32[]{:S(2)}) copy-start(bf16[4,4,128,512]{3,2,0,1:T(8,128)(2,1)S(1)} %copy.38) | copy-start | bytes 6291460
  122.4 0.8 copy-start.6
  184.0 1.3 copy-start.3
  185.3 7.2 %copy-start.1 = (bf16[4,2,2,128,256]{4,3,2,1,0:T(8,128)(2,1)}, bf16[4,2,2,128,256]{4,3,2,1,0:T(8,128)(2,1)S(1)}, u32[]{:S(2)}) copy-start(bf16[4,2,2,128,256]{4,3,2,1,0:T(8,128)(2,1)S(1)} %get-tuple-element.59) | copy-start | bytes 3145732
  206.4 41.5 %copy-start.7 = (bf16[2,128,2048]{2,1,0:T(8,128)(2,1)S(1)}, bf16[2,128,2048]{2,1,0:T(8,128)(2,1)}, u32[]{:S(2)}) copy-start(bf16[2,128,2048]{2,1,0:T(8,128)(2,1)} %param.12) | copy-start | bytes 3145732
  247.6 2.0 copy-start.12
  247.6 210.9 %reduce-scatter.7.cloned.1.call-start = ((), (), s32[]{:S(2)}) async-start(), calls=%async_computation.12 | async-start | bytes 2621440 | tf_op jit(solution)/shard_map/reduce_scatter | solution.py:704
  355.4 143.7 %reduce-scatter.9.cloned.1.call-start = ((), (), s32[]{:S(2)}) async-start(), calls=%async_computation.13 | async-start | bytes 5242880 | tf_op jit(solution)/shard_map/reduce_scatter | solution.py:704
  397.9 220.9 %reduce-scatter.11.cloned.1.call-start = ((), (), s32[]{:S(2)}) async-start(), calls=%async_computation.14 | async-start | bytes 5242880 | tf_op jit(solution)/shard_map/reduce_scatter | solution.py:704
  454.4 224.7 %reduce-scatter.15.cloned.1.call-start = ((), (), s32[]{:S(2)}) async-start(), calls=%async_computation.16 | async-start | bytes 1310720 | tf_op jit(solution)/shard_map/reduce_scatter | solution.py:704
  454.7 2.0 copy-start.10
  454.7 2.2 copy-start.15
  499.0 180.1 %reduce-scatter.13.cloned.1.call-start = ((), (), s32[]{:S(2)}) async-start(), calls=%async_computation.15 | async-start | bytes 1966080 | tf_op jit(solution)/shard_map/reduce_scatter | solution.py:704
  499.1 1.2 copy-start.2
  500.3 1.2 copy-start.5
  599.8 1.0 copy-start.4
  617.3 1.2 copy-start.8
  617.3 96.0 %reduce-scatter.17.cloned.1.call-start = ((), (), s32[]{:S(2)}) async-start(), calls=%async_computation.17 | async-start | bytes 2621440 | tf_op jit(solution)/shard_map/reduce_scatter | solution.py:704
  618.8 51.1 %copy-start.18 = (bf16[64,8192]{1,0:T(8,128)(2,1)S(1)}, bf16[64,8192]{1,0:T(8,128)(2,1)}, u32[]{:S(2)}) copy-start(bf16[64,8192]{1,0:T(8,128)(2,1)} %param.21) | copy-start | bytes 3145732
  618.9 51.1 %copy-start.20 = (bf16[64,8192]{1,0:T(8,128)(2,1)S(1)}, bf16[64,8192]{1,0:T(8,128)(2,1)}, u32[]{:S(2)}) copy-start(bf16[64,8192]{1,0:T(8,128)(2,1)} %param.22) | copy-start | bytes 3145732
  670.0 5.1 copy-start.14
  670.0 5.7 copy-start.13
  670.0 5.7 copy-start.16
  670.0 5.7 copy-start.23
  674.5 1.6 copy-start.11
  693.4 1.0 copy-start.29
  693.4 2.1 copy-start.22
  693.5 1.7 copy-start.30
  693.5 1.8 copy-start.31
  693.5 1.9 copy-start.26
  693.6 19.7 %copy-start.21 = (bf16[256,1024]{1,0:T(8,128)(2,1)S(1)}, bf16[256,1024]{1,0:T(8,128)(2,1)}, u32[]{:S(2)}) copy-start(bf16[256,1024]{1,0:T(8,128)(2,1)} %reduce-scatter.7.cloned.1.call-done.refs_6_) | copy-start | bytes 1572868
  693.9 22.0 %copy-start.27 = (f32[64,512]{1,0:T(8,128)}, f32[64,512]{1,0:T(8,128)S(1)}, u32[]{:S(2)}) copy-start(f32[64,512]{1,0:T(8,128)S(1)} %reshape.269) | copy-start | bytes 393220
  694.2 21.7 %copy-start.28 = (f32[64,512]{1,0:T(8,128)}, f32[64,512]{1,0:T(8,128)S(1)}, u32[]{:S(2)}) copy-start(f32[64,512]{1,0:T(8,128)S(1)} %reshape.268) | copy-start | bytes 393220
Sparse Core Ops, SparseCore 0:
  10.2 33.7 all-gather.6
  45.5 47.8 all-gather.8
  95.0 26.6 all-gather.10
  123.1 83.2 all-gather.12
  207.8 92.2 all-gather.14
  301.5 62.9 all-gather.16
  366.7 42.4 reduce-scatter.6
  411.7 76.0 reduce-scatter.8
  490.1 102.1 reduce-scatter.10
  594.5 31.7 reduce-scatter.14
  628.7 33.9 reduce-scatter.12
  664.8 48.4 reduce-scatter.16

commit v6 on v5

--- a/solution.py
+++ b/solution.py
@@ -385,11 +385,86 @@
     done.wait()
 
 
+def reduce_steps(nz, x_ref, o_ref, mine, above, below, lsem, us, ur, ds, dr):
+    z = lax.axis_index("cm")
+    rows = x_ref.shape[1]
+
+    def load(j):
+        return pltpu.make_async_copy(x_ref.at[j], mine.at[j], lsem.at[j])
+
+    def down(j):
+        return remote(mine.at[j], above.at[j], ds.at[j], dr.at[j], {"cm": jnp.maximum(z - 1, 0)})
+
+    def up(j):
+        return remote(mine.at[j], below.at[j], us.at[j], ur.at[j], {"cm": jnp.minimum(z + 1, nz - 1)})
+
+    for j in range(nz):
+        load(j).start()
+    for j in range(nz):
+        load(j).wait()
+
+    @pl.when(z == nz - 1)
+    def _():
+        for j in range(nz - 1):
+            down(j).start()
+
+    @pl.when(z == 0)
+    def _():
+        for j in range(nz - 1, 0, -1):
+            up(j).start()
+
+    yield
+    yield
+
+    def pass_down():
+        for j in range(nz - 1):
+
+            @pl.when(jnp.logical_and(z > j, z < nz - 1))
+            def _(j=j):
+                down(j).wait_recv()
+                add_rows(mine.at[j], (mine.at[j], above.at[j]), rows)
+                down(j).start()
+
+    def pass_up():
+        for j in range(nz - 1, 0, -1):
+
+            @pl.when(jnp.logical_and(z < j, z > 0))
+            def _(j=j):
+                up(j).wait_recv()
+                add_rows(mine.at[j], (mine.at[j], below.at[j]), rows)
+                up(j).start()
+
+    low = 2 * z < nz - 1
+    pl.when(low)(pass_up)
+    pl.when(jnp.logical_not(low))(pass_down)
+    yield
+    pl.when(low)(pass_down)
+    pl.when(jnp.logical_not(low))(pass_up)
+    yield
+    for j in range(nz):
+
+        @pl.when(z == j)
+        def _(j=j):
+            if j < nz - 1:
+                down(j).wait_recv()
+                add_rows(mine.at[j], (mine.at[j], above.at[j]), rows)
+            if j > 0:
+                up(j).wait_recv()
+                add_rows(mine.at[j], (mine.at[j], below.at[j]), rows)
+            done = pltpu.make_async_copy(mine.at[j], o_ref, lsem.at[nz])
+            done.start()
+            done.wait()
+
+    for j in range(nz):
+        pl.when(z > j)(lambda j=j: down(j).wait_send())
+        pl.when(z < j)(lambda j=j: up(j).wait_send())
+
+
 def row_loads(nz, src, dst, sems):
     run = dst.shape[0] // (4 * nz)
     copies = []
     for c in range(4 * nz):
-        at = (c % nz * 4 + c // nz) * run
+        at = c % nz * (src.shape[0] // nz) + c // nz * run
         copies.append(pltpu.make_async_copy(src.at[pl.ds(at, run)], dst.at[pl.ds(c * run, run)], sems.at[c]))
     return copies
 
@@ -598,6 +673,9 @@
     if kind == "down":
         scratch = [vmem(*x.shape)] * 2 + [dma(nz + 1), dma(nz), dma(nz)]
         return kind, functools.partial(down_steps, nz), xs, [like(*x.shape[1:])], scratch
+    if kind == "reduce":
+        scratch = [vmem(*x.shape)] * 3 + [dma(nz + 1)] + [dma(nz)] * 4
+        return kind, functools.partial(reduce_steps, nz), xs, [like(*x.shape[1:])], scratch
     if kind in ("move", "home"):
         return kind, functools.partial(move_steps, nz, kind == "home"), xs, [like(*x.shape)], [dma(1), dma(1), dma(1)]
     if kind == "mlp":
@@ -650,7 +728,7 @@
     results = [o for p in parts for o in p[3]]
     moves = [k == "home" for k in kinds if k in ("move", "home")]
     whole = any(k in ("slab", "cols", "back") for k in kinds)
-    line = any(k in ("up", "down") for k in kinds)
+    line = any(k in ("up", "down", "reduce") for k in kinds)
 
     def kernel(*refs):
         ins = list(refs[: len(operands)])
@@ -1071,14 +1149,16 @@
     pack, lens = transfer(1, [part("slab", pack), part("slab", lens)])
     lens = lens[::2, 0, :seqs].reshape(-1)
     wg, wo = transfer(2, [part("cols", gained(w_gate), pieces=pieces), part("move", w_out)], (pack,))
+    ff = wg.shape[2]
+    wg = jnp.concatenate([wg.reshape(8 * r, ff), wo.reshape(-1, ff)], 0)
     own = tokens.reshape(rows, width)
     tok_all, wu = transfer(
         3, [part("gather", own), part("cols", gained(w_up), pieces=pieces)], (wg, wd_one)
     )
     pack = gather_planes(pack).reshape(nz, 4, 2 * r, -1).transpose(1, 0, 2, 3).reshape(width, -1)
     gain_row = pack[:, wide + 2 * HD].astype(F32)[None]
-    wg = gather_planes(wg).reshape(width, -1)
-    wo = gather_planes(wo)
+    wg = gather_planes(wg)
+    wo = wg.reshape(nz, -1, ff)[:, 8 * r :].reshape(-1, width)
 
     slot = cm * 2 * block + jnp.arange(2 * block, dtype=jnp.int32).reshape(2, block)
     cos, sin = tables(slot)
@@ -1124,9 +1204,16 @@
     layer_out = (resid_mid + out_sum.astype(F32)).astype(BF)
     e_one, grad_qkv = project_back(dq, dkv, hidden_one, pack, cos, sin, (wd_right,))
     wd_right = sum_planes(wd_right)
-    e_one, grad_wg = transfer(10, [part("sum", e_one), part("back", grad_wg, pieces=pieces)])
+    grad_qkv, e_one, grad_wg = transfer(
+        10,
+        [
+            part("reduce", rows_first(grad_qkv).reshape(nz, 8 * r, -1)),
+            part("sum", e_one),
+            part("back", grad_wg, pieces=pieces),
+        ],
+    )
     grad_wo = sum_planes(grad_wo)
-    grad_qkv = sum_planes(rows_first(grad_qkv))
+    grad_qkv = grad_qkv.reshape(8, r, -1)
     scale_one = rms_scale(resid_in)
     grad_tokens = grad_mid + norm_back(e_one.astype(F32) * gain_row, resid_in * scale_one, scale_one)
     grad_qkv, grad_wo = transfer(11, [part("slab", grad_qkv), part("home", grad_wo)], (e_one,))

time: 735 us -> 728 us (level)
  waiting for transfers between devices: 90.4 us -> 66 us
  Pallas kernels: 564 us -> 577 us
    reduce_scatter x6 -> x5, waiting for transfers between devices: 17.2 us -> 0.04 us  [sum_planes(): return lax.psum_scatter(g, 'cm', scatter_dimension=0, tiled=True)]
    pallas_call x11, Pallas kernels: 478 us -> 491 us  [transfer(): pl.pallas_call(kernel, out_shape=results, in_specs=[ANY] * (len(operands)...]
    all_gather x6 -> x5, waiting for transfers between devices: 71.9 us -> 65.8 us  [gather_planes(): return lax.all_gather(x, 'cm', axis=0, tiled=True)]
  transfers between devices with their start and end apart: 12 -> 10, of which waited for: 4 -> 3; matrix products, arithmetic and copies ran while one was open for 6% -> 7% of each run, Pallas kernels for 78% -> 80%
where the time goes in v6:
time: 728 us; the launch traced here: 717 us
  Pallas kernels  577 us (79%)
  waiting for transfers between devices  66 us (9%)
  other arithmetic  29.7 us (4%)
  local copies, waits for them, and re-layouts  22.3 us (3%)
  between operations  15.3 us (2%)
    pallas_call x11, Pallas kernels, transfer(): pl.pallas_call(kernel, out_shape=results, in_specs=[ANY] * (len(operands)...  491 us
    all_gather x5, waiting for transfers between devices, gather_planes(): return lax.all_gather(x, 'cm', axis=0, tiled=True)  65.8 us
    pallas_call x1, Pallas kernels, inner_back(): pl.pallas_call(functools.partial(inner_back_kernel, nz, width // (8 * nz)...  33.5 us
    pallas_call x1, Pallas kernels, attend_back(): pl.pallas_call(attend_back_kernel, grid=(4, seqs), out_shape=[jax.ShapeDt...  15.6 us
    pallas_call x1, Pallas kernels, project_back(): pl.pallas_call(project_back_kernel, grid=(8,), out_shape=[jax.ShapeDtypeS...  15 us
  transfers between devices with their start and end apart: 10, of which 3 were waited for; matrix products, arithmetic and copies ran while one was open for 7% of the time, Pallas kernels for 80%

profile of v6, /device:TPU:0, one launch (start us, length us, event | category | flops | bytes accessed | tf_op | source)
XLA Modules:
  0.0 716.8 jit_solution(11389872951465072218)
XLA Ops:
  7.2 1.7 slice.25
  9.0 1.1 copy.46
  10.1 1.0 reshape.249
  11.1 1.0 reshape.250
  12.3 0.9 maximum_bitcast_fusion.refs_0_
  13.2 0.6 broadcast_in_dim.11.refs_1_
  13.8 11.9 %slab_slab1.1 = (bf16[8,64,512]{2,1,0:T(8,128)(2,1)}, s32[8,8,128]{2,1,0:T(8,128)}) custom-call(bf16[8,64,512]{2,1,0:T(8,128)(2,1)} %maximum_bitcast_fusion.refs_0_, s32[8,8,128]{2,1,0:T(8,128)} %broadcast_in_dim.11.refs_1_), custom_call_target="tpu_custom_call" | custom-call | tf_op jit(solution)/shard_map/slab_slab1/pallas_call | solution.py:757
  25.9 1.8 fusion.8
  27.7 20.6 %cols_move2.1 = (bf16[8,64,1024]{2,1,0:T(8,128)(2,1)}, bf16[64,2048]{1,0:T(8,128)(2,1)}) custom-call(bf16[64,8192]{1,0:T(8,128)(2,1)} %get-tuple-element.107.refs_0_, bf16[64,2048]{1,0:T(8,128)(2,1)} %refs_1_.1, bf16[8,64,512]{2,1,0:T(8,128)(2,1)} %get-tuple-element.54.refs_2_), custom_call_target="tpu_custom_call" | custom-call | tf_op jit(solution)/shard_map/cols_move2/pallas_call | solution.py:757
  48.4 1.0 reshape.252
  49.4 2.4 pad_maximum_fusion.refs_2_
  51.9 52.7 %gather_cols3.1 = (bf16[8,256,2048]{2,1,0:T(8,128)(2,1)}, bf16[8,64,1024]{2,1,0:T(8,128)(2,1)}) custom-call(bf16[256,2048]{1,0:T(8,128)(2,1)} %bitcast.74, bf16[64,8192]{1,0:T(8,128)(2,1)} %get-tuple-element.108.refs_1_, bf16[640,1024]{1,0:T(8,128)(2,1)} %pad_maximum_fusion.refs_2_, bf16[1024,512]{1,0:T(8,128)(2,1)} %all-gather.6.cloned.1.call-done.refs_3_.wl_ref.refs_4_), custom_call_target="tpu_custom_call" | custom-call | tf_op jit(solution)/shard_map/gather_cols3/pallas_call | solution.py:757
  104.8 1.0 slice.28.refs_1_
  105.8 0.7 slice_reduce_fusion
  106.7 0.5 fusion.16
  107.2 0.2 convert_multiply_fusion.9
  107.4 1.3 copy-done.9
  108.8 1.1 bitcast_convert_fusion.refs_0_
  109.8 1.8 copy.38
  111.6 0.2 convert_reduce_fusion
  111.9 13.5 %project.1 = (bf16[2048,2048]{1,0:T(8,128)(2,1)}, bf16[2048,256]{1,0:T(8,128)(2,1)S(1)}, bf16[2048,128]{1,0:T(8,128)(2,1)S(1)}) custom-call(bf16[2048,2048]{1,0:T(8,128)(2,1)} %bitcast.84, f32[1,2048]{1,0:T(1,128)S(1)} %bitcast.73, bf16[2048,512]{1,0:T(8,128)(2,1)S(1)} %bitcast.64, f32[2,128,128]{2,1,0:T(8,128)S(1)} %get-tuple-element.104.cos_ref, ...), custom_call_target="tpu_custom_call" | custom-call | tf_op jit(solution)/shard_map/project/pallas_call | solution.py:828
  125.3 0.8 copy-done.6
  126.1 52.3 %gather_up4.1 = (bf16[8,256,2048]{2,1,0:T(8,128)(2,1)}, bf16[4,2048,128]{2,1,0:T(8,128)(2,1)}) custom-call(bf16[256,2048]{1,0:T(8,128)(2,1)} %bitcast_convert_fusion.refs_0_, bf16[2048,128]{1,0:T(8,128)(2,1)} %copy-done.6), custom_call_target="tpu_custom_call" | custom-call | tf_op jit(solution)/shard_map/gather_up4/pallas_call | solution.py:757
  178.5 8.4 %attend.1 = (f32[4,2,256,256]{3,2,1,0:T(8,128)S(1)}, bf16[4,2,2,128,256]{4,3,2,1,0:T(8,128)(2,1)S(1)}, f32[4,2,4,256]{3,2,1,0:T(4,128)S(1)}) custom-call(s32[8]{0:T(128)S(1)} %reshape_squeeze.3.lens, bf16[4,2,2,128,256]{4,3,2,1,0:T(8,128)(2,1)S(1)} %bitcast.68, bf16[4,4,2,2,128,128]{5,4,3,2,1,0:T(8,128)(2,1)} %bitcast.87), custom_call_target="tpu_custom_call" | custom-call | tf_op jit(solution)/shard_map/attend/pallas_call | solution.py:1067
  186.9 1.3 copy-done.3
  188.2 11.2 %all-gather.10.cloned.1.call-done.refs_2_.refs_1_.refs_3_ = bf16[2560,1024]{1,0:T(8,128)(2,1)} async-done(((bf16[640,1024]{1,0:T(8,128)(2,1)}), bf16[2560,1024]{1,0:T(8,128)(2,1)}) %all-gather.10.cloned.1.call-update) | async-done | bytes 5242896 | tf_op jit(solution)/shard_map/all_gather | solution.py:786
  199.5 2.3 slice.33
  201.7 1.4 reshape.264.refs_1_
  203.2 5.6 convolution_convert_fusion
  208.8 41.9 %sum_pass5.1 = (bf16[256,2048]{1,0:T(8,128)(2,1)}, bf16[256,1536]{1,0:T(8,128)(2,1)}) custom-call(bf16[8,256,2048]{2,1,0:T(8,128)(2,1)} %bitcast.76, bf16[256,1536]{1,0:T(8,128)(2,1)} %slice.28.refs_1_, bf16[2560,1024]{1,0:T(8,128)(2,1)} %all-gather.10.cloned.1.call-done.refs_2_.refs_1_.refs_3_), custom_call_target="tpu_custom_call" | custom-call | tf_op jit(solution)/shard_map/sum_pass5/pallas_call | solution.py:757
  250.7 0.3 reduce-scatter.6.cloned.1.call-start
  251.0 1.7 multiply_reduce_fusion.1
  252.7 1.4 fusion.15.refs_0_
  254.1 40.9 %all-gather.12.cloned.1.call-done = bf16[32,64,1024]{2,1,0:T(8,128)(2,1)} async-done(((bf16[8,64,1024]{2,1,0:T(8,128)(2,1)}), bf16[32,64,1024]{2,1,0:T(8,128)(2,1)}) %all-gather.12.cloned.1.call-update) | async-done | bytes 4194320 | tf_op jit(solution)/shard_map/all_gather | solution.py:786
  295.0 55.3 %forward6.1 = (bf16[8,256,2048]{2,1,0:T(8,128)(2,1)}, f32[2048,1024]{1,0:T(8,128)}, f32[2048,1024]{1,0:T(8,128)}, bf16[2048,1024]{1,0:T(8,128)(2,1)}, bf16[1024,...) custom-call(bf16[256,2048]{1,0:T(8,128)(2,1)} %fusion.15.refs_0_, ...), custom_call_target="tpu_custom_call" | custom-call | tf_op jit(solution)/shard_map/forward6/pallas_call | solution.py:757
  350.3 13.6 %all-gather.14.cloned.1.call-done.refs_0_ = bf16[1024,1536]{1,0:T(8,128)(2,1)} async-done(((bf16[256,1536]{1,0:T(8,128)(2,1)}), bf16[1024,1536]{1,0:T(8,128)(2,1)}) %all-gather.14.cloned.1.call-update) | async-done | bytes 3145744 | tf_op jit(solution)/shard_map/all_gather | solution.py:786
  363.9 33.5 %inner_back.1 = (bf16[2048,1024]{1,0:T(8,128)(2,1)}, bf16[2048,1024]{1,0:T(8,128)(2,1)}, bf16[2048,1024]{1,0:T(8,128)(2,1)}) custom-call(bf16[2048,2048]{1,0:T(8,128)(2,1)} %bitcast.78, f32[2048,1024]{1,0:T(8,128)} %get-tuple-element.66.gate_ref, f32[2048,1024]{1,0:T(8,128)} %get-tuple-element.67.up_ref, ...), custom_call_target="tpu_custom_call" | custom-call | tf_op jit(solution)/shard_map/inner_back/pallas_call | solution.py:945
  397.4 0.2 reduce-scatter.10.cloned.1.call-start
  397.6 56.2 %mlp7.1 = (bf16[256,2048]{1,0:T(8,128)(2,1)}, bf16[2048,1024]{1,0:T(8,128)(2,1)}) custom-call(bf16[2048,2048]{1,0:T(8,128)(2,1)} %bitcast.80, bf16[2048,1024]{1,0:T(8,128)(2,1)} %get-tuple-element.70.refs_1_, bf16[2048,1024]{1,0:T(8,128)(2,1)} %get-tuple-element.71.refs_2_, bf16[2560,1024]{1,0:T(8,128)(2,1)} %all-gather.10.cloned.1.call-done.refs_2_.refs_1_.refs_3_, ...), custom_call_target="tpu_custom_call" | custom-call | tf_op jit(solution)/shard_map/mlp7/pallas_call | solution.py:757
  453.9 0.3 reduce-scatter.12.cloned.1.call-start
  454.2 2.0 fusion.9
  456.4 1.7 fusion.21.refs_0_
  458.1 40.5 %heads_product8.1 = (bf16[2048,256]{1,0:T(8,128)(2,1)}, bf16[256,2048]{1,0:T(8,128)(2,1)}, bf16[2048,2048]{1,0:T(8,128)(2,1)}) custom-call(bf16[256,2048]{1,0:T(8,128)(2,1)} %fusion.21.refs_0_, bf16[256,2048]{1,0:T(8,128)(2,1)} %copy-done.17, bf16[2048,256]{1,0:T(8,128)(2,1)} %bitcast.67, bf16[2048,1024]{1,0:T(8,128)(2,1)} %get-tuple-element.74.refs_3_, ...), custom_call_target="tpu_custom_call" | custom-call | tf_op jit(solution)/shard_map/heads_product8/pallas_call | solution.py:757
  498.7 1.2 copy-done.2
  499.9 1.2 copy-done.5
  501.1 15.6 %attend_back.1 = (f32[4,2,2,128,256]{4,3,2,1,0:T(8,128)S(1)}, bf16[4,4,2,2,128,128]{5,4,3,2,1,0:T(8,128)(2,1)}) custom-call(s32[8]{0:T(128)S(1)} %reshape_squeeze.3.lens, bf16[4,2,2,128,256]{4,3,2,1,0:T(8,128)(2,1)S(1)} %bitcast.69, bf16[4,4,2,2,128,128]{5,4,3,2,1,0:T(8,128)(2,1)} %bitcast.88, bf16[4,2,2,128,256]{4,3,2,1,0:T(8,128)(2,1)S(1)} %bitcast.72, ...), custom_call_target="tpu_custom_call" | custom-call | tf_op jit(solution)/shard_map/attend_back/pallas_call | solution.py:1094
  516.7 85.3 %down_sum_back9.1 = (bf16[2048,128]{1,0:T(8,128)(2,1)}, bf16[256,2048]{1,0:T(8,128)(2,1)}, bf16[64,8192]{1,0:T(8,128)(2,1)}) custom-call(bf16[4,2048,128]{2,1,0:T(8,128)(2,1)} %bitcast.94, bf16[8,256,2048]{2,1,0:T(8,128)(2,1)} %bitcast.85, bf16[8,64,1024]{2,1,0:T(8,128)(2,1)} %reduce-scatter.8.cloned.1.call-done.rest_0_.refs_2_), custom_call_target="tpu_custom_call" | custom-call | tf_op jit(solution)/shard_map/down_sum_back9/pallas_call | solution.py:757
  602.1 1.6 multiply_reduce_fusion
  603.7 15.0 %project_back.1 = (bf16[2048,2048]{1,0:T(8,128)(2,1)}, bf16[2048,384]{1,0:T(8,128)(2,1)S(1)}) custom-call(f32[2048,256]{1,0:T(8,128)S(1)} %bitcast.70, bf16[2048,128]{1,0:T(8,128)(2,1)S(1)} %copy-done.4, bf16[2048,2048]{1,0:T(8,128)(2,1)} %get-tuple-element.83.hid_ref, bf16[2048,512]{1,0:T(8,128)(2,1)} %bitcast.65, ...), custom_call_target="tpu_custom_call" | custom-call | tf_op jit(solution)/shard_map/project_back/pallas_call | solution.py:877
  618.7 1.4 copy.39
  620.1 63.2 %reduce_sum_back10.1 = (bf16[512,384]{1,0:T(8,128)(2,1)}, bf16[256,2048]{1,0:T(8,128)(2,1)}, bf16[64,8192]{1,0:T(8,128)(2,1)}) custom-call(bf16[4,512,384]{2,1,0:T(8,128)(2,1)} %bitcast.89, bf16[8,256,2048]{2,1,0:T(8,128)(2,1)} %bitcast.86, bf16[8,64,1024]{2,1,0:T(8,128)(2,1)} %reduce-scatter.10.cloned.1.call-done.refs_2_), custom_call_target="tpu_custom_call" | custom-call | tf_op jit(solution)/shard_map/reduce_sum_back10/pallas_call | solution.py:757
  683.3 10.9 %slab_home11.1 = (bf16[8,64,384]{2,1,0:T(8,128)(2,1)}, bf16[64,2048]{1,0:T(8,128)(2,1)}) custom-call(bf16[8,64,384]{2,1,0:T(8,128)(2,1)} %bitcast.100, bf16[64,2048]{1,0:T(8,128)(2,1)} %reduce-scatter.12.cloned.1.call-done.refs_1_, bf16[256,2048]{1,0:T(8,128)(2,1)} %get-tuple-element.88.refs_2_), custom_call_target="tpu_custom_call" | custom-call | tf_op jit(solution)/shard_map/slab_home11/pallas_call | solution.py:757
  694.2 1.1 convert_bitcast_fusion
  695.5 0.2 copy.42
  695.8 0.2 copy.41
  696.1 0.1 copy-done.30
  696.2 0.8 convert_element_type.161
  697.2 4.5 convert_multiply_fusion
  701.8 0.5 add.111
  702.6 0.2 multiply_reduce_fusion.2
  702.8 0.6 fusion.2
  703.4 0.5 convert_divide_fusion
  703.9 3.0 fusion.6
  706.9 2.6 maximum_convert_fusion
  (121 shorter events, 2.0 us)
Async XLA Ops:
  7.2 5.0 copy-start.38
  7.2 5.0 copy-start.36
  7.2 44.7 %all-gather.6.cloned.1.call-start = ((), (), s32[]{:S(2)}) async-start(), calls=%async_computation.5 | async-start | bytes 1310720 | tf_op jit(solution)/shard_map/all_gather | solution.py:786
  8.9 16.9 %copy-start.39 = (bf16[64]{0:T(256)(128)(2,1)S(1)}, bf16[64]{0:T(256)(128)(2,1)}, u32[]{:S(2)}) copy-start(bf16[64]{0:T(256)(128)(2,1)} %param.20) | copy-start | bytes 388
  8.9 16.9 %copy-start.18 = (bf16[64,8192]{1,0:T(8,128)(2,1)S(1)}, bf16[64,8192]{1,0:T(8,128)(2,1)}, u32[]{:S(2)}) copy-start(bf16[64,8192]{1,0:T(8,128)(2,1)} %param.21) | copy-start | bytes 3145732
  8.9 17.0 %copy-start.20 = (bf16[64,8192]{1,0:T(8,128)(2,1)S(1)}, bf16[64,8192]{1,0:T(8,128)(2,1)}, u32[]{:S(2)}) copy-start(bf16[64,8192]{1,0:T(8,128)(2,1)} %param.22) | copy-start | bytes 3145732
  8.9 100.9 %all-gather.8.cloned.1.call-start = ((), (), s32[]{:S(2)}) async-start(), calls=%async_computation.6 | async-start | bytes 2621440 | tf_op jit(solution)/shard_map/all_gather | solution.py:786
  25.8 173.7 %all-gather.10.cloned.1.call-start = ((), (), s32[]{:S(2)}) async-start(), calls=%async_computation.7 | async-start | bytes 6553600 | tf_op jit(solution)/shard_map/all_gather | solution.py:786
  25.9 1.8 copy-start.35
  51.9 243.1 %all-gather.12.cloned.1.call-start = ((), (), s32[]{:S(2)}) async-start(), calls=%async_computation.8 | async-start | bytes 5242880 | tf_op jit(solution)/shard_map/all_gather | solution.py:786
  51.9 52.9 %copy-start.25 = (bf16[256,2048]{1,0:T(8,128)(2,1)S(1)}, bf16[256,2048]{1,0:T(8,128)(2,1)}, u32[]{:S(2)}) copy-start(bf16[256,2048]{1,0:T(8,128)(2,1)} %param.23) | copy-start | bytes 3145732
  104.7 2.5 copy-start.26
  104.7 259.2 %all-gather.14.cloned.1.call-start = ((), (), s32[]{:S(2)}) async-start(), calls=%async_computation.9 | async-start | bytes 3932160 | tf_op jit(solution)/shard_map/all_gather | solution.py:786
  107.4 1.3 copy-start.9
  111.6 13.7 %copy-start = (bf16[4,4,128,512]{3,2,0,1:T(8,128)(2,1)}, bf16[4,4,128,512]{3,2,0,1:T(8,128)(2,1)S(1)}, u32[]{:S(2)}) copy-start(bf16[4,4,128,512]{3,2,0,1:T(8,128)(2,1)S(1)} %copy.38) | copy-start | bytes 6291460
  125.3 0.8 copy-start.6
  186.9 1.3 copy-start.3
  188.2 14.9 %copy-start.1 = (bf16[4,2,2,128,256]{4,3,2,1,0:T(8,128)(2,1)}, bf16[4,2,2,128,256]{4,3,2,1,0:T(8,128)(2,1)S(1)}, u32[]{:S(2)}) copy-start(bf16[4,2,2,128,256]{4,3,2,1,0:T(8,128)(2,1)S(1)} %get-tuple-element.61) | copy-start | bytes 3145732
  203.2 5.7 copy-start.17
  208.8 42.2 %copy-start.7 = (bf16[2,128,2048]{2,1,0:T(8,128)(2,1)S(1)}, bf16[2,128,2048]{2,1,0:T(8,128)(2,1)}, u32[]{:S(2)}) copy-start(bf16[2,128,2048]{2,1,0:T(8,128)(2,1)} %param.12) | copy-start | bytes 3145732
  250.7 2.0 copy-start.12
  250.7 207.4 %reduce-scatter.6.cloned.1.call-start = ((), (), s32[]{:S(2)}) async-start(), calls=%async_computation.10 | async-start | bytes 2621440 | tf_op jit(solution)/shard_map/reduce_scatter | solution.py:782
  350.3 148.4 %reduce-scatter.8.cloned.1.call-start = ((), (), s32[]{:S(2)}) async-start(), calls=%async_computation.11 | async-start | bytes 5242880 | tf_op jit(solution)/shard_map/reduce_scatter | solution.py:782
  397.4 222.7 %reduce-scatter.10.cloned.1.call-start = ((), (), s32[]{:S(2)}) async-start(), calls=%async_computation.12 | async-start | bytes 5242880 | tf_op jit(solution)/shard_map/reduce_scatter | solution.py:782
  453.9 229.4 %reduce-scatter.12.cloned.1.call-start = ((), (), s32[]{:S(2)}) async-start(), calls=%async_computation.13 | async-start | bytes 1310720 | tf_op jit(solution)/shard_map/reduce_scatter | solution.py:782
  454.2 2.0 copy-start.10
  454.2 2.2 copy-start.15
  456.4 1.7 copy-start.33
  498.6 208.3 %reduce-scatter.14.cloned.1.call-start = ((), (), s32[]{:S(2)}) async-start(), calls=%async_computation.14 | async-start | bytes 2621440 | tf_op jit(solution)/shard_map/reduce_scatter | solution.py:782
  498.7 1.2 copy-start.2
  499.9 1.2 copy-start.5
  602.1 1.6 copy-start.4
  695.3 1.0 copy-start.30
  695.3 7.3 %copy-start.23 = (f32[8,8,8,256]{3,2,0,1:T(8,128)}, f32[8,8,8,256]{3,2,0,1:T(8,128)S(1)}, u32[]{:S(2)}) copy-start(f32[8,8,8,256]{3,2,0,1:T(8,128)S(1)} %copy.44) | copy-start | bytes 1572868
  695.4 1.7 copy-start.19
  695.4 1.8 copy-start.21
  695.8 6.6 copy-start.28
  696.1 6.4 copy-start.29
  697.2 5.1 copy-start.31
  697.2 5.3 copy-start.32
  697.2 5.4 copy-start.27
  697.2 5.6 copy-start.8
  697.2 5.6 copy-start.14
  697.2 6.7 copy-start.16
  697.2 6.7 copy-start.24
  701.8 1.6 copy-start.37
  701.8 2.1 copy-start.11
  701.8 2.1 copy-start.13
  701.8 2.1 copy-start.34
  703.9 3.0 copy-start.22
Sparse Core Ops, SparseCore 0:
  10.2 33.6 all-gather.5
  45.5 47.8 all-gather.7
  95.5 103.8 all-gather.9
  200.9 94.0 all-gather.11
  296.4 67.4 all-gather.13
  366.1 42.4 reduce-scatter.5
  411.0 76.0 reduce-scatter.7
  489.4 96.4 reduce-scatter.9
  588.4 31.8 reduce-scatter.11
  622.4 64.4 reduce-scatter.13

commit v7 on v6

--- a/solution.py
+++ b/solution.py
@@ -1141,9 +1141,12 @@
         return (w.astype(F32) * gain_two).astype(BF)
 
     down = w_down if pieces > 1 else lax.ppermute(w_down, ("cm", "cl"), perm)
-    wd_one = gather_planes(down[:, : width // 4])
+    fb = down.shape[0]
+    gains = jnp.pad(attn_gain[None], ((0, 15), (0, width // 4 - r)))
+    wd_one = gather_planes(jnp.concatenate([down[:, : width // 4], gains], 0)).reshape(nz, fb + 16, -1)
+    gains = jnp.pad(wd_one[:, fb, :r].reshape(-1, 2 * HD), ((0, 32 - nz * r // (2 * HD)), (0, 0)))
+    wd_one = wd_one[:, :fb].reshape(nz * fb, -1)
     pack = [w.reshape(r, 8, -1) for w in (w_query, w_key, w_value)]
-    pack.append(jnp.broadcast_to(attn_gain[:, None, None], (r, 8, 2 * HD)))
     pack = jnp.concatenate(pack, -1).transpose(1, 0, 2)
     lens = jnp.broadcast_to(jnp.pad(lengths, (0, 128 - seqs))[None, None], (8, 8, 128))
     pack, lens = transfer(1, [part("slab", pack), part("slab", lens)])
@@ -1152,11 +1155,12 @@
     ff = wg.shape[2]
     wg = jnp.concatenate([wg.reshape(8 * r, ff), wo.reshape(-1, ff)], 0)
     own = tokens.reshape(rows, width)
-    tok_all, wu = transfer(
-        3, [part("gather", own), part("cols", gained(w_up), pieces=pieces)], (wg, wd_one)
+    tok_all, wu, gains = transfer(
+        3, [part("gather", own), part("cols", gained(w_up), pieces=pieces), part("gather", gains)], (wg,)
     )
     pack = gather_planes(pack).reshape(nz, 4, 2 * r, -1).transpose(1, 0, 2, 3).reshape(width, -1)
-    gain_row = pack[:, wide + 2 * HD].astype(F32)[None]
+    gains = gains[:, : nz * r // (2 * HD)].reshape(4, 2, nz, r).transpose(0, 2, 1, 3)
+    gain_row = gains.reshape(1, width).astype(F32)
     wg = gather_planes(wg)
     wo = wg.reshape(nz, -1, ff)[:, 8 * r :].reshape(-1, width)
 

time: 728 us -> 729 us (level); the launches traced: 717 us -> 729 us
  waiting for transfers between devices: 66 us -> 56.7 us
  local copies, waits for them, and re-layouts: 22.3 us -> 31.3 us
  Pallas kernels: 577 us -> 585 us
    pallas_call x11, Pallas kernels: 491 us -> 500 us  [transfer(): pl.pallas_call(kernel, out_shape=results, in_specs=[ANY] * (len(operands)...]
    all_gather x5, waiting for transfers between devices: 65.8 us -> 56.5 us  [gather_planes(): return lax.all_gather(x, 'cm', axis=0, tiled=True)]
where the time goes in v7:
time: 729 us
  Pallas kernels  585 us (80%)
  waiting for transfers between devices  56.7 us (8%)
  other arithmetic  32.6 us (4%)
  local copies, waits for them, and re-layouts  31.3 us (4%)
  between operations  15.3 us (2%)
    pallas_call x11, Pallas kernels, transfer(): pl.pallas_call(kernel, out_shape=results, in_specs=[ANY] * (len(operands)...  500 us
    all_gather x5, waiting for transfers between devices, gather_planes(): return lax.all_gather(x, 'cm', axis=0, tiled=True)  56.5 us
    pallas_call x1, Pallas kernels, inner_back(): pl.pallas_call(functools.partial(inner_back_kernel, nz, width // (8 * nz)...  33.2 us
    pallas_call x1, Pallas kernels, attend_back(): pl.pallas_call(attend_back_kernel, grid=(4, seqs), out_shape=[jax.ShapeDt...  15.6 us
  transfers between devices with their start and end apart: 10, of which 3 were waited for; matrix products, arithmetic and copies ran while one was open for 7% of the time, Pallas kernels for 80%

profile of v7, /device:TPU:0, one launch (start us, length us, event | category | flops | bytes accessed | tf_op | source)
XLA Modules:
  0.0 728.6 jit_solution(6544626903105170155)
XLA Ops:
  7.2 1.0 slice.31
  8.3 1.5 fusion.17
  9.9 1.0 reshape.262
  10.9 1.0 reshape.263
  12.0 0.9 maximum_bitcast_fusion.refs_0_
  12.8 0.6 broadcast_in_dim.12.refs_1_
  13.4 10.5 %slab_slab1.1 = (bf16[8,64,384]{2,1,0:T(8,128)(2,1)}, s32[8,8,128]{2,1,0:T(8,128)}) custom-call(bf16[8,64,384]{2,1,0:T(8,128)(2,1)} %maximum_bitcast_fusion.refs_0_, s32[8,8,128]{2,1,0:T(8,128)} %broadcast_in_dim.12.refs_1_), custom_call_target="tpu_custom_call" | custom-call | tf_op jit(solution)/shard_map/slab_slab1/pallas_call | solution.py:757
  24.1 1.8 fusion.8
  25.9 20.0 %cols_move2.1 = (bf16[8,64,1024]{2,1,0:T(8,128)(2,1)}, bf16[64,2048]{1,0:T(8,128)(2,1)}) custom-call(bf16[64,8192]{1,0:T(8,128)(2,1)} %get-tuple-element.109.refs_0_, bf16[64,2048]{1,0:T(8,128)(2,1)} %refs_1_.1, bf16[8,64,384]{2,1,0:T(8,128)(2,1)} %get-tuple-element.55.refs_2_), custom_call_target="tpu_custom_call" | custom-call | tf_op jit(solution)/shard_map/cols_move2/pallas_call | solution.py:757
  45.9 1.0 reshape.266
  46.9 2.4 pad_maximum_fusion.refs_3_
  49.4 0.7 slice_reduce_fusion
  50.2 0.6 pad.14.refs_2_
  50.8 55.1 %gather_cols_gather3.1 = (bf16[8,256,2048]{2,1,0:T(8,128)(2,1)}, bf16[8,64,1024]{2,1,0:T(8,128)(2,1)}, bf16[8,32,128]{2,1,0:T(8,128)(2,1)}) custom-call(bf16[256,2048]{1,0:T(8,128)(2,1)} %bitcast.77, bf16[64,8192]{1,0:T(8,128)(2,1)} %get-tuple-element.110.refs_1_, bf16[32,128]{1,0:T(8,128)(2,1)} %pad.14.refs_2_, bf16[640,1024]{1,0:T(8,128)(2,1)} %pad_maximum_fusion.refs_3_), custom_call_target="tpu_custom_call" | custom-call | tf_op jit(solution)/shard_map/gather_cols_gather3/pallas_call | solution.py:757
  106.1 0.9 slice.35.refs_1_
  107.0 0.7 slice_reduce_fusion.1
  107.9 0.5 fusion.18
  108.7 1.3 copy-done.13
  110.0 1.1 bitcast_convert_fusion.refs_0_
  111.1 0.7 slice_convert_fusion
  112.0 1.6 copy.43
  113.6 13.0 %project.1 = (bf16[2048,2048]{1,0:T(8,128)(2,1)}, bf16[2048,256]{1,0:T(8,128)(2,1)S(1)}, bf16[2048,128]{1,0:T(8,128)(2,1)S(1)}) custom-call(bf16[2048,2048]{1,0:T(8,128)(2,1)} %bitcast.89, f32[1,2048]{1,0:T(1,128)S(1)} %reshape.297.gain_ref, bf16[2048,384]{1,0:T(8,128)(2,1)S(1)} %bitcast.68, f32[2,128,128]{2,1,0:T(8,128)S(1)} %get-tuple-element.106.cos_ref, ...), custom_call_target="tpu_custom_call" | custom-call | tf_op jit(solution)/shard_map/project/pallas_call | solution.py:828
  126.5 1.0 copy-done.1
  127.5 0.8 copy-done.10
  128.3 51.0 %gather_up4.1 = (bf16[8,256,2048]{2,1,0:T(8,128)(2,1)}, bf16[4,2048,128]{2,1,0:T(8,128)(2,1)}) custom-call(bf16[256,2048]{1,0:T(8,128)(2,1)} %bitcast_convert_fusion.refs_0_, bf16[2048,128]{1,0:T(8,128)(2,1)} %copy-done.10), custom_call_target="tpu_custom_call" | custom-call | tf_op jit(solution)/shard_map/gather_up4/pallas_call | solution.py:757
  179.3 1.2 copy-done.2
  180.5 8.4 %attend.1 = (f32[4,2,256,256]{3,2,1,0:T(8,128)S(1)}, bf16[4,2,2,128,256]{4,3,2,1,0:T(8,128)(2,1)S(1)}, f32[4,2,4,256]{3,2,1,0:T(4,128)S(1)}) custom-call(s32[8]{0:T(128)S(1)} %reshape_squeeze.6.lens, bf16[4,2,2,128,256]{4,3,2,1,0:T(8,128)(2,1)S(1)} %bitcast.72, bf16[4,4,2,2,128,128]{5,4,3,2,1,0:T(8,128)(2,1)} %bitcast.92), custom_call_target="tpu_custom_call" | custom-call | tf_op jit(solution)/shard_map/attend/pallas_call | solution.py:1067
  188.9 1.3 copy-done.8
  190.2 1.6 all-gather.10.cloned.1.call-done.refs_2_.refs_1_.refs_3_
  191.8 2.3 slice.41
  194.1 2.2 reshape.278.refs_1_
  196.3 6.8 convolution_convert_fusion
  203.1 41.9 %sum_pass5.1 = (bf16[256,2048]{1,0:T(8,128)(2,1)}, bf16[256,1536]{1,0:T(8,128)(2,1)}) custom-call(bf16[8,256,2048]{2,1,0:T(8,128)(2,1)} %bitcast.79, bf16[256,1536]{1,0:T(8,128)(2,1)} %slice.35.refs_1_, bf16[2560,1024]{1,0:T(8,128)(2,1)} %all-gather.10.cloned.1.call-done.refs_2_.refs_1_.refs_3_), custom_call_target="tpu_custom_call" | custom-call | tf_op jit(solution)/shard_map/sum_pass5/pallas_call | solution.py:757
  245.3 1.7 multiply_reduce_fusion.1
  247.1 1.4 fusion.15.refs_0_
  248.5 38.9 %all-gather.12.cloned.1.call-done = bf16[32,64,1024]{2,1,0:T(8,128)(2,1)} async-done(((bf16[8,64,1024]{2,1,0:T(8,128)(2,1)}), bf16[32,64,1024]{2,1,0:T(8,128)(2,1)}) %all-gather.12.cloned.1.call-update) | async-done | bytes 4194320 | tf_op jit(solution)/shard_map/all_gather | solution.py:786
  287.4 55.2 %forward6.1 = (bf16[8,256,2048]{2,1,0:T(8,128)(2,1)}, f32[2048,1024]{1,0:T(8,128)}, f32[2048,1024]{1,0:T(8,128)}, bf16[2048,1024]{1,0:T(8,128)(2,1)}, bf16[1024,...) custom-call(bf16[256,2048]{1,0:T(8,128)(2,1)} %fusion.15.refs_0_, ...), custom_call_target="tpu_custom_call" | custom-call | tf_op jit(solution)/shard_map/forward6/pallas_call | solution.py:757
  342.7 2.3 slice.42
  345.0 16.0 %all-gather.14.cloned.1.call-done.refs_0_ = bf16[1024,1536]{1,0:T(8,128)(2,1)} async-done(((bf16[256,1536]{1,0:T(8,128)(2,1)}), bf16[1024,1536]{1,0:T(8,128)(2,1)}) %all-gather.14.cloned.1.call-update) | async-done | bytes 3145744 | tf_op jit(solution)/shard_map/all_gather | solution.py:786
  361.0 33.2 %inner_back.1 = (bf16[2048,1024]{1,0:T(8,128)(2,1)}, bf16[2048,1024]{1,0:T(8,128)(2,1)}, bf16[2048,1024]{1,0:T(8,128)(2,1)}) custom-call(bf16[2048,2048]{1,0:T(8,128)(2,1)} %bitcast.81, f32[2048,1024]{1,0:T(8,128)} %get-tuple-element.68.gate_ref, f32[2048,1024]{1,0:T(8,128)} %get-tuple-element.69.up_ref, bf16[1024,512]{1,0:T(8,128)(2,1)} %bitcast.87, ...), custom_call_target="tpu_custom_call" | custom-call | tf_op jit(solution)/shard_map/inner_back/pallas_call | solution.py:945
  394.5 56.2 %mlp7.1 = (bf16[256,2048]{1,0:T(8,128)(2,1)}, bf16[2048,1024]{1,0:T(8,128)(2,1)}) custom-call(bf16[2048,2048]{1,0:T(8,128)(2,1)} %bitcast.83, bf16[2048,1024]{1,0:T(8,128)(2,1)} %get-tuple-element.72.refs_1_, bf16[2048,1024]{1,0:T(8,128)(2,1)} %get-tuple-element.73.refs_2_, bf16[2560,1024]{1,0:T(8,128)(2,1)} %all-gather.10.cloned.1.call-done.refs_2_.refs_1_.refs_3_, ...), custom_call_target="tpu_custom_call" | custom-call | tf_op jit(solution)/shard_map/mlp7/pallas_call | solution.py:757
  451.0 2.3 fusion.9
  453.5 3.0 fusion.23.refs_0_
  456.5 40.4 %heads_product8.1 = (bf16[2048,256]{1,0:T(8,128)(2,1)}, bf16[256,2048]{1,0:T(8,128)(2,1)}, bf16[2048,2048]{1,0:T(8,128)(2,1)}) custom-call(bf16[256,2048]{1,0:T(8,128)(2,1)} %fusion.23.refs_0_, bf16[256,2048]{1,0:T(8,128)(2,1)} %reshape.278.refs_1_, bf16[2048,256]{1,0:T(8,128)(2,1)} %bitcast.71, bf16[2048,1024]{1,0:T(8,128)(2,1)} %get-tuple-element.76.refs_3_, ...), custom_call_target="tpu_custom_call" | custom-call | tf_op jit(solution)/shard_map/heads_product8/pallas_call | solution.py:757
  497.0 1.2 copy-done.4
  498.2 1.2 copy-done.9
  499.5 15.6 %attend_back.1 = (f32[4,2,2,128,256]{4,3,2,1,0:T(8,128)S(1)}, bf16[4,4,2,2,128,128]{5,4,3,2,1,0:T(8,128)(2,1)}) custom-call(s32[8]{0:T(128)S(1)} %reshape_squeeze.6.lens, bf16[4,2,2,128,256]{4,3,2,1,0:T(8,128)(2,1)S(1)} %bitcast.73, bf16[4,4,2,2,128,128]{5,4,3,2,1,0:T(8,128)(2,1)} %bitcast.93, bf16[4,2,2,128,256]{4,3,2,1,0:T(8,128)(2,1)S(1)} %bitcast.76, ...), custom_call_target="tpu_custom_call" | custom-call | tf_op jit(solution)/shard_map/attend_back/pallas_call | solution.py:1094
  515.1 1.3 copy-done.5
  516.4 103.6 %down_sum_back9.1 = (bf16[2048,128]{1,0:T(8,128)(2,1)}, bf16[256,2048]{1,0:T(8,128)(2,1)}, bf16[64,8192]{1,0:T(8,128)(2,1)}) custom-call(bf16[4,2048,128]{2,1,0:T(8,128)(2,1)} %bitcast.98, bf16[8,256,2048]{2,1,0:T(8,128)(2,1)} %bitcast.90, bf16[8,64,1024]{2,1,0:T(8,128)(2,1)} %reduce-scatter.8.cloned.1.call-done.rest_0_.refs_2_), custom_call_target="tpu_custom_call" | custom-call | tf_op jit(solution)/shard_map/down_sum_back9/pallas_call | solution.py:757
  620.0 1.2 copy-done.12
  621.2 0.3 multiply_reduce_fusion
  621.6 1.6 copy-done.6
  623.2 14.4 %project_back.1 = (bf16[2048,2048]{1,0:T(8,128)(2,1)}, bf16[2048,384]{1,0:T(8,128)(2,1)S(1)}) custom-call(f32[2048,256]{1,0:T(8,128)S(1)} %bitcast.74, bf16[2048,128]{1,0:T(8,128)(2,1)S(1)} %copy-done.7, bf16[2048,2048]{1,0:T(8,128)(2,1)} %get-tuple-element.85.hid_ref, bf16[2048,384]{1,0:T(8,128)(2,1)S(1)} %bitcast.69, ...), custom_call_target="tpu_custom_call" | custom-call | tf_op jit(solution)/shard_map/project_back/pallas_call | solution.py:877
  637.6 1.4 copy.44
  639.0 53.7 %reduce_sum_back10.1 = (bf16[512,384]{1,0:T(8,128)(2,1)}, bf16[256,2048]{1,0:T(8,128)(2,1)}, bf16[64,8192]{1,0:T(8,128)(2,1)}) custom-call(bf16[4,512,384]{2,1,0:T(8,128)(2,1)} %bitcast.94, bf16[8,256,2048]{2,1,0:T(8,128)(2,1)} %bitcast.91, bf16[8,64,1024]{2,1,0:T(8,128)(2,1)} %reduce-scatter.10.cloned.1.call-done.refs_2_), custom_call_target="tpu_custom_call" | custom-call | tf_op jit(solution)/shard_map/reduce_sum_back10/pallas_call | solution.py:757
  692.7 12.7 %slab_home11.1 = (bf16[8,64,384]{2,1,0:T(8,128)(2,1)}, bf16[64,2048]{1,0:T(8,128)(2,1)}) custom-call(bf16[8,64,384]{2,1,0:T(8,128)(2,1)} %bitcast.107, bf16[64,2048]{1,0:T(8,128)(2,1)} %reduce-scatter.12.cloned.1.call-done.refs_1_, bf16[256,2048]{1,0:T(8,128)(2,1)} %get-tuple-element.90.refs_2_), custom_call_target="tpu_custom_call" | custom-call | tf_op jit(solution)/shard_map/slab_home11/pallas_call | solution.py:757
  705.4 1.1 convert_bitcast_fusion
  707.5 0.8 convert_element_type.161
  708.4 5.2 convert_multiply_fusion
  713.6 0.5 add.115
  714.6 0.6 fusion.2
  715.1 0.5 convert_divide_fusion
  715.7 3.0 fusion.6
  718.7 2.6 maximum_convert_fusion
  (131 shorter events, 3.8 us)
Async XLA Ops:
  7.2 4.7 copy-start.28
  7.2 4.8 copy-start.39
  7.2 42.2 %all-gather.6.cloned.1.call-start = ((), (), s32[]{:S(2)}) async-start(), calls=%async_computation.5 | async-start | bytes 1392640 | tf_op jit(solution)/shard_map/all_gather | solution.py:786
  8.2 15.8 %copy-start.40 = (bf16[64]{0:T(256)(128)(2,1)S(1)}, bf16[64]{0:T(256)(128)(2,1)}, u32[]{:S(2)}) copy-start(bf16[64]{0:T(256)(128)(2,1)} %param.20) | copy-start | bytes 388
  8.3 15.8 %copy-start.21 = (bf16[64,8192]{1,0:T(8,128)(2,1)S(1)}, bf16[64,8192]{1,0:T(8,128)(2,1)}, u32[]{:S(2)}) copy-start(bf16[64,8192]{1,0:T(8,128)(2,1)} %param.21) | copy-start | bytes 3145732
  8.3 15.8 %copy-start.22 = (bf16[64,8192]{1,0:T(8,128)(2,1)S(1)}, bf16[64,8192]{1,0:T(8,128)(2,1)}, u32[]{:S(2)}) copy-start(bf16[64,8192]{1,0:T(8,128)(2,1)} %param.22) | copy-start | bytes 3145732
  9.8 102.1 %all-gather.8.cloned.1.call-start = ((), (), s32[]{:S(2)}) async-start(), calls=%async_computation.6 | async-start | bytes 1966080 | tf_op jit(solution)/shard_map/all_gather | solution.py:786
  24.0 167.8 %all-gather.10.cloned.1.call-start = ((), (), s32[]{:S(2)}) async-start(), calls=%async_computation.7 | async-start | bytes 6553600 | tf_op jit(solution)/shard_map/all_gather | solution.py:786
  24.1 1.8 copy-start.37
  49.3 238.1 %all-gather.12.cloned.1.call-start = ((), (), s32[]{:S(2)}) async-start(), calls=%async_computation.8 | async-start | bytes 5242880 | tf_op jit(solution)/shard_map/all_gather | solution.py:786
  50.8 55.2 %copy-start.26 = (bf16[256,2048]{1,0:T(8,128)(2,1)S(1)}, bf16[256,2048]{1,0:T(8,128)(2,1)}, u32[]{:S(2)}) copy-start(bf16[256,2048]{1,0:T(8,128)(2,1)} %param.23) | copy-start | bytes 3145732
  106.0 2.5 copy-start.27
  106.0 255.0 %all-gather.14.cloned.1.call-start = ((), (), s32[]{:S(2)}) async-start(), calls=%async_computation.9 | async-start | bytes 3932160 | tf_op jit(solution)/shard_map/all_gather | solution.py:786
  108.7 1.3 copy-start.13
  126.5 1.0 copy-start.1
  127.5 0.8 copy-start.10
  179.3 1.2 copy-start.2
  188.9 1.3 copy-start.8
  190.2 6.0 copy-start
  203.1 42.2 %copy-start.11 = (bf16[2,128,2048]{2,1,0:T(8,128)(2,1)S(1)}, bf16[2,128,2048]{2,1,0:T(8,128)(2,1)}, u32[]{:S(2)}) copy-start(bf16[2,128,2048]{2,1,0:T(8,128)(2,1)} %param.12) | copy-start | bytes 3145732
  245.0 211.4 %reduce-scatter.6.cloned.1.call-start = ((), (), s32[]{:S(2)}) async-start(), calls=%async_computation.10 | async-start | bytes 2621440 | tf_op jit(solution)/shard_map/reduce_scatter | solution.py:782
  245.3 1.8 copy-start.16
  342.6 154.4 %reduce-scatter.8.cloned.1.call-start = ((), (), s32[]{:S(2)}) async-start(), calls=%async_computation.11 | async-start | bytes 5242880 | tf_op jit(solution)/shard_map/reduce_scatter | solution.py:782
  394.2 244.7 %reduce-scatter.10.cloned.1.call-start = ((), (), s32[]{:S(2)}) async-start(), calls=%async_computation.12 | async-start | bytes 5242880 | tf_op jit(solution)/shard_map/reduce_scatter | solution.py:782
  450.7 242.0 %reduce-scatter.12.cloned.1.call-start = ((), (), s32[]{:S(2)}) async-start(), calls=%async_computation.13 | async-start | bytes 1310720 | tf_op jit(solution)/shard_map/reduce_scatter | solution.py:782
  451.0 2.3 copy-start.14
  451.0 2.5 copy-start.17
  453.4 3.0 copy-start.35
  456.5 40.5 %copy-start.3 = (bf16[2048,256]{1,0:T(8,128)(2,1)S(1)}, bf16[2048,256]{1,0:T(8,128)(2,1)}, u32[]{:S(2)}) copy-start(bf16[2048,256]{1,0:T(8,128)(2,1)} %copy-done.1) | copy-start | bytes 3145732
  496.9 221.8 %reduce-scatter.14.cloned.1.call-start = ((), (), s32[]{:S(2)}) async-start(), calls=%async_computation.14 | async-start | bytes 2621440 | tf_op jit(solution)/shard_map/reduce_scatter | solution.py:782
  497.0 1.2 copy-start.4
  498.2 1.2 copy-start.9
  515.1 1.3 copy-start.5
  620.0 1.2 copy-start.12
  620.0 1.6 copy-start.7
  621.6 1.6 copy-start.6
  706.6 1.0 copy-start.32
  706.8 7.3 copy-start.30
  706.9 7.4 %copy-start.24 = (f32[8,8,8,256]{3,2,0,1:T(8,128)}, f32[8,8,8,256]{3,2,0,1:T(8,128)S(1)}, u32[]{:S(2)}) copy-start(f32[8,8,8,256]{3,2,0,1:T(8,128)S(1)} %copy.50) | copy-start | bytes 1572868
  707.2 7.0 copy-start.31
  708.3 5.8 copy-start.33
  708.3 5.9 copy-start.34
  708.4 6.0 copy-start.29
  708.4 6.2 copy-start.19
  708.4 7.3 %copy-start.20 = (bf16[256,2048]{1,0:T(8,128)(2,1)S(1)}, bf16[256,2048]{1,0:T(8,128)(2,1)}, u32[]{:S(2)}) copy-start(bf16[256,2048]{1,0:T(8,128)(2,1)} %get-tuple-element.75) | copy-start | bytes 3145732
  708.4 7.3 %copy-start.25 = (bf16[256,2048]{1,0:T(8,128)(2,1)S(1)}, bf16[256,2048]{1,0:T(8,128)(2,1)}, u32[]{:S(2)}) copy-start(bf16[256,2048]{1,0:T(8,128)(2,1)} %get-tuple-element.82) | copy-start | bytes 3145732
  713.6 1.6 copy-start.38
  713.6 2.1 copy-start.15
  713.6 2.1 copy-start.18
  713.6 2.1 copy-start.36
  715.7 3.0 copy-start.23
Sparse Core Ops, SparseCore 0:
  10.2 36.1 all-gather.5
  47.9 37.6 all-gather.7
  87.7 104.0 all-gather.9
  193.2 94.1 all-gather.11
  288.8 72.1 all-gather.13
  363.1 42.4 reduce-scatter.5
  408.1 76.0 reduce-scatter.7
  486.5 84.2 reduce-scatter.9
  573.1 42.5 reduce-scatter.11
  620.1 63.2 reduce-scatter.13
